TPU v7x, 32 devices: a whole 2x2x4 slice. The times are simulated.
32 devices in a mesh: seq: 8 (over z, y), ch: 4 (over x, core).
Axes of the slice: x: 2, y: 2, z: 4, core: 2. Of those that a mesh axis runs over, the one named last changes fastest.
Arguments:
- query_proj: bfloat16 [2048, 8192], P('seq', 'ch'), may hold values from -6 to 6
- key_proj: bfloat16 [2048, 8192], P('seq', 'ch'), may hold values from -6 to 6
- value_proj: bfloat16 [2048, 8192], P('seq', 'ch'), may hold values from -6 to 6
- decay_rate: float32 [16, 8192], P(None, 'ch'), may hold values from 9.765625e-06 to 0.033
- pole_angle: float32 [16, 8192], P(None, 'ch'), may hold values from -3.140625 to 3.140625
- residue_real: float32 [16, 8192], P(None, 'ch'), may hold values from -6 to 6
- residue_imag: float32 [16, 8192], P(None, 'ch'), may hold values from -6 to 6
- skip_gain: float32 [8192], P('ch'), may hold values from -6 to 6
- norm_gain: float32 [8192], P('ch'), may hold values from 0.5 to 1.5
Outputs:
- layer_out: bfloat16 [2048, 8192], P('seq', 'ch')
All inputs are finite; a program needn't handle non-finite values.
Results may differ from a plain program's by a relative error of at most 0.0017.
Values sent between devices are 32-bit elements; how exact they have to be, the bound alone decides.
No kernel may reach another device: no remote copies, remote signals or barrier semaphores. Data moves between devices by JAX's collectives and lax.ppermute only.
A program may use at most 64 MiB of HBM per device.

v0:
```python
import jax
import jax.numpy as jnp
from jax import lax
from jax.sharding import PartitionSpec as P


def shifted(block, axis, distance):
    devices = range(lax.axis_size(axis))
    route = [(i - distance, i) for i in devices if i - distance in devices]
    return lax.ppermute(block, axis, route)


def powers(decay_rate, pole_angle, count):
    magnitude = jnp.exp(-count * decay_rate)
    return (magnitude * jnp.cos(count * pole_angle), magnitude * jnp.sin(count * pole_angle))


def filter_tables(decay_rate, pole_angle, residue_real, residue_imag, block_len):
    offsets = jnp.arange(block_len).astype(jnp.float32)[:, None, None]
    weight = jnp.sqrt(decay_rate)
    base_re, base_im = powers(decay_rate, pole_angle, offsets)
    taps = jnp.sum(weight * (residue_real * base_re - residue_imag * base_im), axis=1)
    lag = jnp.arange(block_len)[:, None] - jnp.arange(block_len)[None, :]
    toeplitz = jnp.where((lag >= 0)[:, :, None], taps[jnp.clip(lag, 0, block_len - 1)], 0.0)
    next_re, next_im = powers(decay_rate, pole_angle, offsets + 1.0)
    out_re = weight * (residue_real * next_re - residue_imag * next_im)
    out_im = weight * (residue_real * next_im + residue_imag * next_re)
    in_re, in_im = powers(decay_rate, pole_angle, block_len - 1.0 - offsets)
    step_re, step_im = powers(decay_rate, pole_angle, jnp.float32(block_len))
    return (toeplitz, out_re, out_im, in_re, in_im, step_re, step_im)


def local_blocks(mixed, tables, block_len):
    toeplitz, out_re, out_im, in_re, in_im, step_re, step_im = tables
    highest = lax.Precision.HIGHEST
    blocks = mixed.reshape(mixed.shape[0] // block_len, block_len, mixed.shape[1])

    def local_advance(carry, block):
        state_re, state_im = carry
        near = jnp.einsum("tsc,sc->tc", toeplitz, block, precision=highest)
        far = jnp.einsum("jmc,mc->jc", out_re, state_re, precision=highest) - jnp.einsum(
            "jmc,mc->jc", out_im, state_im, precision=highest
        )
        enter_re = jnp.einsum("jmc,jc->mc", in_re, block, precision=highest)
        enter_im = jnp.einsum("jmc,jc->mc", in_im, block, precision=highest)
        new_re = step_re * state_re - step_im * state_im + enter_re
        new_im = step_re * state_im + step_im * state_re + enter_im
        return ((new_re, new_im), near + far)

    zeros = jnp.zeros(out_re.shape[1:], jnp.float32)
    final_state, outputs = lax.scan(local_advance, (zeros, zeros), blocks)
    return (outputs.reshape(mixed.shape), final_state)


def earlier_blocks(start_re, start_im, tables, block_count, block_len, width):
    toeplitz, out_re, out_im, in_re, in_im, step_re, step_im = tables
    highest = lax.Precision.HIGHEST

    def earlier_advance(carry, unused):
        state_re, state_im = carry
        far = jnp.einsum("jmc,mc->jc", out_re, state_re, precision=highest) - jnp.einsum(
            "jmc,mc->jc", out_im, state_im, precision=highest
        )
        new_re = step_re * state_re - step_im * state_im
        new_im = step_re * state_im + step_im * state_re
        return ((new_re, new_im), far)

    final_state, outputs = lax.scan(earlier_advance, (start_re, start_im), None, length=block_count)
    return outputs.reshape(block_count * block_len, width)


def per_device(
    query_proj,
    key_proj,
    value_proj,
    decay_rate,
    pole_angle,
    residue_real,
    residue_imag,
    skip_gain,
    norm_gain,
):
    mixed = key_proj.astype(jnp.float32) * value_proj.astype(jnp.float32)
    row_count = mixed.shape[0]
    width = mixed.shape[1]
    block_len = min(32, row_count)
    tables = filter_tables(decay_rate, pole_angle, residue_real, residue_imag, block_len)
    local_conv, end_state = local_blocks(mixed, tables, block_len)
    end_re, end_im = end_state
    whole_re, whole_im = powers(decay_rate, pole_angle, jnp.float32(row_count))

    def pass_state(counter, state):
        state_re, state_im = state
        next_re = whole_re * state_re - whole_im * state_im + end_re
        next_im = whole_re * state_im + whole_im * state_re + end_im
        return shifted((next_re, next_im), "seq", 1)

    empty = jnp.zeros_like(end_re)
    start_re, start_im = lax.fori_loop(0, lax.axis_size("seq") - 1, pass_state, (empty, empty))
    far_conv = earlier_blocks(start_re, start_im, tables, row_count // block_len, block_len, width)
    conv = local_conv + far_conv
    gated = query_proj.astype(jnp.float32) * (conv + skip_gain * mixed)
    partial_power = jnp.sum(gated * gated, axis=1)
    total_power = lax.psum(partial_power, "ch")
    power = total_power / (width * lax.axis_size("ch"))
    return (gated * norm_gain * lax.rsqrt(power[:, None] + 1e-05)).astype(jnp.bfloat16)


def solution(mesh):
    in_specs = (
        P("seq", "ch"),
        P("seq", "ch"),
        P("seq", "ch"),
        P(None, "ch"),
        P(None, "ch"),
        P(None, "ch"),
        P(None, "ch"),
        P("ch"),
        P("ch"),
    )
    out_specs = P("seq", "ch")
    return jax.shard_map(
        per_device, mesh=mesh, in_specs=in_specs, out_specs=out_specs, check_vma=False
    )
```

profile of v0, /device:TPU:0, one launch (start us, length us, event | category | flops | bytes accessed | tf_op | source)
XLA Modules:
  0.0 608.0 jit_solution(13349624361269924360)
XLA Ops:
  1.9 18.0 %fusion.28 = f32[32,2048]{1,0:T(8,128)S(1)} fusion(f32[16,2048]{1,0:T(8,128)} %param.21, f32[32]{0:T(128)S(1)} %iota_convert_fusion, f32[32]{0:T(128)S(1)} %fusion.32, f32[16,2048]{1,0:T(8,128)} %param.20, f32[16,2048]{1,0:T(8,128)S(1)} %get-tuple-element.922, f32[16,2048]{1,0:T(8,128)} %param.19, f32[16,2048]{1,0:T(8,128)} %param.18), kind=kLoop, calls=%fused_computation.50 | loop fusion | flops 9371648 | bytes 917760 | tf_op jit(solution)/shard_map/reduce_sum | solution.py:22
  20.0 6.9 %gather_fusion = f32[1024,2048]{1,0:T(8,128)} fusion(f32[32,2048]{1,0:T(8,128)S(1)} %fusion.28, s32[1024]{0:T(1024)S(1)} %broadcast_clamp_fusion), kind=kCustom, calls=%fused_computation | custom fusion | bytes 16781312 | tf_op jit(solution)/shard_map/gather | solution.py:24
  27.0 7.4 %broadcast_select_fusion = f32[32,32,2048]{2,1,0:T(8,128)} fusion(f32[32,32,2048]{2,1,0:T(8,128)} %bitcast.80, pred[32,32]{1,0:T(8,128)(4,1)S(1)} %subtract_compare_fusion), kind=kLoop, calls=%fused_computation.53 | loop fusion | flops 2097152 | bytes 16778240 | tf_op jit(solution)/shard_map/jit(_where)/select_n | solution.py:24
  37.7 328.0 %while.47 = (s32[]{:T(128)}, f32[16,2048]{1,0:T(8,128)S(1)}, f32[16,2048]{1,0:T(8,128)S(1)}, f32[8,32,2048]{2,1,0:T(8,128)}, f32[16,2048]{1,0:T(8,128)S(1)}, /*i...) while((s32[]{:T(128)}, f32[16,2048]{1,0:T(8,128)S(1)}, ...), condition=%wide.region_2.3_spmd.clone.clone.clone, body=%wide.region_1.2_spmd.clone.clone.clone.sunk | while | flops 29556740 | bytes 14025915 | solution.py:51
  38.9 16.1 %fusion.36 = (f32[2048,16]{0,1:T(8,128)S(1)}, f32[2048,16]{0,1:T(8,128)S(1)}) fusion(f32[2048,32]{0,1:T(8,128)S(1)} %dynamic-slice_bitcast_fusion.2, f32[16,2048]{1,0:T(8,128)S(1)} %get-tuple-element.877, f32[32]{0:T(128)S(1)} %get-tuple-element.878, f32[16,2048]{1,0:T(8,128)S(1)} %get-tuple-element.875, f32[32]{0:T(128)S(1)} %get-tuple-element.876), kind=kLoop, calls=%fused_computation.31.clone.1 | loop fusion | flops 8323072 | bytes 786688 | tf_op jit(solution)/shard_map/while/body/eval_jaxpr/jmc,jc->mc/dot_general | solution.py:45
  55.1 18.2 %multiply_reduce_fusion.11 = (f32[2048,32]{0,1:T(8,128)S(1)}, f32[2048,32]{0,1:T(8,128)S(1)}) fusion(f32[2048,16]{0,1:T(8,128)S(1)} %get-tuple-element.825, f32[16,2048]{1,0:T(8,128)S(1)} %get-tuple-element.882, f32[32]{0:T(128)S(1)} %get-tuple-element.881, f32[32]{0:T(128)S(1)} %get-tuple-element.880, f32[16,2048]{1,0:T(8,128)S(1)} %get-tuple-element.879, ...), kind=kLoop, calls=%fused_computation.34.clone.1 | loop fusion | flops 16646144 | bytes 1442048 | tf_op jit(solution)/shard_map/while/body/eval_jaxpr/jmc,mc->jc/dot_general | solution.py:41
  79.9 16.1 %fusion.36 = (f32[2048,16]{0,1:T(8,128)S(1)}, f32[2048,16]{0,1:T(8,128)S(1)}) fusion(f32[2048,32]{0,1:T(8,128)S(1)} %dynamic-slice_bitcast_fusion.2, f32[16,2048]{1,0:T(8,128)S(1)} %get-tuple-element.877, f32[32]{0:T(128)S(1)} %get-tuple-element.878, f32[16,2048]{1,0:T(8,128)S(1)} %get-tuple-element.875, f32[32]{0:T(128)S(1)} %get-tuple-element.876), kind=kLoop, calls=%fused_computation.31.clone.1 | loop fusion | flops 8323072 | bytes 786688 | tf_op jit(solution)/shard_map/while/body/eval_jaxpr/jmc,jc->mc/dot_general | solution.py:45
  96.1 18.2 %multiply_reduce_fusion.11 = (f32[2048,32]{0,1:T(8,128)S(1)}, f32[2048,32]{0,1:T(8,128)S(1)}) fusion(f32[2048,16]{0,1:T(8,128)S(1)} %get-tuple-element.825, f32[16,2048]{1,0:T(8,128)S(1)} %get-tuple-element.882, f32[32]{0:T(128)S(1)} %get-tuple-element.881, f32[32]{0:T(128)S(1)} %get-tuple-element.880, f32[16,2048]{1,0:T(8,128)S(1)} %get-tuple-element.879, ...), kind=kLoop, calls=%fused_computation.34.clone.1 | loop fusion | flops 16646144 | bytes 1442048 | tf_op jit(solution)/shard_map/while/body/eval_jaxpr/jmc,mc->jc/dot_general | solution.py:41
  120.8 16.1 %fusion.36 = (f32[2048,16]{0,1:T(8,128)S(1)}, f32[2048,16]{0,1:T(8,128)S(1)}) fusion(f32[2048,32]{0,1:T(8,128)S(1)} %dynamic-slice_bitcast_fusion.2, f32[16,2048]{1,0:T(8,128)S(1)} %get-tuple-element.877, f32[32]{0:T(128)S(1)} %get-tuple-element.878, f32[16,2048]{1,0:T(8,128)S(1)} %get-tuple-element.875, f32[32]{0:T(128)S(1)} %get-tuple-element.876), kind=kLoop, calls=%fused_computation.31.clone.1 | loop fusion | flops 8323072 | bytes 786688 | tf_op jit(solution)/shard_map/while/body/eval_jaxpr/jmc,jc->mc/dot_general | solution.py:45
  137.1 18.2 %multiply_reduce_fusion.11 = (f32[2048,32]{0,1:T(8,128)S(1)}, f32[2048,32]{0,1:T(8,128)S(1)}) fusion(f32[2048,16]{0,1:T(8,128)S(1)} %get-tuple-element.825, f32[16,2048]{1,0:T(8,128)S(1)} %get-tuple-element.882, f32[32]{0:T(128)S(1)} %get-tuple-element.881, f32[32]{0:T(128)S(1)} %get-tuple-element.880, f32[16,2048]{1,0:T(8,128)S(1)} %get-tuple-element.879, ...), kind=kLoop, calls=%fused_computation.34.clone.1 | loop fusion | flops 16646144 | bytes 1442048 | tf_op jit(solution)/shard_map/while/body/eval_jaxpr/jmc,mc->jc/dot_general | solution.py:41
  161.8 16.1 %fusion.36 = (f32[2048,16]{0,1:T(8,128)S(1)}, f32[2048,16]{0,1:T(8,128)S(1)}) fusion(f32[2048,32]{0,1:T(8,128)S(1)} %dynamic-slice_bitcast_fusion.2, f32[16,2048]{1,0:T(8,128)S(1)} %get-tuple-element.877, f32[32]{0:T(128)S(1)} %get-tuple-element.878, f32[16,2048]{1,0:T(8,128)S(1)} %get-tuple-element.875, f32[32]{0:T(128)S(1)} %get-tuple-element.876), kind=kLoop, calls=%fused_computation.31.clone.1 | loop fusion | flops 8323072 | bytes 786688 | tf_op jit(solution)/shard_map/while/body/eval_jaxpr/jmc,jc->mc/dot_general | solution.py:45
  178.0 18.2 %multiply_reduce_fusion.11 = (f32[2048,32]{0,1:T(8,128)S(1)}, f32[2048,32]{0,1:T(8,128)S(1)}) fusion(f32[2048,16]{0,1:T(8,128)S(1)} %get-tuple-element.825, f32[16,2048]{1,0:T(8,128)S(1)} %get-tuple-element.882, f32[32]{0:T(128)S(1)} %get-tuple-element.881, f32[32]{0:T(128)S(1)} %get-tuple-element.880, f32[16,2048]{1,0:T(8,128)S(1)} %get-tuple-element.879, ...), kind=kLoop, calls=%fused_computation.34.clone.1 | loop fusion | flops 16646144 | bytes 1442048 | tf_op jit(solution)/shard_map/while/body/eval_jaxpr/jmc,mc->jc/dot_general | solution.py:41
  202.8 16.1 %fusion.36 = (f32[2048,16]{0,1:T(8,128)S(1)}, f32[2048,16]{0,1:T(8,128)S(1)}) fusion(f32[2048,32]{0,1:T(8,128)S(1)} %dynamic-slice_bitcast_fusion.2, f32[16,2048]{1,0:T(8,128)S(1)} %get-tuple-element.877, f32[32]{0:T(128)S(1)} %get-tuple-element.878, f32[16,2048]{1,0:T(8,128)S(1)} %get-tuple-element.875, f32[32]{0:T(128)S(1)} %get-tuple-element.876), kind=kLoop, calls=%fused_computation.31.clone.1 | loop fusion | flops 8323072 | bytes 786688 | tf_op jit(solution)/shard_map/while/body/eval_jaxpr/jmc,jc->mc/dot_general | solution.py:45
  219.0 18.2 %multiply_reduce_fusion.11 = (f32[2048,32]{0,1:T(8,128)S(1)}, f32[2048,32]{0,1:T(8,128)S(1)}) fusion(f32[2048,16]{0,1:T(8,128)S(1)} %get-tuple-element.825, f32[16,2048]{1,0:T(8,128)S(1)} %get-tuple-element.882, f32[32]{0:T(128)S(1)} %get-tuple-element.881, f32[32]{0:T(128)S(1)} %get-tuple-element.880, f32[16,2048]{1,0:T(8,128)S(1)} %get-tuple-element.879, ...), kind=kLoop, calls=%fused_computation.34.clone.1 | loop fusion | flops 16646144 | bytes 1442048 | tf_op jit(solution)/shard_map/while/body/eval_jaxpr/jmc,mc->jc/dot_general | solution.py:41
  243.8 16.1 %fusion.36 = (f32[2048,16]{0,1:T(8,128)S(1)}, f32[2048,16]{0,1:T(8,128)S(1)}) fusion(f32[2048,32]{0,1:T(8,128)S(1)} %dynamic-slice_bitcast_fusion.2, f32[16,2048]{1,0:T(8,128)S(1)} %get-tuple-element.877, f32[32]{0:T(128)S(1)} %get-tuple-element.878, f32[16,2048]{1,0:T(8,128)S(1)} %get-tuple-element.875, f32[32]{0:T(128)S(1)} %get-tuple-element.876), kind=kLoop, calls=%fused_computation.31.clone.1 | loop fusion | flops 8323072 | bytes 786688 | tf_op jit(solution)/shard_map/while/body/eval_jaxpr/jmc,jc->mc/dot_general | solution.py:45
  260.0 18.2 %multiply_reduce_fusion.11 = (f32[2048,32]{0,1:T(8,128)S(1)}, f32[2048,32]{0,1:T(8,128)S(1)}) fusion(f32[2048,16]{0,1:T(8,128)S(1)} %get-tuple-element.825, f32[16,2048]{1,0:T(8,128)S(1)} %get-tuple-element.882, f32[32]{0:T(128)S(1)} %get-tuple-element.881, f32[32]{0:T(128)S(1)} %get-tuple-element.880, f32[16,2048]{1,0:T(8,128)S(1)} %get-tuple-element.879, ...), kind=kLoop, calls=%fused_computation.34.clone.1 | loop fusion | flops 16646144 | bytes 1442048 | tf_op jit(solution)/shard_map/while/body/eval_jaxpr/jmc,mc->jc/dot_general | solution.py:41
  284.7 16.1 %fusion.36 = (f32[2048,16]{0,1:T(8,128)S(1)}, f32[2048,16]{0,1:T(8,128)S(1)}) fusion(f32[2048,32]{0,1:T(8,128)S(1)} %dynamic-slice_bitcast_fusion.2, f32[16,2048]{1,0:T(8,128)S(1)} %get-tuple-element.877, f32[32]{0:T(128)S(1)} %get-tuple-element.878, f32[16,2048]{1,0:T(8,128)S(1)} %get-tuple-element.875, f32[32]{0:T(128)S(1)} %get-tuple-element.876), kind=kLoop, calls=%fused_computation.31.clone.1 | loop fusion | flops 8323072 | bytes 786688 | tf_op jit(solution)/shard_map/while/body/eval_jaxpr/jmc,jc->mc/dot_general | solution.py:45
  300.9 18.2 %multiply_reduce_fusion.11 = (f32[2048,32]{0,1:T(8,128)S(1)}, f32[2048,32]{0,1:T(8,128)S(1)}) fusion(f32[2048,16]{0,1:T(8,128)S(1)} %get-tuple-element.825, f32[16,2048]{1,0:T(8,128)S(1)} %get-tuple-element.882, f32[32]{0:T(128)S(1)} %get-tuple-element.881, f32[32]{0:T(128)S(1)} %get-tuple-element.880, f32[16,2048]{1,0:T(8,128)S(1)} %get-tuple-element.879, ...), kind=kLoop, calls=%fused_computation.34.clone.1 | loop fusion | flops 16646144 | bytes 1442048 | tf_op jit(solution)/shard_map/while/body/eval_jaxpr/jmc,mc->jc/dot_general | solution.py:41
  325.7 16.1 %fusion.36 = (f32[2048,16]{0,1:T(8,128)S(1)}, f32[2048,16]{0,1:T(8,128)S(1)}) fusion(f32[2048,32]{0,1:T(8,128)S(1)} %dynamic-slice_bitcast_fusion.2, f32[16,2048]{1,0:T(8,128)S(1)} %get-tuple-element.877, f32[32]{0:T(128)S(1)} %get-tuple-element.878, f32[16,2048]{1,0:T(8,128)S(1)} %get-tuple-element.875, f32[32]{0:T(128)S(1)} %get-tuple-element.876), kind=kLoop, calls=%fused_computation.31.clone.1 | loop fusion | flops 8323072 | bytes 786688 | tf_op jit(solution)/shard_map/while/body/eval_jaxpr/jmc,jc->mc/dot_general | solution.py:45
  341.9 18.2 %multiply_reduce_fusion.11 = (f32[2048,32]{0,1:T(8,128)S(1)}, f32[2048,32]{0,1:T(8,128)S(1)}) fusion(f32[2048,16]{0,1:T(8,128)S(1)} %get-tuple-element.825, f32[16,2048]{1,0:T(8,128)S(1)} %get-tuple-element.882, f32[32]{0:T(128)S(1)} %get-tuple-element.881, f32[32]{0:T(128)S(1)} %get-tuple-element.880, f32[16,2048]{1,0:T(8,128)S(1)} %get-tuple-element.879, ...), kind=kLoop, calls=%fused_computation.34.clone.1 | loop fusion | flops 16646144 | bytes 1442048 | tf_op jit(solution)/shard_map/while/body/eval_jaxpr/jmc,mc->jc/dot_general | solution.py:41
  365.7 75.9 %while.45 = (s32[]{:T(128)}, f32[16,2048]{1,0:T(8,128)S(1)}, f32[16,2048]{1,0:T(8,128)S(1)}, f32[16,2048]{1,0:T(8,128)S(1)}, f32[16,2048]{1,0:T(8,128)S(1)}, /*i...) while((s32[]{:T(128)}, f32[16,2048]{1,0:T(8,128)S(1)}, f32[16,2048]{1,0:T(8,128)S(1)}, ...), condition=%wide.region_4.5_spmd, body=%wide.region_3.4_spmd.sunk | while | flops 262146 | bytes 2097317 | solution.py:99
  365.8 4.9 collective-permute-start
  443.2 152.2 %while.46 = (s32[]{:T(128)}, f32[16,2048]{1,0:T(8,128)S(1)}, f32[16,2048]{1,0:T(8,128)S(1)}, f32[8,32,2048]{2,1,0:T(8,128)}, f32[16,2048]{1,0:T(8,128)S(1)}, /*i...) while((s32[]{:T(128)}, f32[16,2048]{1,0:T(8,128)S(1)}, ...), condition=%wide.region_6.7_spmd.clone.clone, body=%wide.region_5.6_spmd.clone.clone.sunk | while | flops 16908288 | bytes 3015557 | solution.py:68
  443.2 18.2 %multiply_reduce_fusion.9 = (f32[2048,32]{0,1:T(8,128)S(1)}, f32[2048,32]{0,1:T(8,128)S(1)}) fusion(f32[2048,16]{0,1:T(8,128)S(1)} %bitcast.82, f32[16,2048]{1,0:T(8,128)S(1)} %get-tuple-element.949, f32[16,2048]{1,0:T(8,128)S(1)} %get-tuple-element.947, f32[32]{0:T(128)S(1)} %get-tuple-element.948, f32[16,2048]{1,0:T(8,128)S(1)} %get-tuple-element.945, ...), kind=kLoop, calls=%fused_computation.13.clone.1 | loop fusion | flops 16646144 | bytes 1442048 | tf_op jit(solution)/shard_map/while/body/eval_jaxpr/jmc,mc->jc/dot_general | solution.py:61
  462.2 18.2 %multiply_reduce_fusion.9 = (f32[2048,32]{0,1:T(8,128)S(1)}, f32[2048,32]{0,1:T(8,128)S(1)}) fusion(f32[2048,16]{0,1:T(8,128)S(1)} %bitcast.82, f32[16,2048]{1,0:T(8,128)S(1)} %get-tuple-element.949, f32[16,2048]{1,0:T(8,128)S(1)} %get-tuple-element.947, f32[32]{0:T(128)S(1)} %get-tuple-element.948, f32[16,2048]{1,0:T(8,128)S(1)} %get-tuple-element.945, ...), kind=kLoop, calls=%fused_computation.13.clone.1 | loop fusion | flops 16646144 | bytes 1442048 | tf_op jit(solution)/shard_map/while/body/eval_jaxpr/jmc,mc->jc/dot_general | solution.py:61
  481.2 18.2 %multiply_reduce_fusion.9 = (f32[2048,32]{0,1:T(8,128)S(1)}, f32[2048,32]{0,1:T(8,128)S(1)}) fusion(f32[2048,16]{0,1:T(8,128)S(1)} %bitcast.82, f32[16,2048]{1,0:T(8,128)S(1)} %get-tuple-element.949, f32[16,2048]{1,0:T(8,128)S(1)} %get-tuple-element.947, f32[32]{0:T(128)S(1)} %get-tuple-element.948, f32[16,2048]{1,0:T(8,128)S(1)} %get-tuple-element.945, ...), kind=kLoop, calls=%fused_computation.13.clone.1 | loop fusion | flops 16646144 | bytes 1442048 | tf_op jit(solution)/shard_map/while/body/eval_jaxpr/jmc,mc->jc/dot_general | solution.py:61
  500.3 18.2 %multiply_reduce_fusion.9 = (f32[2048,32]{0,1:T(8,128)S(1)}, f32[2048,32]{0,1:T(8,128)S(1)}) fusion(f32[2048,16]{0,1:T(8,128)S(1)} %bitcast.82, f32[16,2048]{1,0:T(8,128)S(1)} %get-tuple-element.949, f32[16,2048]{1,0:T(8,128)S(1)} %get-tuple-element.947, f32[32]{0:T(128)S(1)} %get-tuple-element.948, f32[16,2048]{1,0:T(8,128)S(1)} %get-tuple-element.945, ...), kind=kLoop, calls=%fused_computation.13.clone.1 | loop fusion | flops 16646144 | bytes 1442048 | tf_op jit(solution)/shard_map/while/body/eval_jaxpr/jmc,mc->jc/dot_general | solution.py:61
  519.3 18.2 %multiply_reduce_fusion.9 = (f32[2048,32]{0,1:T(8,128)S(1)}, f32[2048,32]{0,1:T(8,128)S(1)}) fusion(f32[2048,16]{0,1:T(8,128)S(1)} %bitcast.82, f32[16,2048]{1,0:T(8,128)S(1)} %get-tuple-element.949, f32[16,2048]{1,0:T(8,128)S(1)} %get-tuple-element.947, f32[32]{0:T(128)S(1)} %get-tuple-element.948, f32[16,2048]{1,0:T(8,128)S(1)} %get-tuple-element.945, ...), kind=kLoop, calls=%fused_computation.13.clone.1 | loop fusion | flops 16646144 | bytes 1442048 | tf_op jit(solution)/shard_map/while/body/eval_jaxpr/jmc,mc->jc/dot_general | solution.py:61
  538.3 18.2 %multiply_reduce_fusion.9 = (f32[2048,32]{0,1:T(8,128)S(1)}, f32[2048,32]{0,1:T(8,128)S(1)}) fusion(f32[2048,16]{0,1:T(8,128)S(1)} %bitcast.82, f32[16,2048]{1,0:T(8,128)S(1)} %get-tuple-element.949, f32[16,2048]{1,0:T(8,128)S(1)} %get-tuple-element.947, f32[32]{0:T(128)S(1)} %get-tuple-element.948, f32[16,2048]{1,0:T(8,128)S(1)} %get-tuple-element.945, ...), kind=kLoop, calls=%fused_computation.13.clone.1 | loop fusion | flops 16646144 | bytes 1442048 | tf_op jit(solution)/shard_map/while/body/eval_jaxpr/jmc,mc->jc/dot_general | solution.py:61
  557.4 18.2 %multiply_reduce_fusion.9 = (f32[2048,32]{0,1:T(8,128)S(1)}, f32[2048,32]{0,1:T(8,128)S(1)}) fusion(f32[2048,16]{0,1:T(8,128)S(1)} %bitcast.82, f32[16,2048]{1,0:T(8,128)S(1)} %get-tuple-element.949, f32[16,2048]{1,0:T(8,128)S(1)} %get-tuple-element.947, f32[32]{0:T(128)S(1)} %get-tuple-element.948, f32[16,2048]{1,0:T(8,128)S(1)} %get-tuple-element.945, ...), kind=kLoop, calls=%fused_computation.13.clone.1 | loop fusion | flops 16646144 | bytes 1442048 | tf_op jit(solution)/shard_map/while/body/eval_jaxpr/jmc,mc->jc/dot_general | solution.py:61
  576.4 18.2 %multiply_reduce_fusion.9 = (f32[2048,32]{0,1:T(8,128)S(1)}, f32[2048,32]{0,1:T(8,128)S(1)}) fusion(f32[2048,16]{0,1:T(8,128)S(1)} %bitcast.82, f32[16,2048]{1,0:T(8,128)S(1)} %get-tuple-element.949, f32[16,2048]{1,0:T(8,128)S(1)} %get-tuple-element.947, f32[32]{0:T(128)S(1)} %get-tuple-element.948, f32[16,2048]{1,0:T(8,128)S(1)} %get-tuple-element.945, ...), kind=kLoop, calls=%fused_computation.13.clone.1 | loop fusion | flops 16646144 | bytes 1442048 | tf_op jit(solution)/shard_map/while/body/eval_jaxpr/jmc,mc->jc/dot_general | solution.py:61
  598.9 5.7 psum.7
  (122 shorter events, 144.3 us)
Async XLA Ops:
  26.9 7.4 %copy-start = (bf16[256,2048]{1,0:T(8,128)(2,1)S(1)}, bf16[256,2048]{1,0:T(8,128)(2,1)}, u32[]{:S(2)}) copy-start(bf16[256,2048]{1,0:T(8,128)(2,1)} %param.17) | copy-start | bytes 3145732
  26.9 7.4 %copy-start.1 = (bf16[256,2048]{1,0:T(8,128)(2,1)S(1)}, bf16[256,2048]{1,0:T(8,128)(2,1)}, u32[]{:S(2)}) copy-start(bf16[256,2048]{1,0:T(8,128)(2,1)} %param.16) | copy-start | bytes 3145732
  34.3 3.3 copy-start.4
  34.3 3.3 copy-start.5
  34.3 3.3 copy-start.8
  34.3 3.3 copy-start.9
  365.8 8.3 %collective-permute-start = (f32[16,2048]{1,0:T(8,128)S(1)}, f32[16,2048]{1,0:T(8,128)S(1)}, u32[]{:S(2)}, u32[]{:S(2)}) collective-permute-start(f32[16,2048]{1,0:T(8,128)S(1)} %get-tuple-element.785), channel_id=1, source_target_pairs={{0,4},{4,8},{8,12},{12,16},{16,20},{20,24},{24,28},{1,5},{5,9},{9,... | collective-permute-start | bytes 393224 | tf_op jit(solution)/shard_map/while/body/eval_jaxpr/ppermute | solution.py:10
  370.7 5.9 collective-permute-start.1
  376.7 8.7 %collective-permute-start = (f32[16,2048]{1,0:T(8,128)S(1)}, f32[16,2048]{1,0:T(8,128)S(1)}, u32[]{:S(2)}, u32[]{:S(2)}) collective-permute-start(f32[16,2048]{1,0:T(8,128)S(1)} %get-tuple-element.785), channel_id=1, source_target_pairs={{0,4},{4,8},{8,12},{12,16},{16,20},{20,24},{24,28},{1,5},{5,9},{9,... | collective-permute-start | bytes 393224 | tf_op jit(solution)/shard_map/while/body/eval_jaxpr/ppermute | solution.py:10
  381.0 6.8 %collective-permute-start.1 = (f32[16,2048]{1,0:T(8,128)S(1)}, f32[16,2048]{1,0:T(8,128)S(1)}, u32[]{:S(2)}, u32[]{:S(2)}) collective-permute-start(f32[16,2048]{1,0:T(8,128)S(1)} %get-tuple-element.786), channel_id=1, source_target_pairs={{0,4},{4,8},{8,12},{12,16},{16,20},{20,24},{24,28},{1,5},{5,9},{9,... | collective-permute-start | bytes 393224 | tf_op jit(solution)/shard_map/while/body/eval_jaxpr/ppermute | solution.py:10
  387.9 7.8 %collective-permute-start = (f32[16,2048]{1,0:T(8,128)S(1)}, f32[16,2048]{1,0:T(8,128)S(1)}, u32[]{:S(2)}, u32[]{:S(2)}) collective-permute-start(f32[16,2048]{1,0:T(8,128)S(1)} %get-tuple-element.785), channel_id=1, source_target_pairs={{0,4},{4,8},{8,12},{12,16},{16,20},{20,24},{24,28},{1,5},{5,9},{9,... | collective-permute-start | bytes 393224 | tf_op jit(solution)/shard_map/while/body/eval_jaxpr/ppermute | solution.py:10
  392.3 5.9 collective-permute-start.1
  398.2 8.7 %collective-permute-start = (f32[16,2048]{1,0:T(8,128)S(1)}, f32[16,2048]{1,0:T(8,128)S(1)}, u32[]{:S(2)}, u32[]{:S(2)}) collective-permute-start(f32[16,2048]{1,0:T(8,128)S(1)} %get-tuple-element.785), channel_id=1, source_target_pairs={{0,4},{4,8},{8,12},{12,16},{16,20},{20,24},{24,28},{1,5},{5,9},{9,... | collective-permute-start | bytes 393224 | tf_op jit(solution)/shard_map/while/body/eval_jaxpr/ppermute | solution.py:10
  402.6 6.8 %collective-permute-start.1 = (f32[16,2048]{1,0:T(8,128)S(1)}, f32[16,2048]{1,0:T(8,128)S(1)}, u32[]{:S(2)}, u32[]{:S(2)}) collective-permute-start(f32[16,2048]{1,0:T(8,128)S(1)} %get-tuple-element.786), channel_id=1, source_target_pairs={{0,4},{4,8},{8,12},{12,16},{16,20},{20,24},{24,28},{1,5},{5,9},{9,... | collective-permute-start | bytes 393224 | tf_op jit(solution)/shard_map/while/body/eval_jaxpr/ppermute | solution.py:10
  409.5 7.8 %collective-permute-start = (f32[16,2048]{1,0:T(8,128)S(1)}, f32[16,2048]{1,0:T(8,128)S(1)}, u32[]{:S(2)}, u32[]{:S(2)}) collective-permute-start(f32[16,2048]{1,0:T(8,128)S(1)} %get-tuple-element.785), channel_id=1, source_target_pairs={{0,4},{4,8},{8,12},{12,16},{16,20},{20,24},{24,28},{1,5},{5,9},{9,... | collective-permute-start | bytes 393224 | tf_op jit(solution)/shard_map/while/body/eval_jaxpr/ppermute | solution.py:10
  413.8 5.9 collective-permute-start.1
  419.8 8.7 %collective-permute-start = (f32[16,2048]{1,0:T(8,128)S(1)}, f32[16,2048]{1,0:T(8,128)S(1)}, u32[]{:S(2)}, u32[]{:S(2)}) collective-permute-start(f32[16,2048]{1,0:T(8,128)S(1)} %get-tuple-element.785), channel_id=1, source_target_pairs={{0,4},{4,8},{8,12},{12,16},{16,20},{20,24},{24,28},{1,5},{5,9},{9,... | collective-permute-start | bytes 393224 | tf_op jit(solution)/shard_map/while/body/eval_jaxpr/ppermute | solution.py:10
  424.2 6.8 %collective-permute-start.1 = (f32[16,2048]{1,0:T(8,128)S(1)}, f32[16,2048]{1,0:T(8,128)S(1)}, u32[]{:S(2)}, u32[]{:S(2)}) collective-permute-start(f32[16,2048]{1,0:T(8,128)S(1)} %get-tuple-element.786), channel_id=1, source_target_pairs={{0,4},{4,8},{8,12},{12,16},{16,20},{20,24},{24,28},{1,5},{5,9},{9,... | collective-permute-start | bytes 393224 | tf_op jit(solution)/shard_map/while/body/eval_jaxpr/ppermute | solution.py:10
  431.1 8.1 %collective-permute-start = (f32[16,2048]{1,0:T(8,128)S(1)}, f32[16,2048]{1,0:T(8,128)S(1)}, u32[]{:S(2)}, u32[]{:S(2)}) collective-permute-start(f32[16,2048]{1,0:T(8,128)S(1)} %get-tuple-element.785), channel_id=1, source_target_pairs={{0,4},{4,8},{8,12},{12,16},{16,20},{20,24},{24,28},{1,5},{5,9},{9,... | collective-permute-start | bytes 393224 | tf_op jit(solution)/shard_map/while/body/eval_jaxpr/ppermute | solution.py:10
  435.4 6.2 %collective-permute-start.1 = (f32[16,2048]{1,0:T(8,128)S(1)}, f32[16,2048]{1,0:T(8,128)S(1)}, u32[]{:S(2)}, u32[]{:S(2)}) collective-permute-start(f32[16,2048]{1,0:T(8,128)S(1)} %get-tuple-element.786), channel_id=1, source_target_pairs={{0,4},{4,8},{8,12},{12,16},{16,20},{20,24},{24,28},{1,5},{5,9},{9,... | collective-permute-start | bytes 393224 | tf_op jit(solution)/shard_map/while/body/eval_jaxpr/ppermute | solution.py:10
  595.4 2.7 copy-start.2
  595.4 2.8 copy-start.3
  595.4 2.8 copy-start.6
  598.2 6.4 %copy-start.7 = (f32[2048]{0:T(1024)S(1)}, f32[2048]{0:T(1024)}, u32[]{:S(2)}) copy-start(f32[2048]{0:T(1024)} %param.23) | copy-start | bytes 24580
where the time goes:
time: 609 us; the launch traced here: 608 us
  other arithmetic  508 us (83%)
  starting transfers between devices  58 us (10%)
  local copies, waits for them, and re-layouts  18 us (3%)
  waiting for transfers between devices  17.4 us (3%)
    dot_general x8, other arithmetic, local_advance(): jnp.einsum('jmc,mc->jc', out_im, state_im, precision=highest)  146 us
    dot_general x8, other arithmetic, earlier_advance(): jnp.einsum('jmc,mc->jc', out_im, state_im, precision=highest)  145 us
    dot_general x8, other arithmetic, local_advance(): enter_im = jnp.einsum('jmc,jc->mc', in_im, block, precision=highest)  129 us
    ppermute x14, starting transfers between devices, shifted(): return lax.ppermute(block, axis, route)  58 us
    dot_general x8, other arithmetic, local_advance(): near = jnp.einsum('tsc,sc->tc', toeplitz, block, precision=highest)  38.3 us
    reduce_sum x1, other arithmetic, filter_tables(): jnp.sum(weight * (residue_real * base_re - residue_imag * base_im), axis=1)  18 us
    ppermute x14, waiting for transfers between devices, shifted(): return lax.ppermute(block, axis, route)  17.4 us
  transfers between devices with their start and end apart: 14, of which 7 were waited for; matrix products, arithmetic and copies ran while one was open for 0% of the time, Pallas kernels for 0%

commit v1 on v0

v1 whole, which is shorter than its diff:
```python
import functools

import jax
import jax.numpy as jnp
from jax import lax
from jax.experimental import pallas as pl
from jax.experimental.pallas import tpu as pltpu
from jax.sharding import PartitionSpec as P

F32 = jnp.float32
SUB = 8
LANE = 128
BLOCK = 16
STEP = 256
VMEM_LIMIT = 48 * 2**20


def cmul(ar, ai, br, bi):
    return ar * br - ai * bi, ar * bi + ai * br


def cos_sin(r, n):
    z = r * r
    s = r + r * z * (-1.66666667e-1 + z * (8.33333310e-3 + z * (-1.98409296e-4 + z * 2.7181716e-6)))
    c = 1.0 + z * (-0.5 + z * (4.16666664e-2 + z * (-1.38888642e-3 + z * 2.4760495e-5)))
    quarter = n - 4.0 * jnp.floor(n * 0.25)
    odd = (quarter == 1.0) | (quarter == 3.0)
    sin = jnp.where(odd, c, s)
    cos = jnp.where(odd, s, c)
    sin = jnp.where(quarter >= 2.0, -sin, sin)
    cos = jnp.where((quarter == 1.0) | (quarter == 2.0), -cos, cos)
    return cos, sin


def pole_power(decay, angle, count):
    phase = angle * float(count)
    n = jnp.floor(phase * 0.6366197723675814 + 0.5)
    r = ((phase - n * 1.5703125) - n * 4.837512969970703125e-4) - n * 7.549789948768648e-8
    cos, sin = cos_sin(r, n)
    size = jnp.exp(decay * -float(count))
    return size * cos, size * sin


def power_table(pr, pi, first_r, first_i, count):
    tr, ti = [first_r], [first_i]
    for _ in range(count - 1):
        r, i = cmul(tr[-1], ti[-1], pr, pi)
        tr.append(r)
        ti.append(i)
    return tr, ti


def squared(r, i, times):
    for _ in range(times):
        r, i = r * r - i * i, (r + r) * i
    return r, i


def row(ref, index):
    return jnp.broadcast_to(ref[index : index + 1, :], (SUB, LANE))


def end_state_kernel(with_power, off_ref, k_ref, v_ref, a_ref, th_ref, rr_ref, ri_ref, *rest):
    if with_power:
        e_ref, l_ref, hp_ref, pw_ref, xs = rest
    else:
        e_ref, l_ref, hp_ref, xs = rest
    rows = k_ref.shape[0]
    modes = a_ref.shape[0]
    for g in range(k_ref.shape[1] // LANE):
        ls = slice(g * LANE, (g + 1) * LANE)
        xs[...] = k_ref[:, ls].astype(F32) * v_ref[:, ls].astype(F32)
        taps = None
        for m0 in range(0, modes, SUB):
            ms = slice(m0, m0 + SUB)
            decay, angle = a_ref[ms, ls], th_ref[ms, ls]
            pr, pi = pole_power(decay, angle, 1)
            weight = jnp.sqrt(decay)
            tr, ti = power_table(pr, pi, weight * rr_ref[ms, ls], weight * ri_ref[ms, ls], BLOCK)
            taps = tr if taps is None else [x + y for x, y in zip(taps, tr)]
            qr, qi = squared(pr, pi, BLOCK.bit_length() - 1)
            sr = jnp.zeros((SUB, LANE), F32)
            si = jnp.zeros((SUB, LANE), F32)
            for b in range(rows // BLOCK):
                at = b * 2 * modes + m0
                l_ref[at : at + SUB, ls] = sr
                l_ref[at + modes : at + modes + SUB, ls] = si
                sr, si = cmul(qr, qi, sr, si)
                for s in range(BLOCK):
                    x = row(xs, b * BLOCK + s)
                    sr = sr + tr[BLOCK - 1 - s] * x
                    si = si + ti[BLOCK - 1 - s] * x
            e_ref[ms, ls] = sr
            e_ref[modes + m0 : modes + m0 + SUB, ls] = si
            if with_power:
                wr, wi = pole_power(decay, angle, rows)
                pw_ref[ms, ls] = wr
                pw_ref[modes + m0 : modes + m0 + SUB, ls] = wi
        for j in range(BLOCK):
            hp_ref[j * SUB : (j + 1) * SUB, ls] = taps[j]


def near_kernel(off_ref, k_ref, v_ref, hp_ref, skip_ref, y_ref, xs):
    rows = k_ref.shape[0]
    blocks = rows // BLOCK
    for g in range(k_ref.shape[1] // LANE):
        ls = slice(g * LANE, (g + 1) * LANE)
        xs[...] = k_ref[:, ls].astype(F32) * v_ref[:, ls].astype(F32)
        taps = []
        for j in range(BLOCK):
            tap = jnp.sum(hp_ref[j * SUB : (j + 1) * SUB, ls], axis=0, keepdims=True)
            if j == 0:
                tap = tap + skip_ref[0:1, ls]
            taps.append(jnp.broadcast_to(tap, (SUB, LANE)))
        for a0 in range(0, blocks, SUB):
            acc = [None] * BLOCK
            for s in range(BLOCK):
                x = xs[pl.ds(a0 * BLOCK + s, SUB, stride=BLOCK), :]
                for t in range(s, BLOCK):
                    part = taps[t - s] * x
                    acc[t] = part if acc[t] is None else acc[t] + part
            for t in range(BLOCK):
                y_ref[t * blocks + a0 : t * blocks + a0 + SUB, ls] = acc[t]


def far_kernel(off_ref, s_ref, l_ref, y_ref, a_ref, th_ref, q_ref, gated_ref, power_ref, table, state, conv):
    rows = q_ref.shape[0]
    modes = a_ref.shape[0]
    blocks = rows // BLOCK

    @pl.when(pl.program_id(0) == 0)
    def _():
        power_ref[...] = jnp.zeros_like(power_ref)

    for g in range(q_ref.shape[1] // LANE):
        ls = slice(g * LANE, (g + 1) * LANE)
        for m0 in range(0, modes, SUB):
            ms = slice(m0, m0 + SUB)
            pr, pi = pole_power(a_ref[ms, ls], th_ref[ms, ls], 1)
            tr, ti = power_table(pr, pi, pr, pi, BLOCK)
            for j in range(BLOCK):
                at = j * 2 * modes + m0
                table[at : at + SUB, :] = tr[j]
                table[at + modes : at + modes + SUB, :] = ti[j]
            qr, qi = tr[-1], ti[-1]
            sr, si = s_ref[ms, ls], s_ref[modes + m0 : modes + m0 + SUB, ls]
            for b in range(blocks):
                at = b * 2 * modes + m0
                state[at : at + SUB, :] = l_ref[at : at + SUB, ls] + sr
                state[at + modes : at + modes + SUB, :] = l_ref[at + modes : at + modes + SUB, ls] + si
                if b < blocks - 1:
                    sr, si = cmul(qr, qi, sr, si)
        starts = range(0, blocks, SUB)
        acc = {
            (t, a0): y_ref[t * blocks + a0 : t * blocks + a0 + SUB, ls] for t in range(BLOCK) for a0 in starts
        }
        for m in range(modes):
            cr = {a0: state[pl.ds(a0 * 2 * modes + m, SUB, stride=2 * modes), :] for a0 in starts}
            ci = {a0: state[pl.ds(a0 * 2 * modes + modes + m, SUB, stride=2 * modes), :] for a0 in starts}
            for t in range(BLOCK):
                br = row(table, t * 2 * modes + m)
                bi = row(table, t * 2 * modes + modes + m)
                for a0 in starts:
                    acc[t, a0] = acc[t, a0] + cr[a0] * br - ci[a0] * bi
        for (t, a0), y in acc.items():
            conv[pl.ds(a0 * BLOCK + t, SUB, stride=BLOCK), :] = y
        gated = q_ref[:, ls].astype(F32) * conv[...]
        gated_ref[:, ls] = gated
        power_ref[...] += gated * gated


def norm_kernel(steps, off_ref, scale_ref, own_ref, other_ref, gain_ref, out_ref):
    step = pl.program_id(0)

    @pl.when(step < steps)
    def _():
        out_ref[...] = (own_ref[...] * gain_ref[...] * scale_ref[:, 0:1]).astype(out_ref.dtype)

    @pl.when(step >= steps)
    def _():
        out_ref[...] = (other_ref[...] * gain_ref[...] * scale_ref[:, 0:1]).astype(out_ref.dtype)


def call(kernel, offset, steps, ins, outs, scratch):
    def spec(rows, place):
        if place == "half":
            return pl.BlockSpec((rows, STEP), lambda i, off: (0, off[0] * steps + i))
        if place == "local":
            return pl.BlockSpec((rows, STEP), lambda i, off: (0, i))
        return pl.BlockSpec((rows, LANE), lambda i, off: (0, 0))

    return pl.pallas_call(
        kernel,
        grid_spec=pltpu.PrefetchScalarGridSpec(
            num_scalar_prefetch=1,
            grid=(steps,),
            in_specs=[spec(rows, place) for _, rows, place in ins],
            out_specs=[spec(rows, place) for _, _, rows, place in outs],
            scratch_shapes=scratch,
        ),
        out_shape=[jax.ShapeDtypeStruct(shape, dtype) for shape, dtype, _, _ in outs],
        compiler_params=pltpu.CompilerParams(vmem_limit_bytes=VMEM_LIMIT),
    )(offset, *[x for x, _, _ in ins])


def exchange(x, axis, distance):
    return lax.ppermute(x, axis, [(i, i ^ distance) for i in range(lax.axis_size(axis))])


def parts(x):
    half = x.shape[0] // 2
    return x[:half], x[half:]


def times(x, y):
    return jnp.concatenate(cmul(*parts(x), *parts(y)))


def per_device(q, k, v, decay, angle, res_r, res_i, skip_gain, norm_gain):
    rows, width = q.shape
    modes = decay.shape[0]
    half = width // 2
    steps = half // STEP
    blocks = rows // BLOCK
    count = lax.axis_size("seq")
    me = lax.axis_index("seq")
    upper = (me & 1) == 1
    own = (me & 1).astype(jnp.int32).reshape(1)
    other = 1 - own
    skip = skip_gain.reshape(1, width)
    gain = norm_gain.reshape(1, width)
    states = 2 * modes

    def end_state(offset, with_power):
        outs = [
            ((states, half), F32, states, "local"),
            ((blocks * states, half), F32, blocks * states, "local"),
            ((BLOCK * SUB, half), F32, BLOCK * SUB, "local"),
        ]
        if with_power:
            outs.append(((states, half), F32, states, "local"))
        ins = [(k, rows, "half"), (v, rows, "half")] + [
            (x, modes, "half") for x in (decay, angle, res_r, res_i)
        ]
        return call(
            functools.partial(end_state_kernel, with_power),
            offset, steps, ins, outs, [pltpu.VMEM((rows, LANE), F32)],
        )

    def near(offset, taps):
        ins = [(k, rows, "half"), (v, rows, "half"), (taps, BLOCK * SUB, "local"), (skip, 1, "half")]
        outs = [((rows, half), F32, rows, "local")]
        return call(near_kernel, offset, steps, ins, outs, [pltpu.VMEM((rows, LANE), F32)])[0]

    def far(offset, start, local, y):
        ins = [
            (start, states, "local"),
            (local, blocks * states, "local"),
            (y, rows, "local"),
            (decay, modes, "half"),
            (angle, modes, "half"),
            (q, rows, "half"),
        ]
        outs = [((rows, half), F32, rows, "local"), ((rows, LANE), F32, rows, "fixed")]
        scratch = [
            pltpu.VMEM((BLOCK * states, LANE), F32),
            pltpu.VMEM((blocks * states, LANE), F32),
            pltpu.VMEM((rows, LANE), F32),
        ]
        return call(far_kernel, offset, steps, ins, outs, scratch)

    sent_end, sent_local, sent_taps = end_state(other, False)
    pair_end = exchange(sent_end, "seq", 1)
    own_end, own_local, own_taps, step_power = end_state(own, True)
    own_near = near(own, own_taps)
    other_near = near(other, sent_taps)
    low = jnp.where(upper, pair_end, own_end)
    high = jnp.where(upper, own_end, pair_end)
    total = times(step_power, low) + high
    before = jnp.zeros_like(total)
    jump = times(step_power, step_power)
    mine = jnp.concatenate([jnp.ones((modes, half), F32), jnp.zeros((modes, half), F32)])
    distance = 2
    while distance < count:
        got = exchange(total, "seq", distance)
        above = (me & distance) != 0
        before = jnp.where(above, before + times(mine, got), before)
        total = jnp.where(above, times(jump, got) + total, times(jump, total) + got)
        mine = jnp.where(above, times(mine, jump), mine)
        jump = times(jump, jump)
        distance *= 2
    after_low = times(step_power, before) + low
    own_start = jnp.where(upper, after_low, before)
    other_start = exchange(jnp.where(upper, before, after_low), "seq", 1)
    own_gated, own_power = far(own, own_start, own_local, own_near)
    other_gated, other_power = far(other, other_start, sent_local, other_near)
    power = jnp.sum(own_power + other_power, axis=1)
    distance = 1
    while distance < lax.axis_size("ch"):
        power = power + exchange(power, "ch", distance)
        distance *= 2
    scale = lax.rsqrt(power / (width * lax.axis_size("ch")) + 1e-05)
    scale = jnp.broadcast_to(scale[:, None], (rows, LANE))

    def place(i, off):
        return (0, lax.rem(off[0] * steps + i, 2 * steps))

    return pl.pallas_call(
        functools.partial(norm_kernel, steps),
        grid_spec=pltpu.PrefetchScalarGridSpec(
            num_scalar_prefetch=1,
            grid=(2 * steps,),
            in_specs=[
                pl.BlockSpec((rows, LANE), lambda i, off: (0, 0)),
                pl.BlockSpec((rows, STEP), lambda i, off: (0, jnp.minimum(i, steps - 1))),
                pl.BlockSpec((rows, STEP), lambda i, off: (0, jnp.maximum(i - steps, 0))),
                pl.BlockSpec((1, STEP), place),
            ],
            out_specs=pl.BlockSpec((rows, STEP), place),
        ),
        out_shape=jax.ShapeDtypeStruct((rows, width), jnp.bfloat16),
        compiler_params=pltpu.CompilerParams(vmem_limit_bytes=VMEM_LIMIT),
    )(own, scale, own_gated, other_gated, gain)


def solution(mesh):
    rows = P("seq", "ch")
    poles = P(None, "ch")
    return jax.shard_map(
        per_device,
        mesh=mesh,
        in_specs=(rows, rows, rows, poles, poles, poles, poles, P("ch"), P("ch")),
        out_specs=rows,
        check_vma=False,
    )
```

time: 609 us -> 58.1 us (0.10)
  other arithmetic: 508 us -> 2.84 us
  starting transfers between devices: 58 us -> 9.37 us
  Pallas kernels: 0 us -> 24.8 us
  local copies, waits for them, and re-layouts: 18 us -> 9.51 us
  waiting for transfers between devices: 17.4 us -> 11 us
    dot_general x32 -> x0, other arithmetic: 458 us -> none  [the longest x8 146 us: local_advance(): jnp.einsum('jmc,mc->jc', out_im, state_im, precision=highest)]
    ppermute x14 -> x6, starting transfers between devices: 58 us -> 9.37 us  [exchange(): lax.ppermute(x, axis, [(i, i ^ distance) for i in range(lax.axis_size(axi...]
    pallas_call x0 -> x7, Pallas kernels: none -> 24.8 us  [the longest x6 21.4 us: call(): pl.pallas_call(kernel, grid_spec=pltpu.PrefetchScalarGridSpec(num_scalar_...]
    reduce_sum x2 -> x1, other arithmetic: 18.7 us -> 0.11 us  [per_device(): power = jnp.sum(own_power + other_power, axis=1)]
    dynamic_update_slice x16 -> x0, other arithmetic: 11.9 us -> none  [local_blocks(): final_state, outputs = lax.scan(local_advance, (zeros, zeros), blocks)]
    unnamed x20 -> x42, local copies, waits for them, and re-layouts: 0.19 us -> 9.41 us
    while x8 -> x0, local copies, waits for them, and re-layouts: 7.74 us -> none
    gather x1 -> x0, local copies, waits for them, and re-layouts: 6.89 us -> none  [filter_tables(): taps[jnp.clip(lag, 0, block_len - 1)]]
  transfers between devices with their start and end apart: 14 -> 6, of which waited for: 7 -> 4; matrix products, arithmetic and copies ran while one was open for 0% -> 2% of each run, Pallas kernels for 0% -> 21%
where the time goes in v1:
time: 58.1 us; the launch traced here: 57.7 us
  Pallas kernels  24.8 us (43%)
  waiting for transfers between devices  11 us (19%)
  local copies, waits for them, and re-layouts  9.51 us (16%)
  starting transfers between devices  9.37 us (16%)
  other arithmetic  2.84 us (5%)
    pallas_call x6, Pallas kernels, call(): pl.pallas_call(kernel, grid_spec=pltpu.PrefetchScalarGridSpec(num_scalar_...  21.4 us
    ppermute x6, waiting for transfers between devices, exchange(): lax.ppermute(x, axis, [(i, i ^ distance) for i in range(lax.axis_size(axi...  11 us
    unnamed x42, local copies, waits for them, and re-layouts  9.41 us
    ppermute x6, starting transfers between devices, exchange(): lax.ppermute(x, axis, [(i, i ^ distance) for i in range(lax.axis_size(axi...  9.37 us
    pallas_call x1, Pallas kernels, per_device(): pl.pallas_call(functools.partial(norm_kernel, steps), grid_spec=pltpu.Pre...  3.42 us
    sub x4, other arithmetic, cmul(): return (ar * br - ai * bi, ar * bi + ai * br)  1.65 us
  transfers between devices with their start and end apart: 6, of which 4 were waited for; matrix products, arithmetic and copies ran while one was open for 2% of the time, Pallas kernels for 21%

profile of v1, /device:TPU:0, one launch (start us, length us, event | category | flops | bytes accessed | tf_op | source)
XLA Modules:
  0.0 57.7 jit_solution(3829112944069558822)
XLA Ops:
  0.0 1.2 %copy-done = bf16[256,2048]{1,0:T(8,128)(2,1)S(1)} copy-done((bf16[256,2048]{1,0:T(8,128)(2,1)S(1)}, bf16[256,2048]{1,0:T(8,128)(2,1)}, u32[]{:S(2)}) %copy-start) | copy-done | bytes 1048600
  1.2 1.2 %copy-done.2 = bf16[256,2048]{1,0:T(8,128)(2,1)S(1)} copy-done((bf16[256,2048]{1,0:T(8,128)(2,1)S(1)}, bf16[256,2048]{1,0:T(8,128)(2,1)}, u32[]{:S(2)}) %copy-start.2) | copy-done | bytes 1048600
  2.5 0.9 %copy-done.5 = f32[16,2048]{1,0:T(8,128)S(1)} copy-done((f32[16,2048]{1,0:T(8,128)S(1)}, f32[16,2048]{1,0:T(8,128)}, u32[]{:S(2)}) %copy-start.5) | copy-done | bytes 131096
  3.4 0.9 %copy-done.7 = f32[16,2048]{1,0:T(8,128)S(1)} copy-done((f32[16,2048]{1,0:T(8,128)S(1)}, f32[16,2048]{1,0:T(8,128)}, u32[]{:S(2)}) %copy-start.7) | copy-done | bytes 131096
  4.3 0.9 %copy-done.13 = f32[16,2048]{1,0:T(8,128)S(1)} copy-done((f32[16,2048]{1,0:T(8,128)S(1)}, f32[16,2048]{1,0:T(8,128)}, u32[]{:S(2)}) %copy-start.13) | copy-done | bytes 131096
  5.2 0.9 %copy-done.15 = f32[16,2048]{1,0:T(8,128)S(1)} copy-done((f32[16,2048]{1,0:T(8,128)S(1)}, f32[16,2048]{1,0:T(8,128)}, u32[]{:S(2)}) %copy-start.15) | copy-done | bytes 131096
  6.1 4.1 %shard_map.92 = (f32[32,1024]{1,0:T(8,128)S(1)}, f32[512,1024]{1,0:T(8,128)S(1)}, f32[128,1024]{1,0:T(8,128)S(1)}) custom-call(s32[1]{0:T(128)S(6)} %sub.27.off_ref, bf16[256,2048]{1,0:T(8,128)(2,1)S(1)} %copy-done, bf16[256,2048]{1,0:T(8,128)(2,1)S(1)} %copy-done.2, f32[16,2048]{1,0:T(8,128)S(1)} %copy-done.5, f32[16,2048]{1,0:T(8,128)S(1)} %copy-done.7, ...), custom_call_target="tpu_custom_call" | custom-call | tf_op jit(solution)/shard_map/pallas_call | solution.py:192
  10.2 1.3 %copy-done.9 = f32[512,1024]{1,0:T(8,128)} copy-done((f32[512,1024]{1,0:T(8,128)}, f32[512,1024]{1,0:T(8,128)S(1)}, u32[]{:S(2)}) %copy-start.9) | copy-done | bytes 2097176
  11.6 3.0 %collective-permute-start = (f32[32,1024]{1,0:T(8,128)S(1)}, f32[32,1024]{1,0:T(8,128)S(1)}, u32[]{:S(2)}, u32[]{:S(2)}) collective-permute-start(f32[32,1024]{1,0:T(8,128)S(1)} %get-tuple-element.17), channel_id=1, source_target_pairs={{0,4},{4,0},{8,12},{12,8},{16,20},{20,16},{24,28},{28,24},{1,5},{5... | collective-permute-start | bytes 393224 | tf_op jit(solution)/shard_map/ppermute | solution.py:207
  14.6 4.2 %shard_map.91 = (f32[32,1024]{1,0:T(8,128)S(1)}, f32[512,1024]{1,0:T(8,128)S(1)}, f32[128,1024]{1,0:T(8,128)S(1)}, f32[32,1024]{1,0:T(8,128)S(1)}) custom-call(s32[1]{0:T(128)} %bitcast.off_ref, bf16[256,2048]{1,0:T(8,128)(2,1)S(1)} %copy-done.1, bf16[256,2048]{1,0:T(8,128)(2,1)S(1)} %copy-done.3, f32[16,2048]{1,0:T(8,128)S(1)} %copy-done.6, ...), custom_call_target="tpu_custom_call" | custom-call | tf_op jit(solution)/shard_map/pallas_call | solution.py:192
  18.8 1.3 %copy-done.11 = f32[512,1024]{1,0:T(8,128)} copy-done((f32[512,1024]{1,0:T(8,128)}, f32[512,1024]{1,0:T(8,128)S(1)}, u32[]{:S(2)}) %copy-start.11) | copy-done | bytes 2097176
  20.1 0.7 %multiply_subtract_fusion.4 = (f32[16,1024]{1,0:T(8,128)S(1)}, f32[16,1024]{1,0:T(8,128)S(1)}, f32[16,1024]{1,0:T(8,128)}, f32[16,1024]{1,0:T(8,128)S(1)}, f32[16,1024]{1,0:T(8,128)S(1)}) fusion(f32[32,1024]{1,0:T(8,128)S(1)} %get-tuple-element.16, f32[32,1024]{1,0:T(8,128)S(1)} %broadcast_select_fusion.2), kind=kLoop, calls=%fused_computation.19 | loop fusion | flops 212992 | bytes 589824 | tf_op jit(solution)/shard_map/sub | solution.py:19
  20.9 0.0 copy-done.17
  20.9 1.6 %collective-permute-start.1 = (f32[32,1024]{1,0:T(8,128)S(1)}, f32[32,1024]{1,0:T(8,128)S(1)}, u32[]{:S(2)}, u32[]{:S(2)}) collective-permute-start(f32[32,1024]{1,0:T(8,128)S(1)} %maximum_add_fusion), channel_id=1, source_target_pairs={{0,8},{4,12},{8,0},{12,4},{16,24},{20,28},{24,16},{28,20},{1,9},{5... | collective-permute-start | bytes 393224 | tf_op jit(solution)/shard_map/ppermute | solution.py:207
  22.6 3.4 %collective-permute-done.1 = f32[32,1024]{1,0:T(8,128)S(1)} collective-permute-done((f32[32,1024]{1,0:T(8,128)S(1)}, f32[32,1024]{1,0:T(8,128)S(1)}, u32[]{:S(2)}, u32[]{:S(2)}) %collective-permute-start.1) | collective-permute-done | bytes 131104 | tf_op jit(solution)/shard_map/ppermute | solution.py:207
  25.9 0.9 %multiply_subtract_fusion.2 = (f32[16,1024]{1,0:T(8,128)S(1)}, f32[16,1024]{1,0:T(8,128)S(1)}, f32[16,1024]{1,0:T(8,128)S(1)}, f32[16,1024]{1,0:T(8,128)S(1)}, f...) fusion(f32[16,1024]{1,0:T(8,128)} %get-tuple-element.29, ...), kind=kLoop, calls=%fused_computation.15 | loop fusion | flops 294912 | bytes 851968 | tf_op jit(solution)/shard_map/sub | solution.py:19
  26.9 2.7 %collective-permute-start.2 = (f32[32,1024]{1,0:T(8,128)S(1)}, f32[32,1024]{1,0:T(8,128)S(1)}, u32[]{:S(2)}, u32[]{:S(2)}) collective-permute-start(f32[32,1024]{1,0:T(8,128)S(1)} %fusion), channel_id=1, source_target_pairs={{0,16},{4,20},{8,24},{12,28},{16,0},{20,4},{24,8},{28,12},{1,17},{... | collective-permute-start | bytes 393224 | tf_op jit(solution)/shard_map/ppermute | solution.py:207
  29.5 0.9 %maximum_select_fusion.1 = f32[32,1024]{1,0:T(8,128)S(1)} fusion(f32[32,1024]{1,0:T(8,128)} %constant.9.clone.1, f32[16,1024]{1,0:T(8,128)S(1)} %get-tuple-element.42, f32[16,1024]{1,0:T(8,128)S(1)} %get-tuple-element.27, pred[]{:T(512)S(6)} %ne.7), kind=kLoop, calls=%fused_computation.3 | loop fusion | flops 65536 | bytes 393217 | tf_op jit(solution)/shard_map/jit(_where)/select_n | solution.py:289
  30.5 4.0 %collective-permute-done.2 = f32[32,1024]{1,0:T(8,128)S(1)} collective-permute-done((f32[32,1024]{1,0:T(8,128)S(1)}, f32[32,1024]{1,0:T(8,128)S(1)}, u32[]{:S(2)}, u32[]{:S(2)}) %collective-permute-start.2) | collective-permute-done | bytes 131104 | tf_op jit(solution)/shard_map/ppermute | solution.py:207
  34.6 1.0 %collective-permute-start.3 = (f32[32,1024]{1,0:T(8,128)S(1)}, f32[32,1024]{1,0:T(8,128)S(1)}, u32[]{:S(2)}, u32[]{:S(2)}) collective-permute-start(f32[32,1024]{1,0:T(8,128)S(1)} %get-tuple-element.30), channel_id=1, source_target_pairs={{0,4},{4,0},{8,12},{12,8},{16,20},{20,16},{24,28},{28,24},{1,5},{5... | collective-permute-start | bytes 393224 | tf_op jit(solution)/shard_map/ppermute | solution.py:207
  35.5 1.2 %shard_map.95.y_ref = f32[256,1024]{1,0:T(8,128)S(1)} custom-call(s32[1]{0:T(128)S(6)} %sub.27.off_ref, bf16[256,2048]{1,0:T(8,128)(2,1)S(1)} %copy-done.1, bf16[256,2048]{1,0:T(8,128)(2,1)S(1)} %copy-done.3, f32[128,1024]{1,0:T(8,128)S(1)} %get-tuple-element.23.hp_ref, f32[1,2048]{1,0:T(1,128)S(1)} %bitcast.3), custom_call_target="tpu_custom_call" | custom-call | tf_op jit(solution)/shard_map/pallas_call | solution.py:192
  36.8 1.3 %shard_map.93.y_ref = f32[256,1024]{1,0:T(8,128)S(1)} custom-call(s32[1]{0:T(128)} %bitcast.off_ref, bf16[256,2048]{1,0:T(8,128)(2,1)S(1)} %copy-done.1, bf16[256,2048]{1,0:T(8,128)(2,1)S(1)} %copy-done.3, f32[128,1024]{1,0:T(8,128)S(1)} %copy-done.18, f32[1,2048]{1,0:T(1,128)S(1)} %bitcast.4), custom_call_target="tpu_custom_call" | custom-call | tf_op jit(solution)/shard_map/pallas_call | solution.py:192
  38.1 0.6 %copy-done.12 = f32[512,1024]{1,0:T(8,128)S(1)} copy-done((f32[512,1024]{1,0:T(8,128)S(1)}, f32[512,1024]{1,0:T(8,128)}, u32[]{:S(2)}) %copy-start.12) | copy-done | bytes 2097176
  38.7 5.3 %shard_map.94 = (f32[256,1024]{1,0:T(8,128)S(1)}, f32[256,128]{1,0:T(8,128)S(1)}) custom-call(s32[1]{0:T(128)} %bitcast.off_ref, f32[32,1024]{1,0:T(8,128)S(1)} %get-tuple-element.31.s_ref, f32[512,1024]{1,0:T(8,128)S(1)} %copy-done.12, f32[256,1024]{1,0:T(8,128)S(1)} %shard_map.93.y_ref, f32[16,2048]{1,0:T(8,128)S(1)} %copy-done.6, ...), custom_call_target="tpu_custom_call" | custom-call | tf_op jit(solution)/shard_map/pallas_call | solution.py:192
  44.0 5.3 %shard_map.96 = (f32[256,1024]{1,0:T(8,128)S(1)}, f32[256,128]{1,0:T(8,128)S(1)}) custom-call(s32[1]{0:T(128)S(6)} %sub.27.off_ref, f32[32,1024]{1,0:T(8,128)S(1)} %collective-permute-done.3.s_ref, f32[512,1024]{1,0:T(8,128)S(1)} %copy-done.10, f32[256,1024]{1,0:T(8,128)S(1)} %shard_map.95.y_ref, f32[16,2048]{1,0:T(8,128)S(1)} %copy-done.6, ...), custom_call_target="tpu_custom_call" | custom-call | tf_op jit(solution)/shard_map/pallas_call | solution.py:192
  49.3 0.1 add_reduce_fusion
  49.4 0.1 collective-permute-start.4
  49.5 1.1 %collective-permute-done.4 = f32[256]{0:T(256)S(1)} collective-permute-done((f32[256]{0:T(256)S(1)}, f32[256]{0:T(256)S(1)}, u32[]{:S(2)}, u32[]{:S(2)}) %collective-permute-start.4) | collective-permute-done | bytes 1056 | tf_op jit(solution)/shard_map/ppermute | solution.py:207
  50.6 1.1 %collective-permute-start.5 = (f32[256]{0:T(256)S(1)}, f32[256]{0:T(256)S(1)}, u32[]{:S(2)}, u32[]{:S(2)}) collective-permute-start(f32[256]{0:T(256)S(1)} %add.68), channel_id=1, source_target_pairs={{0,2},{1,3},{2,0},{3,1},{4,6},{5,7},{6,4},{7,5},{8,10},{9,11},{10,... | collective-permute-start | bytes 3080 | tf_op jit(solution)/shard_map/ppermute | solution.py:207
  51.7 2.5 %collective-permute-done.5 = f32[256]{0:T(256)S(1)} collective-permute-done((f32[256]{0:T(256)S(1)}, f32[256]{0:T(256)S(1)}, u32[]{:S(2)}, u32[]{:S(2)}) %collective-permute-start.5) | collective-permute-done | bytes 1056 | tf_op jit(solution)/shard_map/ppermute | solution.py:207
  54.2 0.1 broadcast_in_dim.14.scale_ref
  54.3 3.4 %shard_map.97 = bf16[256,2048]{1,0:T(8,128)(2,1)} custom-call(s32[1]{0:T(128)} %bitcast.off_ref, f32[256,128]{1,0:T(8,128)S(1)} %broadcast_in_dim.14.scale_ref, f32[256,1024]{1,0:T(8,128)S(1)} %get-tuple-element.25.own_ref, f32[256,1024]{1,0:T(8,128)S(1)} %get-tuple-element.26.other_ref, f32[1,2048]{1,0:T(1,128)S(1)} %bitcast.5), custom_call_target="tpu_custom_call" | custom-call | tf_op jit(solution)/shard_map/pallas_call | solution.py:308
  (43 shorter events, 0.3 us)
Async XLA Ops:
  0.0 1.2 %copy-start = (bf16[256,2048]{1,0:T(8,128)(2,1)S(1)}, bf16[256,2048]{1,0:T(8,128)(2,1)}, u32[]{:S(2)}) copy-start(bf16[256,2048]{1,0:T(8,128)(2,1)} %k_ref.7) | copy-start | bytes 3145732
  1.2 1.2 %copy-start.2 = (bf16[256,2048]{1,0:T(8,128)(2,1)S(1)}, bf16[256,2048]{1,0:T(8,128)(2,1)}, u32[]{:S(2)}) copy-start(bf16[256,2048]{1,0:T(8,128)(2,1)} %v_ref.7) | copy-start | bytes 3145732
  2.5 0.9 %copy-start.5 = (f32[16,2048]{1,0:T(8,128)S(1)}, f32[16,2048]{1,0:T(8,128)}, u32[]{:S(2)}) copy-start(f32[16,2048]{1,0:T(8,128)} %a_ref.7) | copy-start | bytes 393220
  3.4 0.9 %copy-start.7 = (f32[16,2048]{1,0:T(8,128)S(1)}, f32[16,2048]{1,0:T(8,128)}, u32[]{:S(2)}) copy-start(f32[16,2048]{1,0:T(8,128)} %th_ref.7) | copy-start | bytes 393220
  4.3 0.9 %copy-start.13 = (f32[16,2048]{1,0:T(8,128)S(1)}, f32[16,2048]{1,0:T(8,128)}, u32[]{:S(2)}) copy-start(f32[16,2048]{1,0:T(8,128)} %rr_ref.3) | copy-start | bytes 393220
  5.2 0.9 %copy-start.15 = (f32[16,2048]{1,0:T(8,128)S(1)}, f32[16,2048]{1,0:T(8,128)}, u32[]{:S(2)}) copy-start(f32[16,2048]{1,0:T(8,128)} %ri_ref.3) | copy-start | bytes 393220
  6.1 8.5 %copy-start.1 = (bf16[256,2048]{1,0:T(8,128)(2,1)S(1)}, bf16[256,2048]{1,0:T(8,128)(2,1)}, u32[]{:S(2)}) copy-start(bf16[256,2048]{1,0:T(8,128)(2,1)} %k_ref.7) | copy-start | bytes 3145732
  6.1 8.5 %copy-start.3 = (bf16[256,2048]{1,0:T(8,128)(2,1)S(1)}, bf16[256,2048]{1,0:T(8,128)(2,1)}, u32[]{:S(2)}) copy-start(bf16[256,2048]{1,0:T(8,128)(2,1)} %v_ref.7) | copy-start | bytes 3145732
  6.1 8.5 %copy-start.6 = (f32[16,2048]{1,0:T(8,128)S(1)}, f32[16,2048]{1,0:T(8,128)}, u32[]{:S(2)}) copy-start(f32[16,2048]{1,0:T(8,128)} %a_ref.7) | copy-start | bytes 393220
  6.1 8.5 %copy-start.8 = (f32[16,2048]{1,0:T(8,128)S(1)}, f32[16,2048]{1,0:T(8,128)}, u32[]{:S(2)}) copy-start(f32[16,2048]{1,0:T(8,128)} %th_ref.7) | copy-start | bytes 393220
  6.1 8.5 %copy-start.14 = (f32[16,2048]{1,0:T(8,128)S(1)}, f32[16,2048]{1,0:T(8,128)}, u32[]{:S(2)}) copy-start(f32[16,2048]{1,0:T(8,128)} %rr_ref.3) | copy-start | bytes 393220
  6.1 8.5 %copy-start.16 = (f32[16,2048]{1,0:T(8,128)S(1)}, f32[16,2048]{1,0:T(8,128)}, u32[]{:S(2)}) copy-start(f32[16,2048]{1,0:T(8,128)} %ri_ref.3) | copy-start | bytes 393220
  10.2 1.4 %copy-start.9 = (f32[512,1024]{1,0:T(8,128)}, f32[512,1024]{1,0:T(8,128)S(1)}, u32[]{:S(2)}) copy-start(f32[512,1024]{1,0:T(8,128)S(1)} %get-tuple-element.22.l_ref) | copy-start | bytes 6291460
  11.6 8.6 %collective-permute-start = (f32[32,1024]{1,0:T(8,128)S(1)}, f32[32,1024]{1,0:T(8,128)S(1)}, u32[]{:S(2)}, u32[]{:S(2)}) collective-permute-start(f32[32,1024]{1,0:T(8,128)S(1)} %get-tuple-element.17), channel_id=1, source_target_pairs={{0,4},{4,0},{8,12},{12,8},{16,20},{20,16},{24,28},{28,24},{1,5},{5... | collective-permute-start | bytes 393224 | tf_op jit(solution)/shard_map/ppermute | solution.py:207
  18.8 1.3 %copy-start.11 = (f32[512,1024]{1,0:T(8,128)}, f32[512,1024]{1,0:T(8,128)S(1)}, u32[]{:S(2)}) copy-start(f32[512,1024]{1,0:T(8,128)S(1)} %get-tuple-element.19.l_ref) | copy-start | bytes 6291460
  20.1 0.8 %copy-start.17 = (f32[128,1024]{1,0:T(8,128)}, f32[128,1024]{1,0:T(8,128)S(1)}, u32[]{:S(2)}) copy-start(f32[128,1024]{1,0:T(8,128)S(1)} %get-tuple-element.20.hp_ref) | copy-start | bytes 1572868
  20.9 14.7 %copy-start.19 = (f32[2048]{0:T(1024)S(1)}, f32[2048]{0:T(1024)}, u32[]{:S(2)}) copy-start(f32[2048]{0:T(1024)} %param.16) | copy-start | bytes 24580
  20.9 5.0 %collective-permute-start.1 = (f32[32,1024]{1,0:T(8,128)S(1)}, f32[32,1024]{1,0:T(8,128)S(1)}, u32[]{:S(2)}, u32[]{:S(2)}) collective-permute-start(f32[32,1024]{1,0:T(8,128)S(1)} %maximum_add_fusion), channel_id=1, source_target_pairs={{0,8},{4,12},{8,0},{12,4},{16,24},{20,28},{24,16},{28,20},{1,9},{5... | collective-permute-start | bytes 393224 | tf_op jit(solution)/shard_map/ppermute | solution.py:207
  26.9 7.6 %collective-permute-start.2 = (f32[32,1024]{1,0:T(8,128)S(1)}, f32[32,1024]{1,0:T(8,128)S(1)}, u32[]{:S(2)}, u32[]{:S(2)}) collective-permute-start(f32[32,1024]{1,0:T(8,128)S(1)} %fusion), channel_id=1, source_target_pairs={{0,16},{4,20},{8,24},{12,28},{16,0},{20,4},{24,8},{28,12},{1,17},{... | collective-permute-start | bytes 393224 | tf_op jit(solution)/shard_map/ppermute | solution.py:207
  34.5 2.3 %copy-start.18 = (f32[128,1024]{1,0:T(8,128)S(1)}, f32[128,1024]{1,0:T(8,128)}, u32[]{:S(2)}) copy-start(f32[128,1024]{1,0:T(8,128)} %copy-done.17) | copy-start | bytes 1572868
  34.6 9.4 %collective-permute-start.3 = (f32[32,1024]{1,0:T(8,128)S(1)}, f32[32,1024]{1,0:T(8,128)S(1)}, u32[]{:S(2)}, u32[]{:S(2)}) collective-permute-start(f32[32,1024]{1,0:T(8,128)S(1)} %get-tuple-element.30), channel_id=1, source_target_pairs={{0,4},{4,0},{8,12},{12,8},{16,20},{20,16},{24,28},{28,24},{1,5},{5... | collective-permute-start | bytes 393224 | tf_op jit(solution)/shard_map/ppermute | solution.py:207
  36.8 1.3 %copy-start.4 = (bf16[256,2048]{1,0:T(8,128)(2,1)S(1)}, bf16[256,2048]{1,0:T(8,128)(2,1)}, u32[]{:S(2)}) copy-start(bf16[256,2048]{1,0:T(8,128)(2,1)} %q_ref.3) | copy-start | bytes 3145732
  36.8 1.9 %copy-start.12 = (f32[512,1024]{1,0:T(8,128)S(1)}, f32[512,1024]{1,0:T(8,128)}, u32[]{:S(2)}) copy-start(f32[512,1024]{1,0:T(8,128)} %copy-done.11) | copy-start | bytes 6291460
  38.7 5.3 %copy-start.10 = (f32[512,1024]{1,0:T(8,128)S(1)}, f32[512,1024]{1,0:T(8,128)}, u32[]{:S(2)}) copy-start(f32[512,1024]{1,0:T(8,128)} %copy-done.9) | copy-start | bytes 6291460
  44.0 10.3 %copy-start.20 = (f32[2048]{0:T(1024)S(1)}, f32[2048]{0:T(1024)}, u32[]{:S(2)}) copy-start(f32[2048]{0:T(1024)} %param.17) | copy-start | bytes 24580
  49.4 1.2 %collective-permute-start.4 = (f32[256]{0:T(256)S(1)}, f32[256]{0:T(256)S(1)}, u32[]{:S(2)}, u32[]{:S(2)}) collective-permute-start(f32[256]{0:T(256)S(1)} %add_reduce_fusion), channel_id=1, source_target_pairs={{0,1},{1,0},{2,3},{3,2},{4,5},{5,4},{6,7},{7,6},{8,9},{9,8},{10,11... | collective-permute-start | bytes 3080 | tf_op jit(solution)/shard_map/ppermute | solution.py:207
  50.6 3.6 %collective-permute-start.5 = (f32[256]{0:T(256)S(1)}, f32[256]{0:T(256)S(1)}, u32[]{:S(2)}, u32[]{:S(2)}) collective-permute-start(f32[256]{0:T(256)S(1)} %add.68), channel_id=1, source_target_pairs={{0,2},{1,3},{2,0},{3,1},{4,6},{5,7},{6,4},{7,5},{8,10},{9,11},{10,... | collective-permute-start | bytes 3080 | tf_op jit(solution)/shard_map/ppermute | solution.py:207

commit v2 on v1

v2 whole, which is shorter than its diff:
```python
import functools

import jax
import jax.numpy as jnp
from jax import lax
from jax.experimental import pallas as pl
from jax.experimental.pallas import tpu as pltpu
from jax.sharding import PartitionSpec as P

F32 = jnp.float32
SUB = 8
LANE = 128
BLOCK = 16
APART = BLOCK + 1
FETCH = 256
STORE = 512
TAIL = 2
TOKENS = 8
VMEM_LIMIT = 8 * 2**20


def cmul(ar, ai, br, bi):
    return ar * br - ai * bi, ar * bi + ai * br


def cos_sin(r, n):
    z = r * r
    s = r + r * z * (-1.66666667e-1 + z * (8.33333310e-3 + z * (-1.98409296e-4 + z * 2.7181716e-6)))
    c = 1.0 + z * (-0.5 + z * (4.16666664e-2 + z * (-1.38888642e-3 + z * 2.4760495e-5)))
    quarter = n - 4.0 * jnp.floor(n * 0.25)
    odd = (quarter == 1.0) | (quarter == 3.0)
    sin = jnp.where(odd, c, s)
    cos = jnp.where(odd, s, c)
    sin = jnp.where(quarter >= 2.0, -sin, sin)
    cos = jnp.where((quarter == 1.0) | (quarter == 2.0), -cos, cos)
    return cos, sin


def pole_power(decay, angle, count):
    phase = angle * float(count)
    n = jnp.floor(phase * 0.6366197723675814 + 0.5)
    r = ((phase - n * 1.5703125) - n * 4.837512969970703125e-4) - n * 7.549789948768648e-8
    cos, sin = cos_sin(r, n)
    size = jnp.exp(decay * -float(count))
    return size * cos, size * sin


def power_table(pr, pi, first_r, first_i, count):
    tr, ti = [first_r], [first_i]
    for _ in range(count - 1):
        r, i = cmul(tr[-1], ti[-1], pr, pi)
        tr.append(r)
        ti.append(i)
    return tr, ti


def squared(r, i, times):
    for _ in range(times):
        r, i = r * r - i * i, (r + r) * i
    return r, i


def lanes(start, group):
    return pl.ds(pl.multiple_of(start + group * LANE, LANE), LANE)


def row(ref, index, ls):
    return jnp.broadcast_to(ref[index : index + 1, ls], (SUB, LANE))


def pole_table(a_ref, th_ref, rr_ref, ri_ref, ms, src):
    decay, angle = a_ref[ms, src], th_ref[ms, src]
    pr, pi = pole_power(decay, angle, 1)
    weight = jnp.sqrt(decay)
    return pr, pi, power_table(pr, pi, weight * rr_ref[ms, src], weight * ri_ref[ms, src], BLOCK)


def stream(groups, stores, body):
    def copies(g):
        return [pltpu.make_async_copy(buf.at[g], out.at[g], sem.at[g]) for buf, out, sem in stores]

    def fill(g, carry):
        body(g)
        for copy in copies(g):
            copy.start()
        return carry

    def finish(g, carry):
        for copy in copies(g):
            copy.wait()
        return carry

    lax.fori_loop(0, groups, fill, 0)
    return lambda: lax.fori_loop(0, groups, finish, 0)


def rest(start, stop, body):
    def step(g, carry):
        body(g)
        return carry

    lax.fori_loop(start, stop, step, 0)


def end_states(mixed, poles, at, e_ref, l_buf, pw_ref=None):
    a_ref, th_ref = poles[:2]
    rows = mixed.shape[0]
    modes = a_ref.shape[0]
    src, dst = at
    every = slice(None)
    for m0 in range(0, modes, SUB):
        ms = slice(m0, m0 + SUB)
        pr, pi, (tr, ti) = pole_table(*poles, ms, src)
        qr, qi = squared(pr, pi, BLOCK.bit_length() - 1)
        sr = jnp.zeros((SUB, LANE), F32)
        si = jnp.zeros((SUB, LANE), F32)
        for b in range(rows // BLOCK):
            base = b * 2 * modes + m0
            if l_buf is not None:
                l_buf[base : base + SUB, :] = sr
                l_buf[base + modes : base + modes + SUB, :] = si
            sr, si = cmul(qr, qi, sr, si)
            for s in range(BLOCK):
                x = row(mixed, b * BLOCK + s, every)
                sr = sr + tr[BLOCK - 1 - s] * x
                si = si + ti[BLOCK - 1 - s] * x
        if e_ref is not None:
            e_ref[ms, dst] = sr
            e_ref[modes + m0 : modes + m0 + SUB, dst] = si
        if pw_ref is not None:
            wr, wi = pole_power(a_ref[ms, src], th_ref[ms, src], rows)
            pw_ref[ms, dst] = wr
            pw_ref[modes + m0 : modes + m0 + SUB, dst] = wi


def sent_kernel(off_ref, k_hbm, v_hbm, a_hbm, th_hbm, rr_hbm, ri_hbm, e_ref, l_hbm, kb, vb, pb, mixed, l_buf, kv_sem, p_sem, l_sem):
    half = e_ref.shape[1]
    chunks = half // FETCH
    base = off_ref[0] * half

    def there(c):
        return pl.ds(pl.multiple_of(base + c * FETCH, LANE), FETCH)

    def here(c):
        return pl.ds(pl.multiple_of(c * FETCH, LANE), FETCH)

    def fetches(c):
        return [
            pltpu.make_async_copy(src.at[:, there(c)], dst.at[:, here(c)], kv_sem.at[i, c])
            for i, (src, dst) in enumerate(((k_hbm, kb), (v_hbm, vb)))
        ]

    whole = pl.ds(pl.multiple_of(base, LANE), half)
    poles = [
        pltpu.make_async_copy(src.at[:, whole], pb.at[i], p_sem.at[i])
        for i, src in enumerate((a_hbm, th_hbm, rr_hbm, ri_hbm))
    ]
    for copy in fetches(0) + poles:
        copy.start()
    for c in range(1, chunks):
        for copy in fetches(c):
            copy.start()
    for copy in poles:
        copy.wait()

    def group(g, l_buf):
        @pl.when(lax.rem(g, FETCH // LANE) == 0)
        def _():
            for copy in fetches(g // (FETCH // LANE)):
                copy.wait()

        ls = lanes(0, g)
        mixed[...] = kb[:, ls].astype(F32) * vb[:, ls].astype(F32)
        end_states(mixed, [pb.at[i] for i in range(4)], (ls, ls), e_ref, l_buf)

    stored = l_hbm.shape[0]
    finish = stream(stored, [(l_buf, l_hbm, l_sem)], lambda g: group(g, l_buf.at[g]))
    rest(stored, half // LANE, lambda g: group(g, None))
    finish()


def own_kernel(off_ref, k_ref, v_ref, a_ref, th_ref, rr_ref, ri_ref, e_ref, pw_ref, l_hbm, mixed, l_buf, l_sem):
    half = e_ref.shape[1]

    def group(g, l_buf):
        src, dst = lanes(off_ref[0] * half, g), lanes(0, g)
        mixed[...] = k_ref[:, src].astype(F32) * v_ref[:, src].astype(F32)
        end_states(mixed, (a_ref, th_ref, rr_ref, ri_ref), (src, dst), e_ref, l_buf, pw_ref)

    stored = l_hbm.shape[0]
    finish = stream(stored, [(l_buf, l_hbm, l_sem)], lambda g: group(g, l_buf.at[g]))
    rest(stored, half // LANE, lambda g: group(g, None))
    finish()


def fill_table(table, pr, pi, m0, modes):
    tr, ti = power_table(pr, pi, pr, pi, BLOCK)
    for j in range(BLOCK):
        base = j * 2 * modes + m0
        table[base : base + SUB, :] = tr[j]
        table[base + modes : base + modes + SUB, :] = ti[j]


def near_kernel(
    off_ref, after_ref, k_ref, v_ref, a_ref, th_ref, rr_ref, ri_ref, skip_ref, *refs
):
    with_table = len(refs) > 8
    if with_table:
        l_hbm, y_hbm, table_hbm, plain, mixed, l_buf, y_buf, l_sem, y_sem, table_buf, table_sem = refs
    else:
        l_hbm, y_hbm, plain, mixed, l_buf, y_buf, l_sem, y_sem = refs
    rows = k_ref.shape[0]
    modes = a_ref.shape[0]
    groups = y_hbm.shape[0]
    half = groups * LANE
    blocks = rows // BLOCK

    def group(g):
        src = lanes(off_ref[0] * half, g)
        for b in range(blocks):
            bs = slice(b * BLOCK, (b + 1) * BLOCK)
            mixed[b * APART : b * APART + BLOCK, :] = k_ref[bs, src].astype(F32) * v_ref[bs, src].astype(F32)
        sums = None
        for m0 in range(0, modes, SUB):
            pr, pi, (tr, _) = pole_table(a_ref, th_ref, rr_ref, ri_ref, slice(m0, m0 + SUB), src)
            sums = tr if sums is None else [x + y for x, y in zip(sums, tr)]
            if with_table:
                fill_table(table_buf.at[g], pr, pi, m0, modes)
        taps = []
        for j in range(BLOCK):
            tap = jnp.sum(sums[j], axis=0, keepdims=True)
            if j == 0:
                tap = tap + skip_ref[0:1, src]
            taps.append(jnp.broadcast_to(tap, (SUB, LANE)))
        for a0 in range(0, blocks, SUB):
            acc = [None] * BLOCK
            for s in range(BLOCK):
                x = mixed[pl.ds(a0 * APART + s, SUB, stride=APART), :]
                for t in range(s, BLOCK):
                    part = taps[t - s] * x
                    acc[t] = part if acc[t] is None else acc[t] + part
            for t in range(BLOCK):
                y_buf[g, t * blocks + a0 : t * blocks + a0 + SUB, :] = acc[t]

    tail = l_hbm.shape[0]

    def states(i):
        src = lanes(off_ref[0] * half, groups - tail + i)
        plain[...] = k_ref[:, src].astype(F32) * v_ref[:, src].astype(F32)
        end_states(plain, (a_ref, th_ref, rr_ref, ri_ref), (src, src), None, l_buf.at[i])

    finish_states = stream(tail, [(l_buf, l_hbm, l_sem)], states)
    stores = [(y_buf, y_hbm, y_sem)] + ([(table_buf, table_hbm, table_sem)] if with_table else [])
    finish = stream(groups, stores, group)
    finish_states()
    finish()


def far_kernel(with_table, off_ref, s_ref, l_ref, tail_ref, y_ref, q_ref, *refs):
    if with_table:
        table_ref, gated_ref, power_ref, state, conv = refs
    else:
        a_ref, th_ref, gated_ref, power_ref, state, conv, own_table = refs
    rows = q_ref.shape[0]
    modes = s_ref.shape[0] // 2
    groups = y_ref.shape[0]
    half = groups * LANE
    blocks = rows // BLOCK
    starts = range(0, blocks, SUB)
    apart = 2 * modes + 1
    every = slice(None)
    power_ref[...] = jnp.zeros_like(power_ref)

    def group(g, l_ref):
        src, dst = lanes(off_ref[0] * half, g), lanes(0, g)
        table = table_ref.at[g] if with_table else own_table
        for m0 in range(0, modes, SUB):
            ms = slice(m0, m0 + SUB)
            if not with_table:
                fill_table(table, *pole_power(a_ref[ms, src], th_ref[ms, src], 1), m0, modes)
            last = (BLOCK - 1) * 2 * modes + m0
            qr, qi = table[last : last + SUB, :], table[last + modes : last + modes + SUB, :]
            sr, si = s_ref[ms, dst], s_ref[modes + m0 : modes + m0 + SUB, dst]
            for b in range(blocks):
                at = b * 2 * modes + m0
                to = b * apart + m0
                state[to : to + SUB, :] = l_ref[at : at + SUB, :] + sr
                state[to + modes : to + modes + SUB, :] = l_ref[at + modes : at + modes + SUB, :] + si
                if b < blocks - 1:
                    sr, si = cmul(qr, qi, sr, si)
        for t0 in range(0, BLOCK, TOKENS):
            acc = {
                (t, a0): y_ref[g, t * blocks + a0 : t * blocks + a0 + SUB, :]
                for t in range(t0, t0 + TOKENS)
                for a0 in starts
            }
            for m in range(modes):
                cr = {a0: state[pl.ds(a0 * apart + m, SUB, stride=apart), :] for a0 in starts}
                ci = {a0: state[pl.ds(a0 * apart + modes + m, SUB, stride=apart), :] for a0 in starts}
                for t in range(t0, t0 + TOKENS):
                    br = row(table, t * 2 * modes + m, every)
                    bi = row(table, t * 2 * modes + modes + m, every)
                    for a0 in starts:
                        acc[t, a0] = acc[t, a0] + cr[a0] * br - ci[a0] * bi
            for (t, a0), y in acc.items():
                conv[pl.ds(a0 * APART + t, SUB, stride=APART), :] = y
        for b in range(blocks):
            bs = slice(b * BLOCK, (b + 1) * BLOCK)
            gated = q_ref[bs, src].astype(F32) * conv[b * APART : b * APART + BLOCK, :]
            gated_ref[bs, dst] = gated
            power_ref[bs, :] += gated * gated

    stored = l_ref.shape[0]
    rest(0, stored, lambda g: group(g, l_ref.at[g]))
    rest(stored, groups, lambda g: group(g, tail_ref.at[g - stored]))


def norm_kernel(off_ref, own_ref, other_ref, scale_ref, gain_ref, out_hbm, buf, sem):
    half = own_ref.shape[1]
    copies = []
    for ref, base in ((own_ref, off_ref[0] * half), (other_ref, (1 - off_ref[0]) * half)):
        for first in range(0, half, STORE):
            at = len(copies) * STORE
            for g in range(STORE // LANE):
                gain = gain_ref[0:1, lanes(base + first, g)]
                gated = ref[:, first + g * LANE : first + (g + 1) * LANE]
                buf[:, at + g * LANE : at + (g + 1) * LANE] = (gated * gain * scale_ref[...]).astype(buf.dtype)
            to = pl.ds(pl.multiple_of(base + first, LANE), STORE)
            copies.append(pltpu.make_async_copy(buf.at[:, at : at + STORE], out_hbm.at[:, to], sem.at[len(copies)]))
            copies[-1].start()
    for copy in copies:
        copy.wait()


def call(kernel, offset, ins, outs, far_outs, scratch, space=pltpu.VMEM, dtype=F32):
    return pl.pallas_call(
        kernel,
        in_specs=[pl.BlockSpec(memory_space=pltpu.SMEM)] + [pl.BlockSpec(memory_space=space)] * len(ins),
        out_specs=[pl.BlockSpec(memory_space=pltpu.VMEM)] * len(outs)
        + [pl.BlockSpec(memory_space=pltpu.HBM)] * len(far_outs),
        out_shape=[pltpu.VMEM(shape, dtype) for shape in outs] + [pltpu.HBM(shape, dtype) for shape in far_outs],
        scratch_shapes=scratch,
        compiler_params=pltpu.CompilerParams(vmem_limit_bytes=VMEM_LIMIT),
    )(offset, *[pltpu.with_memory_space_constraint(x, space) for x in ins])


def exchange(x, axis, distance):
    return lax.ppermute(x, axis, [(i, i ^ distance) for i in range(lax.axis_size(axis))])


def parts(x):
    half = x.shape[0] // 2
    return x[:half], x[half:]


def times(x, y):
    return jnp.concatenate(cmul(*parts(x), *parts(y)))


def per_device(q, k, v, decay, angle, res_r, res_i, skip_gain, norm_gain):
    rows, width = q.shape
    modes = decay.shape[0]
    half = width // 2
    blocks = rows // BLOCK
    count = lax.axis_size("seq")
    me = lax.axis_index("seq")
    upper = (me & 1) == 1
    own = (me & 1).astype(jnp.int32).reshape(1)
    other = 1 - own
    skip = skip_gain.reshape(1, width)
    gain = norm_gain.reshape(1, width)
    states = 2 * modes
    poles = (decay, angle, res_r, res_i)
    mixed = pltpu.VMEM((rows, LANE), F32)
    padded = pltpu.VMEM((blocks * APART, LANE), F32)
    state = (states, half)
    groups = half // LANE
    local = (groups - TAIL, blocks * states, LANE)
    tail = (TAIL, blocks * states, LANE)
    table = (groups, BLOCK * states, LANE)
    near_shape = (groups, rows, LANE)

    group_sem = pltpu.SemaphoreType.DMA((groups,))
    stored_sem = pltpu.SemaphoreType.DMA((groups - TAIL,))

    def near(offset, after, with_table):
        ins = [after, k, v, *poles, skip]
        outs = [tail, near_shape]
        tail_sem = pltpu.SemaphoreType.DMA((TAIL,))
        scratch = [mixed, padded, pltpu.VMEM(tail, F32), pltpu.VMEM(near_shape, F32), tail_sem, group_sem]
        if with_table:
            outs.append(table)
            scratch += [pltpu.VMEM(table, F32), group_sem]
        return call(near_kernel, offset, ins, [], outs, scratch)

    def far(offset, start, local, tail, y, *table):
        ins = [start, local, tail, y, q, *(table or (decay, angle))]
        scratch = [pltpu.VMEM((blocks * (states + 1), LANE), F32), padded]
        if not table:
            scratch.append(pltpu.VMEM((BLOCK * states, LANE), F32))
        kernel = functools.partial(far_kernel, bool(table))
        return call(kernel, offset, ins, [(rows, half), (rows, LANE)], [], scratch)

    scratch = [
        pltpu.VMEM((rows, half), k.dtype),
        pltpu.VMEM((rows, half), v.dtype),
        pltpu.VMEM((4, modes, half), F32),
        mixed,
        pltpu.VMEM(local, F32),
        pltpu.SemaphoreType.DMA((2, half // FETCH)),
        pltpu.SemaphoreType.DMA((4,)),
        stored_sem,
    ]
    sent_end, sent_local = call(sent_kernel, other, [k, v, *poles], [state], [local], scratch, pltpu.HBM)
    pair_end = exchange(sent_end, "seq", 1)
    scratch = [mixed, pltpu.VMEM(local, F32), stored_sem]
    own_end, step_power, own_local = call(own_kernel, own, [k, v, *poles], [state] * 2, [local], scratch)
    low = jnp.where(upper, pair_end, own_end)
    high = jnp.where(upper, own_end, pair_end)
    total = times(step_power, low) + high
    before = mine = None
    jump = times(step_power, step_power)
    pending = [own, other]
    ready = []
    distance = 2
    while distance < count:
        got = exchange(total, "seq", distance)
        if pending:
            ready.append(near(pending.pop(0), total, False))
            got, ready[-1] = lax.optimization_barrier((got, ready[-1]))
        above = (me & distance) != 0
        if before is None:
            before = jnp.where(above, got, 0.0)
            mine = jnp.concatenate([jnp.where(above, parts(jump)[0], 1.0), jnp.where(above, parts(jump)[1], 0.0)])
        else:
            before = jnp.where(above, before + times(mine, got), before)
            mine = jnp.where(above, times(mine, jump), mine)
        total = jnp.where(above, times(jump, got) + total, times(jump, total) + got)
        jump = times(jump, jump)
        distance *= 2
    for offset in pending:
        ready.append(near(offset, total, False))
    after_low = times(step_power, before) + low
    own_start = jnp.where(upper, after_low, before)
    other_start = exchange(jnp.where(upper, before, after_low), "seq", 1)
    own_gated, own_power = far(own, own_start, own_local, *ready[0])
    other_gated, other_power = far(other, other_start, sent_local, *ready[1])
    power = jnp.sum(own_power + other_power, axis=1)
    distance = 1
    while distance < lax.axis_size("ch"):
        power = power + exchange(power, "ch", distance)
        distance *= 2
    scale = lax.rsqrt(power / (width * lax.axis_size("ch")) + 1e-05)
    scale = jnp.broadcast_to(scale[:, None], (rows, LANE))
    scratch = [pltpu.VMEM((rows, width), jnp.bfloat16), pltpu.SemaphoreType.DMA((width // STORE,))]
    ins = [own_gated, other_gated, scale, gain]
    return call(norm_kernel, own, ins, [], [(rows, width)], scratch, dtype=jnp.bfloat16)[0]


def solution(mesh):
    rows = P("seq", "ch")
    poles = P(None, "ch")
    return jax.shard_map(
        per_device,
        mesh=mesh,
        in_specs=(rows, rows, rows, poles, poles, poles, poles, P("ch"), P("ch")),
        out_specs=rows,
        check_vma=False,
    )
```

time: 58.1 us -> 40.2 us (0.69)
  local copies, waits for them, and re-layouts: 9.51 us -> 0.16 us
  waiting for transfers between devices: 11 us -> 6.97 us
  other arithmetic: 2.84 us -> 0.39 us
  Pallas kernels: 24.8 us -> 22.6 us
    unnamed x42 -> x30, local copies, waits for them, and re-layouts: 9.41 us -> 0.07 us
    ppermute x6, waiting for transfers between devices: 11 us -> 6.97 us  [exchange(): lax.ppermute(x, axis, [(i, i ^ distance) for i in range(lax.axis_size(axi...]
    pallas_call x7, Pallas kernels: 24.8 us -> 22.6 us  [call(): pl.pallas_call(kernel, in_specs=[pl.BlockSpec(memory_space=pltpu.SMEM)] +...]
    sub x4 -> x5, other arithmetic: 1.65 us -> 0.12 us  [cmul(): return (ar * br - ai * bi, ar * bi + ai * br)]
    select_n x1 -> x0, other arithmetic: 0.92 us -> none  [per_device(): mine = jnp.where(above, times(mine, jump), mine)]
  transfers between devices with their start and end apart: 6 -> 6, of which waited for: 4 -> 5; matrix products, arithmetic and copies ran while one was open for 2% -> 0% of each run, Pallas kernels for 21% -> 32%
where the time goes in v2:
time: 40.2 us; the launch traced here: 40.1 us
  Pallas kernels  22.6 us (56%)
  starting transfers between devices  9.7 us (24%)
  waiting for transfers between devices  6.97 us (17%)
    pallas_call x7, Pallas kernels, call(): pl.pallas_call(kernel, in_specs=[pl.BlockSpec(memory_space=pltpu.SMEM)] +...  22.6 us
    ppermute x6, starting transfers between devices, exchange(): lax.ppermute(x, axis, [(i, i ^ distance) for i in range(lax.axis_size(axi...  9.7 us
    ppermute x6, waiting for transfers between devices, exchange(): lax.ppermute(x, axis, [(i, i ^ distance) for i in range(lax.axis_size(axi...  6.97 us
  transfers between devices with their start and end apart: 6, of which 5 were waited for; matrix products, arithmetic and copies ran while one was open for 0% of the time, Pallas kernels for 32%

profile of v2, /device:TPU:0, one launch (start us, length us, event | category | flops | bytes accessed | tf_op | source)
XLA Modules:
  0.0 40.1 jit_solution(9712405433823296790)
XLA Ops:
  0.0 0.0 copy-start
  0.0 5.3 %shard_map.92 = (f32[32,1024]{1,0:T(8,128)S(1)}, f32[6,512,128]{2,1,0:T(8,128)}) custom-call(s32[1]{0:T(128)S(6)} %sub.21.off_ref, bf16[256,2048]{1,0:T(8,128)(2,1)} %k_ref.5, bf16[256,2048]{1,0:T(8,128)(2,1)} %v_ref.5, f32[16,2048]{1,0:T(8,128)} %refs_0_.3, f32[16,2048]{1,0:T(8,128)} %refs_1_.3, f32[16,2048]{1,0:T(8,128)} %rr_ref.5, f32[16,2048]{1,0:T(8,128)} %ri_ref.5), custom_call_target="tpu_custom_call" | custom-call | tf_op jit(solution)/shard_map/pallas_call | solution.py:336
  5.3 3.0 %collective-permute-start = (f32[32,1024]{1,0:T(8,128)S(1)}, f32[32,1024]{1,0:T(8,128)S(1)}, u32[]{:S(2)}, u32[]{:S(2)}) collective-permute-start(f32[32,1024]{1,0:T(8,128)S(1)} %get-tuple-element.25), channel_id=1, source_target_pairs={{0,4},{4,0},{8,12},{12,8},{16,20},{20,16},{24,28},{28,24},{1,5},{5... | collective-permute-start | bytes 393224 | tf_op jit(solution)/shard_map/ppermute | solution.py:348
  8.4 0.0 copy-done.6
  8.4 0.0 copy-start.13
  8.4 3.8 %shard_map.91 = (f32[32,1024]{1,0:T(8,128)S(1)}, f32[32,1024]{1,0:T(8,128)S(1)}, f32[6,512,128]{2,1,0:T(8,128)}) custom-call(s32[1]{0:T(128)} %bitcast.off_ref, bf16[256,2048]{1,0:T(8,128)(2,1)S(1)} %copy-done, bf16[256,2048]{1,0:T(8,128)(2,1)S(1)} %copy-done.1, f32[16,2048]{1,0:T(8,128)S(1)} %copy-done.2, f32[16,2048]{1,0:T(8,128)S(1)} %copy-done.3, ...), custom_call_target="tpu_custom_call" | custom-call | tf_op jit(solution)/shard_map/pallas_call | solution.py:336
  12.3 0.0 collective-permute-done
  12.4 1.6 %collective-permute-start.1 = (f32[32,1024]{1,0:T(8,128)S(1)}, f32[32,1024]{1,0:T(8,128)S(1)}, u32[]{:S(2)}, u32[]{:S(2)}) collective-permute-start(f32[32,1024]{1,0:T(8,128)S(1)} %maximum_add_fusion.after_ref), channel_id=1, source_target_pairs={{0,8},{4,12},{8,0},{12,4},{16,24},{20,28},{24,16},{28,20},{1,9},{5... | collective-permute-start | bytes 393224 | tf_op jit(solution)/shard_map/ppermute | solution.py:348
  14.0 0.0 copy-done.13
  14.0 3.0 %shard_map.93 = (f32[2,512,128]{2,1,0:T(8,128)}, f32[8,256,128]{2,1,0:T(8,128)}) custom-call(s32[1]{0:T(128)} %bitcast.off_ref, f32[32,1024]{1,0:T(8,128)S(1)} %maximum_add_fusion.after_ref, bf16[256,2048]{1,0:T(8,128)(2,1)S(1)} %copy-done, bf16[256,2048]{1,0:T(8,128)(2,1)S(1)} %copy-done.1, f32[16,2048]{1,0:T(8,128)S(1)} %copy-done.2, ...), custom_call_target="tpu_custom_call" | custom-call | tf_op jit(solution)/shard_map/pallas_call | solution.py:336
  17.0 0.4 collective-permute-done.1
  17.5 2.7 %collective-permute-start.2 = (f32[32,1024]{1,0:T(8,128)S(1)}, f32[32,1024]{1,0:T(8,128)S(1)}, u32[]{:S(2)}, u32[]{:S(2)}) collective-permute-start(f32[32,1024]{1,0:T(8,128)S(1)} %fusion.after_ref), channel_id=1, source_target_pairs={{0,16},{4,20},{8,24},{12,28},{16,0},{20,4},{24,8},{28,12},{1,17},{... | collective-permute-start | bytes 393224 | tf_op jit(solution)/shard_map/ppermute | solution.py:348
  20.1 3.0 %shard_map.94 = (f32[2,512,128]{2,1,0:T(8,128)}, f32[8,256,128]{2,1,0:T(8,128)}) custom-call(s32[1]{0:T(128)S(6)} %sub.21.off_ref, f32[32,1024]{1,0:T(8,128)S(1)} %fusion.after_ref, bf16[256,2048]{1,0:T(8,128)(2,1)S(1)} %copy-done, bf16[256,2048]{1,0:T(8,128)(2,1)S(1)} %copy-done.1, f32[16,2048]{1,0:T(8,128)S(1)} %copy-done.2, f32[16,2048]{1,0:T(8,128)S(1)} %copy-done.3, ...), custom_call_target="tpu_custom_call" | custom-call | tf_op jit(solution)/shard_map/pallas_call | solution.py:336
  23.1 0.0 copy-start.4
  23.1 0.0 copy-start.11
  23.1 2.4 %collective-permute-done.2 = f32[32,1024]{1,0:T(8,128)S(1)} collective-permute-done((f32[32,1024]{1,0:T(8,128)S(1)}, f32[32,1024]{1,0:T(8,128)S(1)}, u32[]{:S(2)}, u32[]{:S(2)}) %collective-permute-start.2) | collective-permute-done | bytes 131104 | tf_op jit(solution)/shard_map/ppermute | solution.py:348
  25.7 0.8 %collective-permute-start.3 = (f32[32,1024]{1,0:T(8,128)S(1)}, f32[32,1024]{1,0:T(8,128)S(1)}, u32[]{:S(2)}, u32[]{:S(2)}) collective-permute-start(f32[32,1024]{1,0:T(8,128)S(1)} %get-tuple-element.46), channel_id=1, source_target_pairs={{0,4},{4,0},{8,12},{12,8},{16,20},{20,16},{24,28},{28,24},{1,5},{5... | collective-permute-start | bytes 393224 | tf_op jit(solution)/shard_map/ppermute | solution.py:348
  26.5 0.0 copy-done.8
  26.5 0.0 copy-done.4
  26.5 3.2 %shard_map.95 = (f32[256,1024]{1,0:T(8,128)S(1)}, f32[256,128]{1,0:T(8,128)S(1)}) custom-call(s32[1]{0:T(128)} %bitcast.off_ref, f32[32,1024]{1,0:T(8,128)S(1)} %get-tuple-element.47.s_ref, f32[6,512,128]{2,1,0:T(8,128)S(1)} %copy-done.8, f32[2,512,128]{2,1,0:T(8,128)S(1)} %copy-done.11, f32[8,256,128]{2,1,0:T(8,128)S(1)} %copy-done.9, ...), custom_call_target="tpu_custom_call" | custom-call | tf_op jit(solution)/shard_map/pallas_call | solution.py:336
  29.7 1.0 %collective-permute-done.3.s_ref = f32[32,1024]{1,0:T(8,128)S(1)} collective-permute-done((f32[32,1024]{1,0:T(8,128)S(1)}, f32[32,1024]{1,0:T(8,128)S(1)}, u32[]{:S(2)}, u32[]{:S(2)}) %collective-permute-start.3) | collective-permute-done | bytes 131104 | tf_op jit(solution)/shard_map/ppermute | solution.py:348
  30.7 0.0 copy-done.7
  30.7 0.0 copy-start.14
  30.7 3.2 %shard_map.96 = (f32[256,1024]{1,0:T(8,128)S(1)}, f32[256,128]{1,0:T(8,128)S(1)}) custom-call(s32[1]{0:T(128)S(6)} %sub.21.off_ref, f32[32,1024]{1,0:T(8,128)S(1)} %collective-permute-done.3.s_ref, f32[6,512,128]{2,1,0:T(8,128)S(1)} %copy-done.7, f32[2,512,128]{2,1,0:T(8,128)S(1)} %copy-done.12, f32[8,256,128]{2,1,0:T(8,128)S(1)} %copy-done.10, ...), custom_call_target="tpu_custom_call" | custom-call | tf_op jit(solution)/shard_map/pallas_call | solution.py:336
  34.0 0.1 add_reduce_fusion
  34.1 0.1 collective-permute-start.4
  34.2 1.1 %collective-permute-done.4 = f32[256]{0:T(256)S(1)} collective-permute-done((f32[256]{0:T(256)S(1)}, f32[256]{0:T(256)S(1)}, u32[]{:S(2)}, u32[]{:S(2)}) %collective-permute-start.4) | collective-permute-done | bytes 1056 | tf_op jit(solution)/shard_map/ppermute | solution.py:348
  35.3 1.5 %collective-permute-start.5 = (f32[256]{0:T(256)S(1)}, f32[256]{0:T(256)S(1)}, u32[]{:S(2)}, u32[]{:S(2)}) collective-permute-start(f32[256]{0:T(256)S(1)} %add.60), channel_id=1, source_target_pairs={{0,2},{1,3},{2,0},{3,1},{4,6},{5,7},{6,4},{7,5},{8,10},{9,11},{10,... | collective-permute-start | bytes 3080 | tf_op jit(solution)/shard_map/ppermute | solution.py:348
  36.8 2.1 %collective-permute-done.5 = f32[256]{0:T(256)S(1)} collective-permute-done((f32[256]{0:T(256)S(1)}, f32[256]{0:T(256)S(1)}, u32[]{:S(2)}, u32[]{:S(2)}) %collective-permute-start.5) | collective-permute-done | bytes 1056 | tf_op jit(solution)/shard_map/ppermute | solution.py:348
  38.9 0.1 broadcast_in_dim.20.scale_ref
  39.0 0.0 copy-done.14
  39.0 1.1 %shard_map.97 = bf16[256,2048]{1,0:T(8,128)(2,1)} custom-call(s32[1]{0:T(128)} %bitcast.off_ref, f32[256,1024]{1,0:T(8,128)S(1)} %get-tuple-element.36.own_ref, f32[256,1024]{1,0:T(8,128)S(1)} %get-tuple-element.40.other_ref, f32[256,128]{1,0:T(8,128)S(1)} %broadcast_in_dim.20.scale_ref, f32[1,2048]{1,0:T(1,128)S(1)} %bitcast.5), custom_call_target="tpu_custom_call" | custom-call | tf_op jit(solution)/shard_map/pallas_call | solution.py:336
  (31 shorter events, 0.3 us)
Async XLA Ops:
  0.0 8.4 %copy-start.3 = (f32[16,2048]{1,0:T(8,128)S(1)}, f32[16,2048]{1,0:T(8,128)}, u32[]{:S(2)}) copy-start(f32[16,2048]{1,0:T(8,128)} %refs_1_.3) | copy-start | bytes 393220
  0.0 8.4 %copy-start.2 = (f32[16,2048]{1,0:T(8,128)S(1)}, f32[16,2048]{1,0:T(8,128)}, u32[]{:S(2)}) copy-start(f32[16,2048]{1,0:T(8,128)} %refs_0_.3) | copy-start | bytes 393220
  0.0 8.4 %copy-start.6 = (f32[16,2048]{1,0:T(8,128)S(1)}, f32[16,2048]{1,0:T(8,128)}, u32[]{:S(2)}) copy-start(f32[16,2048]{1,0:T(8,128)} %ri_ref.5) | copy-start | bytes 393220
  0.0 8.4 %copy-start.5 = (f32[16,2048]{1,0:T(8,128)S(1)}, f32[16,2048]{1,0:T(8,128)}, u32[]{:S(2)}) copy-start(f32[16,2048]{1,0:T(8,128)} %rr_ref.5) | copy-start | bytes 393220
  0.0 8.4 %copy-start.1 = (bf16[256,2048]{1,0:T(8,128)(2,1)S(1)}, bf16[256,2048]{1,0:T(8,128)(2,1)}, u32[]{:S(2)}) copy-start(bf16[256,2048]{1,0:T(8,128)(2,1)} %v_ref.5) | copy-start | bytes 3145732
  0.0 8.4 %copy-start = (bf16[256,2048]{1,0:T(8,128)(2,1)S(1)}, bf16[256,2048]{1,0:T(8,128)(2,1)}, u32[]{:S(2)}) copy-start(bf16[256,2048]{1,0:T(8,128)(2,1)} %k_ref.5) | copy-start | bytes 3145732
  5.3 7.0 %collective-permute-start = (f32[32,1024]{1,0:T(8,128)S(1)}, f32[32,1024]{1,0:T(8,128)S(1)}, u32[]{:S(2)}, u32[]{:S(2)}) collective-permute-start(f32[32,1024]{1,0:T(8,128)S(1)} %get-tuple-element.25), channel_id=1, source_target_pairs={{0,4},{4,0},{8,12},{12,8},{16,20},{20,16},{24,28},{28,24},{1,5},{5... | collective-permute-start | bytes 393224 | tf_op jit(solution)/shard_map/ppermute | solution.py:348
  8.4 5.6 %copy-start.13 = (f32[2048]{0:T(1024)S(1)}, f32[2048]{0:T(1024)}, u32[]{:S(2)}) copy-start(f32[2048]{0:T(1024)} %param.16) | copy-start | bytes 24580
  12.4 5.0 %collective-permute-start.1 = (f32[32,1024]{1,0:T(8,128)S(1)}, f32[32,1024]{1,0:T(8,128)S(1)}, u32[]{:S(2)}, u32[]{:S(2)}) collective-permute-start(f32[32,1024]{1,0:T(8,128)S(1)} %maximum_add_fusion.after_ref), channel_id=1, source_target_pairs={{0,8},{4,12},{8,0},{12,4},{16,24},{20,28},{24,16},{28,20},{1,9},{5... | collective-permute-start | bytes 393224 | tf_op jit(solution)/shard_map/ppermute | solution.py:348
  17.5 8.1 %collective-permute-start.2 = (f32[32,1024]{1,0:T(8,128)S(1)}, f32[32,1024]{1,0:T(8,128)S(1)}, u32[]{:S(2)}, u32[]{:S(2)}) collective-permute-start(f32[32,1024]{1,0:T(8,128)S(1)} %fusion.after_ref), channel_id=1, source_target_pairs={{0,16},{4,20},{8,24},{12,28},{16,0},{20,4},{24,8},{28,12},{1,17},{... | collective-permute-start | bytes 393224 | tf_op jit(solution)/shard_map/ppermute | solution.py:348
  20.1 6.3 %copy-start.8 = (f32[6,512,128]{2,1,0:T(8,128)S(1)}, f32[6,512,128]{2,1,0:T(8,128)}, u32[]{:S(2)}) copy-start(f32[6,512,128]{2,1,0:T(8,128)} %get-tuple-element.33.l_ref) | copy-start | bytes 4718596
  20.1 6.3 %copy-start.9 = (f32[8,256,128]{2,1,0:T(8,128)S(1)}, f32[8,256,128]{2,1,0:T(8,128)}, u32[]{:S(2)}) copy-start(f32[8,256,128]{2,1,0:T(8,128)} %get-tuple-element.35.y_ref) | copy-start | bytes 3145732
  23.1 3.4 %copy-start.4 = (bf16[256,2048]{1,0:T(8,128)(2,1)S(1)}, bf16[256,2048]{1,0:T(8,128)(2,1)}, u32[]{:S(2)}) copy-start(bf16[256,2048]{1,0:T(8,128)(2,1)} %q_ref.3) | copy-start | bytes 3145732
  23.1 3.4 %copy-start.11 = (f32[2,512,128]{2,1,0:T(8,128)S(1)}, f32[2,512,128]{2,1,0:T(8,128)}, u32[]{:S(2)}) copy-start(f32[2,512,128]{2,1,0:T(8,128)} %get-tuple-element.34.tail_ref) | copy-start | bytes 1572868
  25.7 5.0 %collective-permute-start.3 = (f32[32,1024]{1,0:T(8,128)S(1)}, f32[32,1024]{1,0:T(8,128)S(1)}, u32[]{:S(2)}, u32[]{:S(2)}) collective-permute-start(f32[32,1024]{1,0:T(8,128)S(1)} %get-tuple-element.46), channel_id=1, source_target_pairs={{0,4},{4,0},{8,12},{12,8},{16,20},{20,16},{24,28},{28,24},{1,5},{5... | collective-permute-start | bytes 393224 | tf_op jit(solution)/shard_map/ppermute | solution.py:348
  26.5 4.2 %copy-start.7 = (f32[6,512,128]{2,1,0:T(8,128)S(1)}, f32[6,512,128]{2,1,0:T(8,128)}, u32[]{:S(2)}) copy-start(f32[6,512,128]{2,1,0:T(8,128)} %get-tuple-element.37.l_ref) | copy-start | bytes 4718596
  26.5 4.2 %copy-start.10 = (f32[8,256,128]{2,1,0:T(8,128)S(1)}, f32[8,256,128]{2,1,0:T(8,128)}, u32[]{:S(2)}) copy-start(f32[8,256,128]{2,1,0:T(8,128)} %get-tuple-element.39.y_ref) | copy-start | bytes 3145732
  26.5 4.2 %copy-start.12 = (f32[2,512,128]{2,1,0:T(8,128)S(1)}, f32[2,512,128]{2,1,0:T(8,128)}, u32[]{:S(2)}) copy-start(f32[2,512,128]{2,1,0:T(8,128)} %get-tuple-element.38.tail_ref) | copy-start | bytes 1572868
  30.7 8.3 %copy-start.14 = (f32[2048]{0:T(1024)S(1)}, f32[2048]{0:T(1024)}, u32[]{:S(2)}) copy-start(f32[2048]{0:T(1024)} %param.17) | copy-start | bytes 24580
  34.1 1.2 %collective-permute-start.4 = (f32[256]{0:T(256)S(1)}, f32[256]{0:T(256)S(1)}, u32[]{:S(2)}, u32[]{:S(2)}) collective-permute-start(f32[256]{0:T(256)S(1)} %add_reduce_fusion), channel_id=1, source_target_pairs={{0,1},{1,0},{2,3},{3,2},{4,5},{5,4},{6,7},{7,6},{8,9},{9,8},{10,11... | collective-permute-start | bytes 3080 | tf_op jit(solution)/shard_map/ppermute | solution.py:348
  35.3 3.6 %collective-permute-start.5 = (f32[256]{0:T(256)S(1)}, f32[256]{0:T(256)S(1)}, u32[]{:S(2)}, u32[]{:S(2)}) collective-permute-start(f32[256]{0:T(256)S(1)} %add.60), channel_id=1, source_target_pairs={{0,2},{1,3},{2,0},{3,1},{4,6},{5,7},{6,4},{7,5},{8,10},{9,11},{10,... | collective-permute-start | bytes 3080 | tf_op jit(solution)/shard_map/ppermute | solution.py:348

commit v3 on v2

--- a/solution.py
+++ b/solution.py
@@ -108,29 +108,35 @@
     modes = a_ref.shape[0]
     src, dst = at
     every = slice(None)
-    for m0 in range(0, modes, SUB):
+    starts = range(0, modes, SUB)
+    tables, jump, state = {}, {}, {}
+    for m0 in starts:
         ms = slice(m0, m0 + SUB)
-        pr, pi, (tr, ti) = pole_table(*poles, ms, src)
-        qr, qi = squared(pr, pi, BLOCK.bit_length() - 1)
-        sr = jnp.zeros((SUB, LANE), F32)
-        si = jnp.zeros((SUB, LANE), F32)
-        for b in range(rows // BLOCK):
-            base = b * 2 * modes + m0
-            if l_buf is not None:
-                l_buf[base : base + SUB, :] = sr
-                l_buf[base + modes : base + modes + SUB, :] = si
-            sr, si = cmul(qr, qi, sr, si)
-            for s in range(BLOCK):
-                x = row(mixed, b * BLOCK + s, every)
-                sr = sr + tr[BLOCK - 1 - s] * x
-                si = si + ti[BLOCK - 1 - s] * x
-        if e_ref is not None:
-            e_ref[ms, dst] = sr
-            e_ref[modes + m0 : modes + m0 + SUB, dst] = si
+        pr, pi, tables[m0] = pole_table(*poles, ms, src)
+        jump[m0] = squared(pr, pi, BLOCK.bit_length() - 1)
+        state[m0] = jnp.zeros((SUB, LANE), F32), jnp.zeros((SUB, LANE), F32)
         if pw_ref is not None:
             wr, wi = pole_power(a_ref[ms, src], th_ref[ms, src], rows)
             pw_ref[ms, dst] = wr
             pw_ref[modes + m0 : modes + m0 + SUB, dst] = wi
+    for b in range(rows // BLOCK):
+        enter = {}
+        for s in range(BLOCK):
+            x = row(mixed, b * BLOCK + s, every)
+            for m0 in starts:
+                r, i = tables[m0][0][BLOCK - 1 - s] * x, tables[m0][1][BLOCK - 1 - s] * x
+                enter[m0] = (r, i) if s == 0 else (enter[m0][0] + r, enter[m0][1] + i)
+        for m0 in starts:
+            base = b * 2 * modes + m0
+            sr, si = state[m0]
+            if l_buf is not None:
+                l_buf[base : base + SUB, :] = sr
+                l_buf[base + modes : base + modes + SUB, :] = si
+            sr, si = cmul(*jump[m0], sr, si)
+            state[m0] = sr + enter[m0][0], si + enter[m0][1]
+    if e_ref is not None:
+        for m0 in starts:
+            e_ref[m0 : m0 + SUB, dst], e_ref[modes + m0 : modes + m0 + SUB, dst] = state[m0]
 
 
 def sent_kernel(off_ref, k_hbm, v_hbm, a_hbm, th_hbm, rr_hbm, ri_hbm, e_ref, l_hbm, kb, vb, pb, mixed, l_buf, kv_sem, p_sem, l_sem):
@@ -155,19 +161,22 @@
         pltpu.make_async_copy(src.at[:, whole], pb.at[i], p_sem.at[i])
         for i, src in enumerate((a_hbm, th_hbm, rr_hbm, ri_hbm))
     ]
-    for copy in fetches(0) + poles:
+    for copy in poles + fetches(0) + fetches(1):
         copy.start()
-    for c in range(1, chunks):
-        for copy in fetches(c):
-            copy.start()
     for copy in poles:
         copy.wait()
 
     def group(g, l_buf):
         @pl.when(lax.rem(g, FETCH // LANE) == 0)
         def _():
-            for copy in fetches(g // (FETCH // LANE)):
+            c = g // (FETCH // LANE)
+            for copy in fetches(c):
                 copy.wait()
+
+            @pl.when(c + 2 < chunks)
+            def _():
+                for copy in fetches(c + 2):
+                    copy.start()
 
         ls = lanes(0, g)
         mixed[...] = kb[:, ls].astype(F32) * vb[:, ls].astype(F32)
@@ -204,11 +213,11 @@
 def near_kernel(
     off_ref, after_ref, k_ref, v_ref, a_ref, th_ref, rr_ref, ri_ref, skip_ref, *refs
 ):
-    with_table = len(refs) > 8
-    if with_table:
-        l_hbm, y_hbm, table_hbm, plain, mixed, l_buf, y_buf, l_sem, y_sem, table_buf, table_sem = refs
+    if len(refs) > 8:
+        table_ref, *refs = refs
     else:
-        l_hbm, y_hbm, plain, mixed, l_buf, y_buf, l_sem, y_sem = refs
+        table_ref = None
+    l_hbm, y_hbm, plain, mixed, l_buf, y_buf, l_sem, y_sem = refs
     rows = k_ref.shape[0]
     modes = a_ref.shape[0]
     groups = y_hbm.shape[0]
@@ -224,8 +233,9 @@
         for m0 in range(0, modes, SUB):
             pr, pi, (tr, _) = pole_table(a_ref, th_ref, rr_ref, ri_ref, slice(m0, m0 + SUB), src)
             sums = tr if sums is None else [x + y for x, y in zip(sums, tr)]
-            if with_table:
-                fill_table(table_buf.at[g], pr, pi, m0, modes)
+            if table_ref is not None:
+                ms, there = slice(m0, m0 + SUB), lanes((1 - off_ref[0]) * half, g)
+                fill_table(table_ref.at[g], *pole_power(a_ref[ms, there], th_ref[ms, there], 1), m0, modes)
         taps = []
         for j in range(BLOCK):
             tap = jnp.sum(sums[j], axis=0, keepdims=True)
@@ -250,17 +260,17 @@
         end_states(plain, (a_ref, th_ref, rr_ref, ri_ref), (src, src), None, l_buf.at[i])
 
     finish_states = stream(tail, [(l_buf, l_hbm, l_sem)], states)
-    stores = [(y_buf, y_hbm, y_sem)] + ([(table_buf, table_hbm, table_sem)] if with_table else [])
-    finish = stream(groups, stores, group)
+    finish = stream(groups, [(y_buf, y_hbm, y_sem)], group)
     finish_states()
     finish()
 
 
-def far_kernel(with_table, off_ref, s_ref, l_ref, tail_ref, y_ref, q_ref, *refs):
-    if with_table:
-        table_ref, gated_ref, power_ref, state, conv = refs
+def far_kernel(off_ref, s_ref, l_ref, tail_ref, y_ref, q_ref, table_ref, *refs):
+    if len(refs) > 4:
+        a_ref, th_ref, gated_ref, power_ref, next_ref, state, conv = refs
     else:
-        a_ref, th_ref, gated_ref, power_ref, state, conv, own_table = refs
+        gated_ref, power_ref, state, conv = refs
+        next_ref = None
     rows = q_ref.shape[0]
     modes = s_ref.shape[0] // 2
     groups = y_ref.shape[0]
@@ -273,11 +283,12 @@
 
     def group(g, l_ref):
         src, dst = lanes(off_ref[0] * half, g), lanes(0, g)
-        table = table_ref.at[g] if with_table else own_table
+        table = table_ref.at[g]
         for m0 in range(0, modes, SUB):
             ms = slice(m0, m0 + SUB)
-            if not with_table:
-                fill_table(table, *pole_power(a_ref[ms, src], th_ref[ms, src], 1), m0, modes)
+            if next_ref is not None:
+                there = lanes((1 - off_ref[0]) * half, g)
+                fill_table(next_ref.at[g], *pole_power(a_ref[ms, there], th_ref[ms, there], 1), m0, modes)
             last = (BLOCK - 1) * 2 * modes + m0
             qr, qi = table[last : last + SUB, :], table[last + modes : last + modes + SUB, :]
             sr, si = s_ref[ms, dst], s_ref[modes + m0 : modes + m0 + SUB, dst]
@@ -385,21 +396,14 @@
 
     def near(offset, after, with_table):
         ins = [after, k, v, *poles, skip]
-        outs = [tail, near_shape]
         tail_sem = pltpu.SemaphoreType.DMA((TAIL,))
         scratch = [mixed, padded, pltpu.VMEM(tail, F32), pltpu.VMEM(near_shape, F32), tail_sem, group_sem]
-        if with_table:
-            outs.append(table)
-            scratch += [pltpu.VMEM(table, F32), group_sem]
-        return call(near_kernel, offset, ins, [], outs, scratch)
-
-    def far(offset, start, local, tail, y, *table):
-        ins = [start, local, tail, y, q, *(table or (decay, angle))]
+        return call(near_kernel, offset, ins, [table] * with_table, [tail, near_shape], scratch)
+
+    def far(offset, start, local, tail, y, *ins):
         scratch = [pltpu.VMEM((blocks * (states + 1), LANE), F32), padded]
-        if not table:
-            scratch.append(pltpu.VMEM((BLOCK * states, LANE), F32))
-        kernel = functools.partial(far_kernel, bool(table))
-        return call(kernel, offset, ins, [(rows, half), (rows, LANE)], [], scratch)
+        outs = [(rows, half), (rows, LANE)] + [table] * (len(ins) > 1)
+        return call(far_kernel, offset, [start, local, tail, y, q, *ins], outs, [], scratch)
 
     scratch = [
         pltpu.VMEM((rows, half), k.dtype),
@@ -426,7 +430,7 @@
     while distance < count:
         got = exchange(total, "seq", distance)
         if pending:
-            ready.append(near(pending.pop(0), total, False))
+            ready.append(near(pending.pop(0), total, bool(ready)))
             got, ready[-1] = lax.optimization_barrier((got, ready[-1]))
         above = (me & distance) != 0
         if before is None:
@@ -439,12 +443,13 @@
         jump = times(jump, jump)
         distance *= 2
     for offset in pending:
-        ready.append(near(offset, total, False))
+        ready.append(near(offset, total, bool(ready)))
     after_low = times(step_power, before) + low
     own_start = jnp.where(upper, after_low, before)
     other_start = exchange(jnp.where(upper, before, after_low), "seq", 1)
-    own_gated, own_power = far(own, own_start, own_local, *ready[0])
-    other_gated, other_power = far(other, other_start, sent_local, *ready[1])
+    own_table, *other_ready = ready[1]
+    own_gated, own_power, other_table = far(own, own_start, own_local, *ready[0], own_table, decay, angle)
+    other_gated, other_power = far(other, other_start, sent_local, *other_ready, other_table)
     power = jnp.sum(own_power + other_power, axis=1)
     distance = 1
     while distance < lax.axis_size("ch"):

time: 40.2 us -> 38.6 us (0.960)
  Pallas kernels: 22.6 us -> 21.1 us
  waiting for transfers between devices: 6.97 us -> 5.9 us
  starting transfers between devices: 9.7 us -> 10.7 us
    pallas_call x7, Pallas kernels: 22.6 us -> 21.1 us  [call(): pl.pallas_call(kernel, in_specs=[pl.BlockSpec(memory_space=pltpu.SMEM)] +...]
    ppermute x6, waiting for transfers between devices: 6.97 us -> 5.9 us  [exchange(): lax.ppermute(x, axis, [(i, i ^ distance) for i in range(lax.axis_size(axi...]
    ppermute x6, starting transfers between devices: 9.7 us -> 10.7 us  [exchange(): lax.ppermute(x, axis, [(i, i ^ distance) for i in range(lax.axis_size(axi...]
  transfers between devices with their start and end apart: 6 -> 6, of which waited for: 5 -> 6; matrix products, arithmetic and copies ran while one was open for 0% -> 0% of each run, Pallas kernels for 32% -> 32%
where the time goes in v3:
time: 38.6 us; the launch traced here: 38.5 us
  Pallas kernels  21.1 us (55%)
  starting transfers between devices  10.7 us (28%)
  waiting for transfers between devices  5.9 us (15%)
  other arithmetic  0.39 us (1%)
    pallas_call x7, Pallas kernels, call(): pl.pallas_call(kernel, in_specs=[pl.BlockSpec(memory_space=pltpu.SMEM)] +...  21.1 us
    ppermute x6, starting transfers between devices, exchange(): lax.ppermute(x, axis, [(i, i ^ distance) for i in range(lax.axis_size(axi...  10.7 us
    ppermute x6, waiting for transfers between devices, exchange(): lax.ppermute(x, axis, [(i, i ^ distance) for i in range(lax.axis_size(axi...  5.9 us
  transfers between devices with their start and end apart: 6, of which 6 were waited for; matrix products, arithmetic and copies ran while one was open for 0% of the time, Pallas kernels for 32%

profile of v3, /device:TPU:0, one launch (start us, length us, event | category | flops | bytes accessed | tf_op | source)
XLA Modules:
  0.0 38.5 jit_solution(5711701805175350478)
XLA Ops:
  0.0 0.0 copy-start
  0.0 4.7 %shard_map.92 = (f32[32,1024]{1,0:T(8,128)S(1)}, f32[6,512,128]{2,1,0:T(8,128)}) custom-call(s32[1]{0:T(128)S(6)} %sub.21.off_ref, bf16[256,2048]{1,0:T(8,128)(2,1)} %k_ref.5, bf16[256,2048]{1,0:T(8,128)(2,1)} %v_ref.5, f32[16,2048]{1,0:T(8,128)} %refs_0_.1, f32[16,2048]{1,0:T(8,128)} %refs_1_.1, f32[16,2048]{1,0:T(8,128)} %rr_ref.5, f32[16,2048]{1,0:T(8,128)} %ri_ref.5), custom_call_target="tpu_custom_call" | custom-call | tf_op jit(solution)/shard_map/pallas_call | solution.py:347
  4.7 0.0 copy-start.13
  4.7 3.0 %collective-permute-start = (f32[32,1024]{1,0:T(8,128)S(1)}, f32[32,1024]{1,0:T(8,128)S(1)}, u32[]{:S(2)}, u32[]{:S(2)}) collective-permute-start(f32[32,1024]{1,0:T(8,128)S(1)} %get-tuple-element.28), channel_id=1, source_target_pairs={{0,4},{4,0},{8,12},{12,8},{16,20},{20,16},{24,28},{28,24},{1,5},{5... | collective-permute-start | bytes 393224 | tf_op jit(solution)/shard_map/ppermute | solution.py:359
  7.8 0.0 copy-done.4
  7.8 0.0 copy-done.3
  7.8 0.0 copy-done.6
  7.8 0.0 copy-done.5
  7.8 0.0 copy-done.1
  7.8 3.3 %shard_map.91 = (f32[32,1024]{1,0:T(8,128)S(1)}, f32[32,1024]{1,0:T(8,128)S(1)}, f32[6,512,128]{2,1,0:T(8,128)}) custom-call(s32[1]{0:T(128)} %bitcast.off_ref, bf16[256,2048]{1,0:T(8,128)(2,1)S(1)} %copy-done, bf16[256,2048]{1,0:T(8,128)(2,1)S(1)} %copy-done.1, f32[16,2048]{1,0:T(8,128)S(1)} %copy-done.3, f32[16,2048]{1,0:T(8,128)S(1)} %copy-done.4, ...), custom_call_target="tpu_custom_call" | custom-call | tf_op jit(solution)/shard_map/pallas_call | solution.py:347
  11.1 0.2 collective-permute-done
  11.3 1.9 %collective-permute-start.1 = (f32[32,1024]{1,0:T(8,128)S(1)}, f32[32,1024]{1,0:T(8,128)S(1)}, u32[]{:S(2)}, u32[]{:S(2)}) collective-permute-start(f32[32,1024]{1,0:T(8,128)S(1)} %maximum_add_fusion.after_ref), channel_id=1, source_target_pairs={{0,8},{4,12},{8,0},{12,4},{16,24},{20,28},{24,16},{28,20},{1,9},{5... | collective-permute-start | bytes 393224 | tf_op jit(solution)/shard_map/ppermute | solution.py:359
  13.2 2.8 %shard_map.93 = (f32[2,512,128]{2,1,0:T(8,128)}, f32[8,256,128]{2,1,0:T(8,128)}) custom-call(s32[1]{0:T(128)} %bitcast.off_ref, f32[32,1024]{1,0:T(8,128)S(1)} %maximum_add_fusion.after_ref, bf16[256,2048]{1,0:T(8,128)(2,1)S(1)} %copy-done, bf16[256,2048]{1,0:T(8,128)(2,1)S(1)} %copy-done.1, f32[16,2048]{1,0:T(8,128)S(1)} %copy-done.3, ...), custom_call_target="tpu_custom_call" | custom-call | tf_op jit(solution)/shard_map/pallas_call | solution.py:347
  16.1 0.3 collective-permute-done.1
  16.4 2.9 %collective-permute-start.2 = (f32[32,1024]{1,0:T(8,128)S(1)}, f32[32,1024]{1,0:T(8,128)S(1)}, u32[]{:S(2)}, u32[]{:S(2)}) collective-permute-start(f32[32,1024]{1,0:T(8,128)S(1)} %fusion.after_ref), channel_id=1, source_target_pairs={{0,16},{4,20},{8,24},{12,28},{16,0},{20,4},{24,8},{28,12},{1,17},{... | collective-permute-start | bytes 393224 | tf_op jit(solution)/shard_map/ppermute | solution.py:359
  19.3 3.1 %shard_map.94 = (f32[8,512,128]{2,1,0:T(8,128)S(1)}, f32[2,512,128]{2,1,0:T(8,128)}, f32[8,256,128]{2,1,0:T(8,128)}) custom-call(s32[1]{0:T(128)S(6)} %sub.21.off_ref, f32[32,1024]{1,0:T(8,128)S(1)} %fusion.after_ref, bf16[256,2048]{1,0:T(8,128)(2,1)S(1)} %copy-done, bf16[256,2048]{1,0:T(8,128)(2,1)S(1)} %copy-done.1, f32[16,2048]{1,0:T(8,128)S(1)} %copy-done.3, ...), custom_call_target="tpu_custom_call" | custom-call | tf_op jit(solution)/shard_map/pallas_call | solution.py:347
  22.4 1.8 %collective-permute-done.2 = f32[32,1024]{1,0:T(8,128)S(1)} collective-permute-done((f32[32,1024]{1,0:T(8,128)S(1)}, f32[32,1024]{1,0:T(8,128)S(1)}, u32[]{:S(2)}, u32[]{:S(2)}) %collective-permute-start.2) | collective-permute-done | bytes 131104 | tf_op jit(solution)/shard_map/ppermute | solution.py:359
  24.4 1.3 %collective-permute-start.3 = (f32[32,1024]{1,0:T(8,128)S(1)}, f32[32,1024]{1,0:T(8,128)S(1)}, u32[]{:S(2)}, u32[]{:S(2)}) collective-permute-start(f32[32,1024]{1,0:T(8,128)S(1)} %get-tuple-element.52), channel_id=1, source_target_pairs={{0,4},{4,0},{8,12},{12,8},{16,20},{20,16},{24,28},{28,24},{1,5},{5... | collective-permute-start | bytes 393224 | tf_op jit(solution)/shard_map/ppermute | solution.py:359
  25.7 0.0 copy-done.8
  25.7 0.0 copy-done.12
  25.8 3.2 %shard_map.95 = (f32[256,1024]{1,0:T(8,128)S(1)}, f32[256,128]{1,0:T(8,128)S(1)}, f32[8,512,128]{2,1,0:T(8,128)S(1)}) custom-call(s32[1]{0:T(128)} %bitcast.off_ref, f32[32,1024]{1,0:T(8,128)S(1)} %get-tuple-element.53.s_ref, f32[6,512,128]{2,1,0:T(8,128)S(1)} %copy-done.8, f32[2,512,128]{2,1,0:T(8,128)S(1)} %copy-done.12, f32[8,256,128]{2,1,0:T(8,128)S(1)} %copy-done.10, ...), custom_call_target="tpu_custom_call" | custom-call | tf_op jit(solution)/shard_map/pallas_call | solution.py:347
  29.0 0.4 %collective-permute-done.3.s_ref = f32[32,1024]{1,0:T(8,128)S(1)} collective-permute-done((f32[32,1024]{1,0:T(8,128)S(1)}, f32[32,1024]{1,0:T(8,128)S(1)}, u32[]{:S(2)}, u32[]{:S(2)}) %collective-permute-start.3) | collective-permute-done | bytes 131104 | tf_op jit(solution)/shard_map/ppermute | solution.py:359
  29.4 0.0 copy-done.9
  29.4 0.0 copy-start.14
  29.4 2.9 %shard_map.96 = (f32[256,1024]{1,0:T(8,128)S(1)}, f32[256,128]{1,0:T(8,128)S(1)}) custom-call(s32[1]{0:T(128)S(6)} %sub.21.off_ref, f32[32,1024]{1,0:T(8,128)S(1)} %collective-permute-done.3.s_ref, f32[6,512,128]{2,1,0:T(8,128)S(1)} %copy-done.7, f32[2,512,128]{2,1,0:T(8,128)S(1)} %copy-done.11, f32[8,256,128]{2,1,0:T(8,128)S(1)} %copy-done.9, ...), custom_call_target="tpu_custom_call" | custom-call | tf_op jit(solution)/shard_map/pallas_call | solution.py:347
  32.4 0.1 add_reduce_fusion
  32.5 0.1 collective-permute-start.4
  32.6 1.1 %collective-permute-done.4 = f32[256]{0:T(256)S(1)} collective-permute-done((f32[256]{0:T(256)S(1)}, f32[256]{0:T(256)S(1)}, u32[]{:S(2)}, u32[]{:S(2)}) %collective-permute-start.4) | collective-permute-done | bytes 1056 | tf_op jit(solution)/shard_map/ppermute | solution.py:359
  33.7 1.5 %collective-permute-start.5 = (f32[256]{0:T(256)S(1)}, f32[256]{0:T(256)S(1)}, u32[]{:S(2)}, u32[]{:S(2)}) collective-permute-start(f32[256]{0:T(256)S(1)} %add.60), channel_id=1, source_target_pairs={{0,2},{1,3},{2,0},{3,1},{4,6},{5,7},{6,4},{7,5},{8,10},{9,11},{10,... | collective-permute-start | bytes 3080 | tf_op jit(solution)/shard_map/ppermute | solution.py:359
  35.2 2.1 %collective-permute-done.5 = f32[256]{0:T(256)S(1)} collective-permute-done((f32[256]{0:T(256)S(1)}, f32[256]{0:T(256)S(1)}, u32[]{:S(2)}, u32[]{:S(2)}) %collective-permute-start.5) | collective-permute-done | bytes 1056 | tf_op jit(solution)/shard_map/ppermute | solution.py:359
  37.3 0.1 broadcast_in_dim.20.scale_ref
  37.4 1.1 %shard_map.97 = bf16[256,2048]{1,0:T(8,128)(2,1)} custom-call(s32[1]{0:T(128)} %bitcast.off_ref, f32[256,1024]{1,0:T(8,128)S(1)} %get-tuple-element.41.own_ref, f32[256,1024]{1,0:T(8,128)S(1)} %get-tuple-element.46.other_ref, f32[256,128]{1,0:T(8,128)S(1)} %broadcast_in_dim.20.scale_ref, f32[1,2048]{1,0:T(1,128)S(1)} %bitcast.5), custom_call_target="tpu_custom_call" | custom-call | tf_op jit(solution)/shard_map/pallas_call | solution.py:347
  (31 shorter events, 0.3 us)
Async XLA Ops:
  0.0 7.8 %copy-start.4 = (f32[16,2048]{1,0:T(8,128)S(1)}, f32[16,2048]{1,0:T(8,128)}, u32[]{:S(2)}) copy-start(f32[16,2048]{1,0:T(8,128)} %refs_1_.1) | copy-start | bytes 393220
  0.0 7.8 %copy-start.3 = (f32[16,2048]{1,0:T(8,128)S(1)}, f32[16,2048]{1,0:T(8,128)}, u32[]{:S(2)}) copy-start(f32[16,2048]{1,0:T(8,128)} %refs_0_.1) | copy-start | bytes 393220
  0.0 7.8 %copy-start.6 = (f32[16,2048]{1,0:T(8,128)S(1)}, f32[16,2048]{1,0:T(8,128)}, u32[]{:S(2)}) copy-start(f32[16,2048]{1,0:T(8,128)} %ri_ref.5) | copy-start | bytes 393220
  0.0 7.8 %copy-start.5 = (f32[16,2048]{1,0:T(8,128)S(1)}, f32[16,2048]{1,0:T(8,128)}, u32[]{:S(2)}) copy-start(f32[16,2048]{1,0:T(8,128)} %rr_ref.5) | copy-start | bytes 393220
  0.0 7.8 %copy-start.1 = (bf16[256,2048]{1,0:T(8,128)(2,1)S(1)}, bf16[256,2048]{1,0:T(8,128)(2,1)}, u32[]{:S(2)}) copy-start(bf16[256,2048]{1,0:T(8,128)(2,1)} %v_ref.5) | copy-start | bytes 3145732
  0.0 7.8 %copy-start = (bf16[256,2048]{1,0:T(8,128)(2,1)S(1)}, bf16[256,2048]{1,0:T(8,128)(2,1)}, u32[]{:S(2)}) copy-start(bf16[256,2048]{1,0:T(8,128)(2,1)} %k_ref.5) | copy-start | bytes 3145732
  4.7 8.5 %copy-start.13 = (f32[2048]{0:T(1024)S(1)}, f32[2048]{0:T(1024)}, u32[]{:S(2)}) copy-start(f32[2048]{0:T(1024)} %param.16) | copy-start | bytes 24580
  4.7 6.5 %collective-permute-start = (f32[32,1024]{1,0:T(8,128)S(1)}, f32[32,1024]{1,0:T(8,128)S(1)}, u32[]{:S(2)}, u32[]{:S(2)}) collective-permute-start(f32[32,1024]{1,0:T(8,128)S(1)} %get-tuple-element.28), channel_id=1, source_target_pairs={{0,4},{4,0},{8,12},{12,8},{16,20},{20,16},{24,28},{28,24},{1,5},{5... | collective-permute-start | bytes 393224 | tf_op jit(solution)/shard_map/ppermute | solution.py:359
  11.3 5.0 %collective-permute-start.1 = (f32[32,1024]{1,0:T(8,128)S(1)}, f32[32,1024]{1,0:T(8,128)S(1)}, u32[]{:S(2)}, u32[]{:S(2)}) collective-permute-start(f32[32,1024]{1,0:T(8,128)S(1)} %maximum_add_fusion.after_ref), channel_id=1, source_target_pairs={{0,8},{4,12},{8,0},{12,4},{16,24},{20,28},{24,16},{28,20},{1,9},{5... | collective-permute-start | bytes 393224 | tf_op jit(solution)/shard_map/ppermute | solution.py:359
  16.4 7.8 %collective-permute-start.2 = (f32[32,1024]{1,0:T(8,128)S(1)}, f32[32,1024]{1,0:T(8,128)S(1)}, u32[]{:S(2)}, u32[]{:S(2)}) collective-permute-start(f32[32,1024]{1,0:T(8,128)S(1)} %fusion.after_ref), channel_id=1, source_target_pairs={{0,16},{4,20},{8,24},{12,28},{16,0},{20,4},{24,8},{28,12},{1,17},{... | collective-permute-start | bytes 393224 | tf_op jit(solution)/shard_map/ppermute | solution.py:359
  19.3 6.4 %copy-start.2 = (bf16[256,2048]{1,0:T(8,128)(2,1)S(1)}, bf16[256,2048]{1,0:T(8,128)(2,1)}, u32[]{:S(2)}) copy-start(bf16[256,2048]{1,0:T(8,128)(2,1)} %q_ref.3) | copy-start | bytes 3145732
  19.3 6.4 %copy-start.8 = (f32[6,512,128]{2,1,0:T(8,128)S(1)}, f32[6,512,128]{2,1,0:T(8,128)}, u32[]{:S(2)}) copy-start(f32[6,512,128]{2,1,0:T(8,128)} %get-tuple-element.37.l_ref) | copy-start | bytes 4718596
  19.3 6.4 %copy-start.10 = (f32[8,256,128]{2,1,0:T(8,128)S(1)}, f32[8,256,128]{2,1,0:T(8,128)}, u32[]{:S(2)}) copy-start(f32[8,256,128]{2,1,0:T(8,128)} %get-tuple-element.39.y_ref) | copy-start | bytes 3145732
  19.3 6.4 %copy-start.12 = (f32[2,512,128]{2,1,0:T(8,128)S(1)}, f32[2,512,128]{2,1,0:T(8,128)}, u32[]{:S(2)}) copy-start(f32[2,512,128]{2,1,0:T(8,128)} %get-tuple-element.38.tail_ref) | copy-start | bytes 1572868
  24.4 5.0 %collective-permute-start.3 = (f32[32,1024]{1,0:T(8,128)S(1)}, f32[32,1024]{1,0:T(8,128)S(1)}, u32[]{:S(2)}, u32[]{:S(2)}) collective-permute-start(f32[32,1024]{1,0:T(8,128)S(1)} %get-tuple-element.52), channel_id=1, source_target_pairs={{0,4},{4,0},{8,12},{12,8},{16,20},{20,16},{24,28},{28,24},{1,5},{5... | collective-permute-start | bytes 393224 | tf_op jit(solution)/shard_map/ppermute | solution.py:359
  25.7 3.7 %copy-start.7 = (f32[6,512,128]{2,1,0:T(8,128)S(1)}, f32[6,512,128]{2,1,0:T(8,128)}, u32[]{:S(2)}) copy-start(f32[6,512,128]{2,1,0:T(8,128)} %get-tuple-element.42.l_ref) | copy-start | bytes 4718596
  25.7 3.7 %copy-start.9 = (f32[8,256,128]{2,1,0:T(8,128)S(1)}, f32[8,256,128]{2,1,0:T(8,128)}, u32[]{:S(2)}) copy-start(f32[8,256,128]{2,1,0:T(8,128)} %get-tuple-element.44.y_ref) | copy-start | bytes 3145732
  25.8 3.7 %copy-start.11 = (f32[2,512,128]{2,1,0:T(8,128)S(1)}, f32[2,512,128]{2,1,0:T(8,128)}, u32[]{:S(2)}) copy-start(f32[2,512,128]{2,1,0:T(8,128)} %get-tuple-element.43.tail_ref) | copy-start | bytes 1572868
  29.4 8.0 %copy-start.14 = (f32[2048]{0:T(1024)S(1)}, f32[2048]{0:T(1024)}, u32[]{:S(2)}) copy-start(f32[2048]{0:T(1024)} %param.17) | copy-start | bytes 24580
  32.5 1.2 %collective-permute-start.4 = (f32[256]{0:T(256)S(1)}, f32[256]{0:T(256)S(1)}, u32[]{:S(2)}, u32[]{:S(2)}) collective-permute-start(f32[256]{0:T(256)S(1)} %add_reduce_fusion), channel_id=1, source_target_pairs={{0,1},{1,0},{2,3},{3,2},{4,5},{5,4},{6,7},{7,6},{8,9},{9,8},{10,11... | collective-permute-start | bytes 3080 | tf_op jit(solution)/shard_map/ppermute | solution.py:359
  33.7 3.6 %collective-permute-start.5 = (f32[256]{0:T(256)S(1)}, f32[256]{0:T(256)S(1)}, u32[]{:S(2)}, u32[]{:S(2)}) collective-permute-start(f32[256]{0:T(256)S(1)} %add.60), channel_id=1, source_target_pairs={{0,2},{1,3},{2,0},{3,1},{4,6},{5,7},{6,4},{7,5},{8,10},{9,11},{10,... | collective-permute-start | bytes 3080 | tf_op jit(solution)/shard_map/ppermute | solution.py:359

commit v4 on v3

--- a/solution.py
+++ b/solution.py
@@ -12,7 +12,7 @@
 LANE = 128
 BLOCK = 16
 APART = BLOCK + 1
-FETCH = 256
+FETCH = 128
 STORE = 512
 TAIL = 2
 TOKENS = 8
@@ -114,7 +114,6 @@
         ms = slice(m0, m0 + SUB)
         pr, pi, tables[m0] = pole_table(*poles, ms, src)
         jump[m0] = squared(pr, pi, BLOCK.bit_length() - 1)
-        state[m0] = jnp.zeros((SUB, LANE), F32), jnp.zeros((SUB, LANE), F32)
         if pw_ref is not None:
             wr, wi = pole_power(a_ref[ms, src], th_ref[ms, src], rows)
             pw_ref[ms, dst] = wr
@@ -128,6 +127,9 @@
                 enter[m0] = (r, i) if s == 0 else (enter[m0][0] + r, enter[m0][1] + i)
         for m0 in starts:
             base = b * 2 * modes + m0
+            if b == 0:
+                state[m0] = enter[m0]
+                continue
             sr, si = state[m0]
             if l_buf is not None:
                 l_buf[base : base + SUB, :] = sr
@@ -141,18 +143,13 @@
 
 def sent_kernel(off_ref, k_hbm, v_hbm, a_hbm, th_hbm, rr_hbm, ri_hbm, e_ref, l_hbm, kb, vb, pb, mixed, l_buf, kv_sem, p_sem, l_sem):
     half = e_ref.shape[1]
-    chunks = half // FETCH
     base = off_ref[0] * half
 
-    def there(c):
-        return pl.ds(pl.multiple_of(base + c * FETCH, LANE), FETCH)
-
-    def here(c):
-        return pl.ds(pl.multiple_of(c * FETCH, LANE), FETCH)
-
     def fetches(c):
+        first, size = ((0, FETCH), (FETCH, half - FETCH))[c]
+        there = pl.ds(pl.multiple_of(base + first, LANE), size)
         return [
-            pltpu.make_async_copy(src.at[:, there(c)], dst.at[:, here(c)], kv_sem.at[i, c])
+            pltpu.make_async_copy(src.at[:, there], dst.at[:, first : first + size], kv_sem.at[i, c])
             for i, (src, dst) in enumerate(((k_hbm, kb), (v_hbm, vb)))
         ]
 
@@ -167,16 +164,12 @@
         copy.wait()
 
     def group(g, l_buf):
-        @pl.when(lax.rem(g, FETCH // LANE) == 0)
-        def _():
-            c = g // (FETCH // LANE)
-            for copy in fetches(c):
-                copy.wait()
-
-            @pl.when(c + 2 < chunks)
+        for c in range(2):
+
+            @pl.when(g == c * FETCH // LANE)
             def _():
-                for copy in fetches(c + 2):
-                    copy.start()
+                for copy in fetches(c):
+                    copy.wait()
 
         ls = lanes(0, g)
         mixed[...] = kb[:, ls].astype(F32) * vb[:, ls].astype(F32)
@@ -295,8 +288,9 @@
             for b in range(blocks):
                 at = b * 2 * modes + m0
                 to = b * apart + m0
-                state[to : to + SUB, :] = l_ref[at : at + SUB, :] + sr
-                state[to + modes : to + modes + SUB, :] = l_ref[at + modes : at + modes + SUB, :] + si
+                lr, li = (l_ref[at : at + SUB, :], l_ref[at + modes : at + modes + SUB, :]) if b else (0.0, 0.0)
+                state[to : to + SUB, :] = lr + sr
+                state[to + modes : to + modes + SUB, :] = li + si
                 if b < blocks - 1:
                     sr, si = cmul(qr, qi, sr, si)
         for t0 in range(0, BLOCK, TOKENS):
@@ -383,7 +377,7 @@
     states = 2 * modes
     poles = (decay, angle, res_r, res_i)
     mixed = pltpu.VMEM((rows, LANE), F32)
-    padded = pltpu.VMEM((blocks * APART, LANE), F32)
+    padded = pltpu.VMEM(((blocks + 1) * APART + SUB, LANE), F32)
     state = (states, half)
     groups = half // LANE
     local = (groups - TAIL, blocks * states, LANE)
@@ -401,7 +395,7 @@
         return call(near_kernel, offset, ins, [table] * with_table, [tail, near_shape], scratch)
 
     def far(offset, start, local, tail, y, *ins):
-        scratch = [pltpu.VMEM((blocks * (states + 1), LANE), F32), padded]
+        scratch = [pltpu.VMEM(((blocks + 1) * (states + 1) + SUB, LANE), F32), padded]
         outs = [(rows, half), (rows, LANE)] + [table] * (len(ins) > 1)
         return call(far_kernel, offset, [start, local, tail, y, q, *ins], outs, [], scratch)
 
@@ -411,7 +405,7 @@
         pltpu.VMEM((4, modes, half), F32),
         mixed,
         pltpu.VMEM(local, F32),
-        pltpu.SemaphoreType.DMA((2, half // FETCH)),
+        pltpu.SemaphoreType.DMA((2, 2)),
         pltpu.SemaphoreType.DMA((4,)),
         stored_sem,
     ]

time: 38.6 us -> 38.5 us (level)
  no operation moved by 1% of the time
where the time goes in v4:
time: 38.5 us; the launch traced here: 38.3 us
  Pallas kernels  21 us (55%)
  starting transfers between devices  10.7 us (28%)
  waiting for transfers between devices  5.88 us (15%)
  other arithmetic  0.39 us (1%)
    pallas_call x7, Pallas kernels, call(): pl.pallas_call(kernel, in_specs=[pl.BlockSpec(memory_space=pltpu.SMEM)] +...  21 us
    ppermute x6, starting transfers between devices, exchange(): lax.ppermute(x, axis, [(i, i ^ distance) for i in range(lax.axis_size(axi...  10.7 us
    ppermute x6, waiting for transfers between devices, exchange(): lax.ppermute(x, axis, [(i, i ^ distance) for i in range(lax.axis_size(axi...  5.88 us
  transfers between devices with their start and end apart: 6, of which 6 were waited for; matrix products, arithmetic and copies ran while one was open for 0% of the time, Pallas kernels for 32%

profile of v4, /device:TPU:0, one launch (start us, length us, event | category | flops | bytes accessed | tf_op | source)
XLA Modules:
  0.0 38.3 jit_solution(18377997209532452539)
XLA Ops:
  0.0 0.0 copy-start
  0.0 4.6 %shard_map.92 = (f32[32,1024]{1,0:T(8,128)S(1)}, f32[6,512,128]{2,1,0:T(8,128)}) custom-call(s32[1]{0:T(128)S(6)} %sub.21.off_ref, bf16[256,2048]{1,0:T(8,128)(2,1)} %k_ref.5, bf16[256,2048]{1,0:T(8,128)(2,1)} %v_ref.5, f32[16,2048]{1,0:T(8,128)} %refs_0_.1, f32[16,2048]{1,0:T(8,128)} %refs_1_.1, f32[16,2048]{1,0:T(8,128)} %rr_ref.5, f32[16,2048]{1,0:T(8,128)} %ri_ref.5), custom_call_target="tpu_custom_call" | custom-call | tf_op jit(solution)/shard_map/pallas_call | solution.py:341
  4.6 0.0 copy-start.13
  4.6 3.0 %collective-permute-start = (f32[32,1024]{1,0:T(8,128)S(1)}, f32[32,1024]{1,0:T(8,128)S(1)}, u32[]{:S(2)}, u32[]{:S(2)}) collective-permute-start(f32[32,1024]{1,0:T(8,128)S(1)} %get-tuple-element.28), channel_id=1, source_target_pairs={{0,4},{4,0},{8,12},{12,8},{16,20},{20,16},{24,28},{28,24},{1,5},{5... | collective-permute-start | bytes 393224 | tf_op jit(solution)/shard_map/ppermute | solution.py:353
  7.7 0.0 copy-done.4
  7.7 0.0 copy-done.3
  7.7 0.0 copy-done.6
  7.7 0.0 copy-done.5
  7.7 0.0 copy-done.1
  7.7 0.0 copy-done
  7.7 3.3 %shard_map.91 = (f32[32,1024]{1,0:T(8,128)S(1)}, f32[32,1024]{1,0:T(8,128)S(1)}, f32[6,512,128]{2,1,0:T(8,128)}) custom-call(s32[1]{0:T(128)} %bitcast.off_ref, bf16[256,2048]{1,0:T(8,128)(2,1)S(1)} %copy-done, bf16[256,2048]{1,0:T(8,128)(2,1)S(1)} %copy-done.1, f32[16,2048]{1,0:T(8,128)S(1)} %copy-done.3, f32[16,2048]{1,0:T(8,128)S(1)} %copy-done.4, ...), custom_call_target="tpu_custom_call" | custom-call | tf_op jit(solution)/shard_map/pallas_call | solution.py:341
  11.0 0.2 collective-permute-done
  11.2 1.9 %collective-permute-start.1 = (f32[32,1024]{1,0:T(8,128)S(1)}, f32[32,1024]{1,0:T(8,128)S(1)}, u32[]{:S(2)}, u32[]{:S(2)}) collective-permute-start(f32[32,1024]{1,0:T(8,128)S(1)} %maximum_add_fusion.after_ref), channel_id=1, source_target_pairs={{0,8},{4,12},{8,0},{12,4},{16,24},{20,28},{24,16},{28,20},{1,9},{5... | collective-permute-start | bytes 393224 | tf_op jit(solution)/shard_map/ppermute | solution.py:353
  13.1 2.8 %shard_map.93 = (f32[2,512,128]{2,1,0:T(8,128)}, f32[8,256,128]{2,1,0:T(8,128)}) custom-call(s32[1]{0:T(128)} %bitcast.off_ref, f32[32,1024]{1,0:T(8,128)S(1)} %maximum_add_fusion.after_ref, bf16[256,2048]{1,0:T(8,128)(2,1)S(1)} %copy-done, bf16[256,2048]{1,0:T(8,128)(2,1)S(1)} %copy-done.1, f32[16,2048]{1,0:T(8,128)S(1)} %copy-done.3, ...), custom_call_target="tpu_custom_call" | custom-call | tf_op jit(solution)/shard_map/pallas_call | solution.py:341
  16.0 0.3 collective-permute-done.1
  16.3 2.9 %collective-permute-start.2 = (f32[32,1024]{1,0:T(8,128)S(1)}, f32[32,1024]{1,0:T(8,128)S(1)}, u32[]{:S(2)}, u32[]{:S(2)}) collective-permute-start(f32[32,1024]{1,0:T(8,128)S(1)} %fusion.after_ref), channel_id=1, source_target_pairs={{0,16},{4,20},{8,24},{12,28},{16,0},{20,4},{24,8},{28,12},{1,17},{... | collective-permute-start | bytes 393224 | tf_op jit(solution)/shard_map/ppermute | solution.py:353
  19.2 3.1 %shard_map.94 = (f32[8,512,128]{2,1,0:T(8,128)S(1)}, f32[2,512,128]{2,1,0:T(8,128)}, f32[8,256,128]{2,1,0:T(8,128)}) custom-call(s32[1]{0:T(128)S(6)} %sub.21.off_ref, f32[32,1024]{1,0:T(8,128)S(1)} %fusion.after_ref, bf16[256,2048]{1,0:T(8,128)(2,1)S(1)} %copy-done, bf16[256,2048]{1,0:T(8,128)(2,1)S(1)} %copy-done.1, f32[16,2048]{1,0:T(8,128)S(1)} %copy-done.3, ...), custom_call_target="tpu_custom_call" | custom-call | tf_op jit(solution)/shard_map/pallas_call | solution.py:341
  22.3 1.8 %collective-permute-done.2 = f32[32,1024]{1,0:T(8,128)S(1)} collective-permute-done((f32[32,1024]{1,0:T(8,128)S(1)}, f32[32,1024]{1,0:T(8,128)S(1)}, u32[]{:S(2)}, u32[]{:S(2)}) %collective-permute-start.2) | collective-permute-done | bytes 131104 | tf_op jit(solution)/shard_map/ppermute | solution.py:353
  24.2 1.4 %collective-permute-start.3 = (f32[32,1024]{1,0:T(8,128)S(1)}, f32[32,1024]{1,0:T(8,128)S(1)}, u32[]{:S(2)}, u32[]{:S(2)}) collective-permute-start(f32[32,1024]{1,0:T(8,128)S(1)} %get-tuple-element.52), channel_id=1, source_target_pairs={{0,4},{4,0},{8,12},{12,8},{16,20},{20,16},{24,28},{28,24},{1,5},{5... | collective-permute-start | bytes 393224 | tf_op jit(solution)/shard_map/ppermute | solution.py:353
  25.6 0.0 copy-done.10
  25.7 3.2 %shard_map.95 = (f32[256,1024]{1,0:T(8,128)S(1)}, f32[256,128]{1,0:T(8,128)S(1)}, f32[8,512,128]{2,1,0:T(8,128)S(1)}) custom-call(s32[1]{0:T(128)} %bitcast.off_ref, f32[32,1024]{1,0:T(8,128)S(1)} %get-tuple-element.53.s_ref, f32[6,512,128]{2,1,0:T(8,128)S(1)} %copy-done.8, f32[2,512,128]{2,1,0:T(8,128)S(1)} %copy-done.12, f32[8,256,128]{2,1,0:T(8,128)S(1)} %copy-done.10, ...), custom_call_target="tpu_custom_call" | custom-call | tf_op jit(solution)/shard_map/pallas_call | solution.py:341
  28.9 0.4 %collective-permute-done.3.s_ref = f32[32,1024]{1,0:T(8,128)S(1)} collective-permute-done((f32[32,1024]{1,0:T(8,128)S(1)}, f32[32,1024]{1,0:T(8,128)S(1)}, u32[]{:S(2)}, u32[]{:S(2)}) %collective-permute-start.3) | collective-permute-done | bytes 131104 | tf_op jit(solution)/shard_map/ppermute | solution.py:353
  29.3 0.0 copy-done.9
  29.3 0.0 copy-start.14
  29.3 2.9 %shard_map.96 = (f32[256,1024]{1,0:T(8,128)S(1)}, f32[256,128]{1,0:T(8,128)S(1)}) custom-call(s32[1]{0:T(128)S(6)} %sub.21.off_ref, f32[32,1024]{1,0:T(8,128)S(1)} %collective-permute-done.3.s_ref, f32[6,512,128]{2,1,0:T(8,128)S(1)} %copy-done.7, f32[2,512,128]{2,1,0:T(8,128)S(1)} %copy-done.11, f32[8,256,128]{2,1,0:T(8,128)S(1)} %copy-done.9, ...), custom_call_target="tpu_custom_call" | custom-call | tf_op jit(solution)/shard_map/pallas_call | solution.py:341
  32.2 0.1 add_reduce_fusion
  32.3 0.1 collective-permute-start.4
  32.4 1.1 %collective-permute-done.4 = f32[256]{0:T(256)S(1)} collective-permute-done((f32[256]{0:T(256)S(1)}, f32[256]{0:T(256)S(1)}, u32[]{:S(2)}, u32[]{:S(2)}) %collective-permute-start.4) | collective-permute-done | bytes 1056 | tf_op jit(solution)/shard_map/ppermute | solution.py:353
  33.5 1.5 %collective-permute-start.5 = (f32[256]{0:T(256)S(1)}, f32[256]{0:T(256)S(1)}, u32[]{:S(2)}, u32[]{:S(2)}) collective-permute-start(f32[256]{0:T(256)S(1)} %add.60), channel_id=1, source_target_pairs={{0,2},{1,3},{2,0},{3,1},{4,6},{5,7},{6,4},{7,5},{8,10},{9,11},{10,... | collective-permute-start | bytes 3080 | tf_op jit(solution)/shard_map/ppermute | solution.py:353
  35.0 2.1 %collective-permute-done.5 = f32[256]{0:T(256)S(1)} collective-permute-done((f32[256]{0:T(256)S(1)}, f32[256]{0:T(256)S(1)}, u32[]{:S(2)}, u32[]{:S(2)}) %collective-permute-start.5) | collective-permute-done | bytes 1056 | tf_op jit(solution)/shard_map/ppermute | solution.py:353
  37.1 0.1 broadcast_in_dim.20.scale_ref
  37.2 1.1 %shard_map.97 = bf16[256,2048]{1,0:T(8,128)(2,1)} custom-call(s32[1]{0:T(128)} %bitcast.off_ref, f32[256,1024]{1,0:T(8,128)S(1)} %get-tuple-element.41.own_ref, f32[256,1024]{1,0:T(8,128)S(1)} %get-tuple-element.46.other_ref, f32[256,128]{1,0:T(8,128)S(1)} %broadcast_in_dim.20.scale_ref, f32[1,2048]{1,0:T(1,128)S(1)} %bitcast.5), custom_call_target="tpu_custom_call" | custom-call | tf_op jit(solution)/shard_map/pallas_call | solution.py:341
  (31 shorter events, 0.3 us)
Async XLA Ops:
  0.0 7.7 %copy-start.4 = (f32[16,2048]{1,0:T(8,128)S(1)}, f32[16,2048]{1,0:T(8,128)}, u32[]{:S(2)}) copy-start(f32[16,2048]{1,0:T(8,128)} %refs_1_.1) | copy-start | bytes 393220
  0.0 7.7 %copy-start.3 = (f32[16,2048]{1,0:T(8,128)S(1)}, f32[16,2048]{1,0:T(8,128)}, u32[]{:S(2)}) copy-start(f32[16,2048]{1,0:T(8,128)} %refs_0_.1) | copy-start | bytes 393220
  0.0 7.7 %copy-start.6 = (f32[16,2048]{1,0:T(8,128)S(1)}, f32[16,2048]{1,0:T(8,128)}, u32[]{:S(2)}) copy-start(f32[16,2048]{1,0:T(8,128)} %ri_ref.5) | copy-start | bytes 393220
  0.0 7.7 %copy-start.5 = (f32[16,2048]{1,0:T(8,128)S(1)}, f32[16,2048]{1,0:T(8,128)}, u32[]{:S(2)}) copy-start(f32[16,2048]{1,0:T(8,128)} %rr_ref.5) | copy-start | bytes 393220
  0.0 7.7 %copy-start.1 = (bf16[256,2048]{1,0:T(8,128)(2,1)S(1)}, bf16[256,2048]{1,0:T(8,128)(2,1)}, u32[]{:S(2)}) copy-start(bf16[256,2048]{1,0:T(8,128)(2,1)} %v_ref.5) | copy-start | bytes 3145732
  0.0 7.7 %copy-start = (bf16[256,2048]{1,0:T(8,128)(2,1)S(1)}, bf16[256,2048]{1,0:T(8,128)(2,1)}, u32[]{:S(2)}) copy-start(bf16[256,2048]{1,0:T(8,128)(2,1)} %k_ref.5) | copy-start | bytes 3145732
  4.6 8.5 %copy-start.13 = (f32[2048]{0:T(1024)S(1)}, f32[2048]{0:T(1024)}, u32[]{:S(2)}) copy-start(f32[2048]{0:T(1024)} %param.16) | copy-start | bytes 24580
  4.6 6.5 %collective-permute-start = (f32[32,1024]{1,0:T(8,128)S(1)}, f32[32,1024]{1,0:T(8,128)S(1)}, u32[]{:S(2)}, u32[]{:S(2)}) collective-permute-start(f32[32,1024]{1,0:T(8,128)S(1)} %get-tuple-element.28), channel_id=1, source_target_pairs={{0,4},{4,0},{8,12},{12,8},{16,20},{20,16},{24,28},{28,24},{1,5},{5... | collective-permute-start | bytes 393224 | tf_op jit(solution)/shard_map/ppermute | solution.py:353
  11.2 5.0 %collective-permute-start.1 = (f32[32,1024]{1,0:T(8,128)S(1)}, f32[32,1024]{1,0:T(8,128)S(1)}, u32[]{:S(2)}, u32[]{:S(2)}) collective-permute-start(f32[32,1024]{1,0:T(8,128)S(1)} %maximum_add_fusion.after_ref), channel_id=1, source_target_pairs={{0,8},{4,12},{8,0},{12,4},{16,24},{20,28},{24,16},{28,20},{1,9},{5... | collective-permute-start | bytes 393224 | tf_op jit(solution)/shard_map/ppermute | solution.py:353
  16.3 7.8 %collective-permute-start.2 = (f32[32,1024]{1,0:T(8,128)S(1)}, f32[32,1024]{1,0:T(8,128)S(1)}, u32[]{:S(2)}, u32[]{:S(2)}) collective-permute-start(f32[32,1024]{1,0:T(8,128)S(1)} %fusion.after_ref), channel_id=1, source_target_pairs={{0,16},{4,20},{8,24},{12,28},{16,0},{20,4},{24,8},{28,12},{1,17},{... | collective-permute-start | bytes 393224 | tf_op jit(solution)/shard_map/ppermute | solution.py:353
  19.2 6.4 %copy-start.2 = (bf16[256,2048]{1,0:T(8,128)(2,1)S(1)}, bf16[256,2048]{1,0:T(8,128)(2,1)}, u32[]{:S(2)}) copy-start(bf16[256,2048]{1,0:T(8,128)(2,1)} %q_ref.3) | copy-start | bytes 3145732
  19.2 6.4 %copy-start.8 = (f32[6,512,128]{2,1,0:T(8,128)S(1)}, f32[6,512,128]{2,1,0:T(8,128)}, u32[]{:S(2)}) copy-start(f32[6,512,128]{2,1,0:T(8,128)} %get-tuple-element.37.l_ref) | copy-start | bytes 4718596
  19.2 6.4 %copy-start.10 = (f32[8,256,128]{2,1,0:T(8,128)S(1)}, f32[8,256,128]{2,1,0:T(8,128)}, u32[]{:S(2)}) copy-start(f32[8,256,128]{2,1,0:T(8,128)} %get-tuple-element.39.y_ref) | copy-start | bytes 3145732
  19.2 6.4 %copy-start.12 = (f32[2,512,128]{2,1,0:T(8,128)S(1)}, f32[2,512,128]{2,1,0:T(8,128)}, u32[]{:S(2)}) copy-start(f32[2,512,128]{2,1,0:T(8,128)} %get-tuple-element.38.tail_ref) | copy-start | bytes 1572868
  24.2 5.0 %collective-permute-start.3 = (f32[32,1024]{1,0:T(8,128)S(1)}, f32[32,1024]{1,0:T(8,128)S(1)}, u32[]{:S(2)}, u32[]{:S(2)}) collective-permute-start(f32[32,1024]{1,0:T(8,128)S(1)} %get-tuple-element.52), channel_id=1, source_target_pairs={{0,4},{4,0},{8,12},{12,8},{16,20},{20,16},{24,28},{28,24},{1,5},{5... | collective-permute-start | bytes 393224 | tf_op jit(solution)/shard_map/ppermute | solution.py:353
  25.6 3.7 %copy-start.7 = (f32[6,512,128]{2,1,0:T(8,128)S(1)}, f32[6,512,128]{2,1,0:T(8,128)}, u32[]{:S(2)}) copy-start(f32[6,512,128]{2,1,0:T(8,128)} %get-tuple-element.42.l_ref) | copy-start | bytes 4718596
  25.6 3.6 %copy-start.9 = (f32[8,256,128]{2,1,0:T(8,128)S(1)}, f32[8,256,128]{2,1,0:T(8,128)}, u32[]{:S(2)}) copy-start(f32[8,256,128]{2,1,0:T(8,128)} %get-tuple-element.44.y_ref) | copy-start | bytes 3145732
  25.6 3.6 %copy-start.11 = (f32[2,512,128]{2,1,0:T(8,128)S(1)}, f32[2,512,128]{2,1,0:T(8,128)}, u32[]{:S(2)}) copy-start(f32[2,512,128]{2,1,0:T(8,128)} %get-tuple-element.43.tail_ref) | copy-start | bytes 1572868
  29.3 7.9 %copy-start.14 = (f32[2048]{0:T(1024)S(1)}, f32[2048]{0:T(1024)}, u32[]{:S(2)}) copy-start(f32[2048]{0:T(1024)} %param.17) | copy-start | bytes 24580
  32.3 1.2 %collective-permute-start.4 = (f32[256]{0:T(256)S(1)}, f32[256]{0:T(256)S(1)}, u32[]{:S(2)}, u32[]{:S(2)}) collective-permute-start(f32[256]{0:T(256)S(1)} %add_reduce_fusion), channel_id=1, source_target_pairs={{0,1},{1,0},{2,3},{3,2},{4,5},{5,4},{6,7},{7,6},{8,9},{9,8},{10,11... | collective-permute-start | bytes 3080 | tf_op jit(solution)/shard_map/ppermute | solution.py:353
  33.5 3.6 %collective-permute-start.5 = (f32[256]{0:T(256)S(1)}, f32[256]{0:T(256)S(1)}, u32[]{:S(2)}, u32[]{:S(2)}) collective-permute-start(f32[256]{0:T(256)S(1)} %add.60), channel_id=1, source_target_pairs={{0,2},{1,3},{2,0},{3,1},{4,6},{5,7},{6,4},{7,5},{8,10},{9,11},{10,... | collective-permute-start | bytes 3080 | tf_op jit(solution)/shard_map/ppermute | solution.py:353

commit v5 on v4

--- a/solution.py
+++ b/solution.py
@@ -103,7 +103,7 @@
 
 
 def end_states(mixed, poles, at, e_ref, l_buf, pw_ref=None):
-    a_ref, th_ref = poles[:2]
+    a_ref, th_ref = poles
     rows = mixed.shape[0]
     modes = a_ref.shape[0]
     src, dst = at
@@ -112,8 +112,9 @@
     tables, jump, state = {}, {}, {}
     for m0 in starts:
         ms = slice(m0, m0 + SUB)
-        pr, pi, tables[m0] = pole_table(*poles, ms, src)
-        jump[m0] = squared(pr, pi, BLOCK.bit_length() - 1)
+        pr, pi = pole_power(a_ref[ms, src], th_ref[ms, src], 1)
+        tr, ti = tables[m0] = power_table(pr, pi, pr, pi, BLOCK)
+        jump[m0] = tr[-1], ti[-1]
         if pw_ref is not None:
             wr, wi = pole_power(a_ref[ms, src], th_ref[ms, src], rows)
             pw_ref[ms, dst] = wr
@@ -123,7 +124,10 @@
         for s in range(BLOCK):
             x = row(mixed, b * BLOCK + s, every)
             for m0 in starts:
-                r, i = tables[m0][0][BLOCK - 1 - s] * x, tables[m0][1][BLOCK - 1 - s] * x
+                if s == BLOCK - 1:
+                    enter[m0] = enter[m0][0] + x, enter[m0][1]
+                    continue
+                r, i = tables[m0][0][BLOCK - 2 - s] * x, tables[m0][1][BLOCK - 2 - s] * x
                 enter[m0] = (r, i) if s == 0 else (enter[m0][0] + r, enter[m0][1] + i)
         for m0 in starts:
             base = b * 2 * modes + m0
@@ -141,7 +145,7 @@
             e_ref[m0 : m0 + SUB, dst], e_ref[modes + m0 : modes + m0 + SUB, dst] = state[m0]
 
 
-def sent_kernel(off_ref, k_hbm, v_hbm, a_hbm, th_hbm, rr_hbm, ri_hbm, e_ref, l_hbm, kb, vb, pb, mixed, l_buf, kv_sem, p_sem, l_sem):
+def sent_kernel(off_ref, k_hbm, v_hbm, a_hbm, th_hbm, e_ref, l_hbm, kb, vb, pb, mixed, l_buf, kv_sem, p_sem, l_sem):
     half = e_ref.shape[1]
     base = off_ref[0] * half
 
@@ -156,7 +160,7 @@
     whole = pl.ds(pl.multiple_of(base, LANE), half)
     poles = [
         pltpu.make_async_copy(src.at[:, whole], pb.at[i], p_sem.at[i])
-        for i, src in enumerate((a_hbm, th_hbm, rr_hbm, ri_hbm))
+        for i, src in enumerate((a_hbm, th_hbm))
     ]
     for copy in poles + fetches(0) + fetches(1):
         copy.start()
@@ -173,7 +177,7 @@
 
         ls = lanes(0, g)
         mixed[...] = kb[:, ls].astype(F32) * vb[:, ls].astype(F32)
-        end_states(mixed, [pb.at[i] for i in range(4)], (ls, ls), e_ref, l_buf)
+        end_states(mixed, [pb.at[i] for i in range(2)], (ls, ls), e_ref, l_buf)
 
     stored = l_hbm.shape[0]
     finish = stream(stored, [(l_buf, l_hbm, l_sem)], lambda g: group(g, l_buf.at[g]))
@@ -181,13 +185,13 @@
     finish()
 
 
-def own_kernel(off_ref, k_ref, v_ref, a_ref, th_ref, rr_ref, ri_ref, e_ref, pw_ref, l_hbm, mixed, l_buf, l_sem):
+def own_kernel(off_ref, k_ref, v_ref, a_ref, th_ref, e_ref, pw_ref, l_hbm, mixed, l_buf, l_sem):
     half = e_ref.shape[1]
 
     def group(g, l_buf):
         src, dst = lanes(off_ref[0] * half, g), lanes(0, g)
         mixed[...] = k_ref[:, src].astype(F32) * v_ref[:, src].astype(F32)
-        end_states(mixed, (a_ref, th_ref, rr_ref, ri_ref), (src, dst), e_ref, l_buf, pw_ref)
+        end_states(mixed, (a_ref, th_ref), (src, dst), e_ref, l_buf, pw_ref)
 
     stored = l_hbm.shape[0]
     finish = stream(stored, [(l_buf, l_hbm, l_sem)], lambda g: group(g, l_buf.at[g]))
@@ -195,12 +199,15 @@
     finish()
 
 
-def fill_table(table, pr, pi, m0, modes):
-    tr, ti = power_table(pr, pi, pr, pi, BLOCK)
-    for j in range(BLOCK):
+def fill_table(table, poles, m0, src):
+    modes = poles[0].shape[0]
+    pr, pi, (tr, ti) = pole_table(*poles, slice(m0, m0 + SUB), src)
+    tr, ti = power_table(pr, pi, tr[1], ti[1], BLOCK)
+    qr, qi = squared(pr, pi, BLOCK.bit_length() - 1)
+    for j, (r, i) in enumerate(zip(tr + [qr], ti + [qi])):
         base = j * 2 * modes + m0
-        table[base : base + SUB, :] = tr[j]
-        table[base + modes : base + modes + SUB, :] = ti[j]
+        table[base : base + SUB, :] = r
+        table[base + modes : base + modes + SUB, :] = i
 
 
 def near_kernel(
@@ -227,8 +234,8 @@
             pr, pi, (tr, _) = pole_table(a_ref, th_ref, rr_ref, ri_ref, slice(m0, m0 + SUB), src)
             sums = tr if sums is None else [x + y for x, y in zip(sums, tr)]
             if table_ref is not None:
-                ms, there = slice(m0, m0 + SUB), lanes((1 - off_ref[0]) * half, g)
-                fill_table(table_ref.at[g], *pole_power(a_ref[ms, there], th_ref[ms, there], 1), m0, modes)
+                there = lanes((1 - off_ref[0]) * half, g)
+                fill_table(table_ref.at[g], (a_ref, th_ref, rr_ref, ri_ref), m0, there)
         taps = []
         for j in range(BLOCK):
             tap = jnp.sum(sums[j], axis=0, keepdims=True)
@@ -250,7 +257,7 @@
     def states(i):
         src = lanes(off_ref[0] * half, groups - tail + i)
         plain[...] = k_ref[:, src].astype(F32) * v_ref[:, src].astype(F32)
-        end_states(plain, (a_ref, th_ref, rr_ref, ri_ref), (src, src), None, l_buf.at[i])
+        end_states(plain, (a_ref, th_ref), (src, src), None, l_buf.at[i])
 
     finish_states = stream(tail, [(l_buf, l_hbm, l_sem)], states)
     finish = stream(groups, [(y_buf, y_hbm, y_sem)], group)
@@ -260,7 +267,7 @@
 
 def far_kernel(off_ref, s_ref, l_ref, tail_ref, y_ref, q_ref, table_ref, *refs):
     if len(refs) > 4:
-        a_ref, th_ref, gated_ref, power_ref, next_ref, state, conv = refs
+        *poles, gated_ref, power_ref, next_ref, state, conv = refs
     else:
         gated_ref, power_ref, state, conv = refs
         next_ref = None
@@ -281,8 +288,8 @@
             ms = slice(m0, m0 + SUB)
             if next_ref is not None:
                 there = lanes((1 - off_ref[0]) * half, g)
-                fill_table(next_ref.at[g], *pole_power(a_ref[ms, there], th_ref[ms, there], 1), m0, modes)
-            last = (BLOCK - 1) * 2 * modes + m0
+                fill_table(next_ref.at[g], poles, m0, there)
+            last = BLOCK * 2 * modes + m0
             qr, qi = table[last : last + SUB, :], table[last + modes : last + modes + SUB, :]
             sr, si = s_ref[ms, dst], s_ref[modes + m0 : modes + m0 + SUB, dst]
             for b in range(blocks):
@@ -382,7 +389,7 @@
     groups = half // LANE
     local = (groups - TAIL, blocks * states, LANE)
     tail = (TAIL, blocks * states, LANE)
-    table = (groups, BLOCK * states, LANE)
+    table = (groups, (BLOCK + 1) * states, LANE)
     near_shape = (groups, rows, LANE)
 
     group_sem = pltpu.SemaphoreType.DMA((groups,))
@@ -402,17 +409,17 @@
     scratch = [
         pltpu.VMEM((rows, half), k.dtype),
         pltpu.VMEM((rows, half), v.dtype),
-        pltpu.VMEM((4, modes, half), F32),
+        pltpu.VMEM((2, modes, half), F32),
         mixed,
         pltpu.VMEM(local, F32),
         pltpu.SemaphoreType.DMA((2, 2)),
-        pltpu.SemaphoreType.DMA((4,)),
+        pltpu.SemaphoreType.DMA((2,)),
         stored_sem,
     ]
-    sent_end, sent_local = call(sent_kernel, other, [k, v, *poles], [state], [local], scratch, pltpu.HBM)
+    sent_end, sent_local = call(sent_kernel, other, [k, v, decay, angle], [state], [local], scratch, pltpu.HBM)
     pair_end = exchange(sent_end, "seq", 1)
     scratch = [mixed, pltpu.VMEM(local, F32), stored_sem]
-    own_end, step_power, own_local = call(own_kernel, own, [k, v, *poles], [state] * 2, [local], scratch)
+    own_end, step_power, own_local = call(own_kernel, own, [k, v, decay, angle], [state] * 2, [local], scratch)
     low = jnp.where(upper, pair_end, own_end)
     high = jnp.where(upper, own_end, pair_end)
     total = times(step_power, low) + high
@@ -442,7 +449,7 @@
     own_start = jnp.where(upper, after_low, before)
     other_start = exchange(jnp.where(upper, before, after_low), "seq", 1)
     own_table, *other_ready = ready[1]
-    own_gated, own_power, other_table = far(own, own_start, own_local, *ready[0], own_table, decay, angle)
+    own_gated, own_power, other_table = far(own, own_start, own_local, *ready[0], own_table, *poles)
     other_gated, other_power = far(other, other_start, sent_local, *other_ready, other_table)
     power = jnp.sum(own_power + other_power, axis=1)
     distance = 1

time: 38.5 us -> 38 us (0.987)
  transfers between devices with their start and end apart: 6 -> 6, of which waited for: 6 -> 6; matrix products, arithmetic and copies ran while one was open for 0% -> 0% of each run, Pallas kernels for 32% -> 33%
where the time goes in v5:
time: 38 us; the launch traced here: 37.9 us
  Pallas kernels  20.7 us (54%)
  starting transfers between devices  10.9 us (29%)
  waiting for transfers between devices  5.55 us (15%)
  other arithmetic  0.39 us (1%)
    pallas_call x7, Pallas kernels, call(): pl.pallas_call(kernel, in_specs=[pl.BlockSpec(memory_space=pltpu.SMEM)] +...  20.7 us
    ppermute x6, starting transfers between devices, exchange(): lax.ppermute(x, axis, [(i, i ^ distance) for i in range(lax.axis_size(axi...  10.9 us
    ppermute x6, waiting for transfers between devices, exchange(): lax.ppermute(x, axis, [(i, i ^ distance) for i in range(lax.axis_size(axi...  5.55 us
  transfers between devices with their start and end apart: 6, of which 6 were waited for; matrix products, arithmetic and copies ran while one was open for 0% of the time, Pallas kernels for 33%

profile of v5, /device:TPU:0, one launch (start us, length us, event | category | flops | bytes accessed | tf_op | source)
XLA Modules:
  0.0 37.9 jit_solution(13517319755960631611)
XLA Ops:
  0.0 4.4 %shard_map.92 = (f32[32,1024]{1,0:T(8,128)S(1)}, f32[6,512,128]{2,1,0:T(8,128)}) custom-call(s32[1]{0:T(128)S(6)} %sub.21.off_ref, bf16[256,2048]{1,0:T(8,128)(2,1)} %k_ref.5, bf16[256,2048]{1,0:T(8,128)(2,1)} %v_ref.5, f32[16,2048]{1,0:T(8,128)} %refs_0_.1, f32[16,2048]{1,0:T(8,128)} %refs_1_.1), custom_call_target="tpu_custom_call" | custom-call | tf_op jit(solution)/shard_map/pallas_call | solution.py:348
  4.4 0.0 copy-start.7
  4.4 0.0 copy-start.8
  4.4 0.0 copy-start.13
  4.4 3.1 %collective-permute-start = (f32[32,1024]{1,0:T(8,128)S(1)}, f32[32,1024]{1,0:T(8,128)S(1)}, u32[]{:S(2)}, u32[]{:S(2)}) collective-permute-start(f32[32,1024]{1,0:T(8,128)S(1)} %get-tuple-element.28), channel_id=1, source_target_pairs={{0,4},{4,0},{8,12},{12,8},{16,20},{20,16},{24,28},{28,24},{1,5},{5... | collective-permute-start | bytes 393224 | tf_op jit(solution)/shard_map/ppermute | solution.py:360
  7.5 0.0 copy-done.4
  7.5 0.0 copy-done.3
  7.5 0.0 copy-done.1
  7.5 0.0 copy-done
  7.5 3.1 %shard_map.91 = (f32[32,1024]{1,0:T(8,128)S(1)}, f32[32,1024]{1,0:T(8,128)S(1)}, f32[6,512,128]{2,1,0:T(8,128)}) custom-call(s32[1]{0:T(128)} %bitcast.off_ref, bf16[256,2048]{1,0:T(8,128)(2,1)S(1)} %copy-done, bf16[256,2048]{1,0:T(8,128)(2,1)S(1)} %copy-done.1, f32[16,2048]{1,0:T(8,128)S(1)} %copy-done.3, f32[16,2048]{1,0:T(8,128)S(1)} %copy-done.4), custom_call_target="tpu_custom_call" | custom-call | tf_op jit(solution)/shard_map/pallas_call | solution.py:348
  10.6 0.4 collective-permute-done
  11.0 1.9 %collective-permute-start.1 = (f32[32,1024]{1,0:T(8,128)S(1)}, f32[32,1024]{1,0:T(8,128)S(1)}, u32[]{:S(2)}, u32[]{:S(2)}) collective-permute-start(f32[32,1024]{1,0:T(8,128)S(1)} %maximum_add_fusion.after_ref), channel_id=1, source_target_pairs={{0,8},{4,12},{8,0},{12,4},{16,24},{20,28},{24,16},{28,20},{1,9},{5... | collective-permute-start | bytes 393224 | tf_op jit(solution)/shard_map/ppermute | solution.py:360
  12.9 2.8 %shard_map.93 = (f32[2,512,128]{2,1,0:T(8,128)}, f32[8,256,128]{2,1,0:T(8,128)}) custom-call(s32[1]{0:T(128)} %bitcast.off_ref, f32[32,1024]{1,0:T(8,128)S(1)} %maximum_add_fusion.after_ref, bf16[256,2048]{1,0:T(8,128)(2,1)S(1)} %copy-done, bf16[256,2048]{1,0:T(8,128)(2,1)S(1)} %copy-done.1, f32[16,2048]{1,0:T(8,128)S(1)} %copy-done.3, ...), custom_call_target="tpu_custom_call" | custom-call | tf_op jit(solution)/shard_map/pallas_call | solution.py:348
  15.8 0.3 collective-permute-done.1
  16.1 2.9 %collective-permute-start.2 = (f32[32,1024]{1,0:T(8,128)S(1)}, f32[32,1024]{1,0:T(8,128)S(1)}, u32[]{:S(2)}, u32[]{:S(2)}) collective-permute-start(f32[32,1024]{1,0:T(8,128)S(1)} %fusion.after_ref), channel_id=1, source_target_pairs={{0,16},{4,20},{8,24},{12,28},{16,0},{20,4},{24,8},{28,12},{1,17},{... | collective-permute-start | bytes 393224 | tf_op jit(solution)/shard_map/ppermute | solution.py:360
  19.0 3.1 %shard_map.94 = (f32[8,544,128]{2,1,0:T(8,128)S(1)}, f32[2,512,128]{2,1,0:T(8,128)}, f32[8,256,128]{2,1,0:T(8,128)}) custom-call(s32[1]{0:T(128)S(6)} %sub.21.off_ref, f32[32,1024]{1,0:T(8,128)S(1)} %fusion.after_ref, bf16[256,2048]{1,0:T(8,128)(2,1)S(1)} %copy-done, bf16[256,2048]{1,0:T(8,128)(2,1)S(1)} %copy-done.1, f32[16,2048]{1,0:T(8,128)S(1)} %copy-done.3, ...), custom_call_target="tpu_custom_call" | custom-call | tf_op jit(solution)/shard_map/pallas_call | solution.py:348
  22.2 1.6 %collective-permute-done.2 = f32[32,1024]{1,0:T(8,128)S(1)} collective-permute-done((f32[32,1024]{1,0:T(8,128)S(1)}, f32[32,1024]{1,0:T(8,128)S(1)}, u32[]{:S(2)}, u32[]{:S(2)}) %collective-permute-start.2) | collective-permute-done | bytes 131104 | tf_op jit(solution)/shard_map/ppermute | solution.py:360
  23.9 1.5 %collective-permute-start.3 = (f32[32,1024]{1,0:T(8,128)S(1)}, f32[32,1024]{1,0:T(8,128)S(1)}, u32[]{:S(2)}, u32[]{:S(2)}) collective-permute-start(f32[32,1024]{1,0:T(8,128)S(1)} %get-tuple-element.52), channel_id=1, source_target_pairs={{0,4},{4,0},{8,12},{12,8},{16,20},{20,16},{24,28},{28,24},{1,5},{5... | collective-permute-start | bytes 393224 | tf_op jit(solution)/shard_map/ppermute | solution.py:360
  25.4 0.0 copy-done.9
  25.4 3.3 %shard_map.95 = (f32[256,1024]{1,0:T(8,128)S(1)}, f32[256,128]{1,0:T(8,128)S(1)}, f32[8,544,128]{2,1,0:T(8,128)S(1)}) custom-call(s32[1]{0:T(128)} %bitcast.off_ref, f32[32,1024]{1,0:T(8,128)S(1)} %get-tuple-element.53.s_ref, f32[6,512,128]{2,1,0:T(8,128)S(1)} %copy-done.5, f32[2,512,128]{2,1,0:T(8,128)S(1)} %copy-done.11, f32[8,256,128]{2,1,0:T(8,128)S(1)} %copy-done.9, ...), custom_call_target="tpu_custom_call" | custom-call | tf_op jit(solution)/shard_map/pallas_call | solution.py:348
  28.8 0.1 collective-permute-done.3.s_ref
  28.9 0.0 copy-done.10
  28.9 0.0 copy-start.14
  28.9 2.9 %shard_map.96 = (f32[256,1024]{1,0:T(8,128)S(1)}, f32[256,128]{1,0:T(8,128)S(1)}) custom-call(s32[1]{0:T(128)S(6)} %sub.21.off_ref, f32[32,1024]{1,0:T(8,128)S(1)} %collective-permute-done.3.s_ref, f32[6,512,128]{2,1,0:T(8,128)S(1)} %copy-done.6, f32[2,512,128]{2,1,0:T(8,128)S(1)} %copy-done.12, f32[8,256,128]{2,1,0:T(8,128)S(1)} %copy-done.10, ...), custom_call_target="tpu_custom_call" | custom-call | tf_op jit(solution)/shard_map/pallas_call | solution.py:348
  31.8 0.1 add_reduce_fusion
  31.9 0.1 collective-permute-start.4
  32.0 1.1 %collective-permute-done.4 = f32[256]{0:T(256)S(1)} collective-permute-done((f32[256]{0:T(256)S(1)}, f32[256]{0:T(256)S(1)}, u32[]{:S(2)}, u32[]{:S(2)}) %collective-permute-start.4) | collective-permute-done | bytes 1056 | tf_op jit(solution)/shard_map/ppermute | solution.py:360
  33.1 1.5 %collective-permute-start.5 = (f32[256]{0:T(256)S(1)}, f32[256]{0:T(256)S(1)}, u32[]{:S(2)}, u32[]{:S(2)}) collective-permute-start(f32[256]{0:T(256)S(1)} %add.60), channel_id=1, source_target_pairs={{0,2},{1,3},{2,0},{3,1},{4,6},{5,7},{6,4},{7,5},{8,10},{9,11},{10,... | collective-permute-start | bytes 3080 | tf_op jit(solution)/shard_map/ppermute | solution.py:360
  34.6 2.1 %collective-permute-done.5 = f32[256]{0:T(256)S(1)} collective-permute-done((f32[256]{0:T(256)S(1)}, f32[256]{0:T(256)S(1)}, u32[]{:S(2)}, u32[]{:S(2)}) %collective-permute-start.5) | collective-permute-done | bytes 1056 | tf_op jit(solution)/shard_map/ppermute | solution.py:360
  36.7 0.1 broadcast_in_dim.20.scale_ref
  36.8 0.0 copy-done.14
  36.8 1.1 %shard_map.97 = bf16[256,2048]{1,0:T(8,128)(2,1)} custom-call(s32[1]{0:T(128)} %bitcast.off_ref, f32[256,1024]{1,0:T(8,128)S(1)} %get-tuple-element.41.own_ref, f32[256,1024]{1,0:T(8,128)S(1)} %get-tuple-element.46.other_ref, f32[256,128]{1,0:T(8,128)S(1)} %broadcast_in_dim.20.scale_ref, f32[1,2048]{1,0:T(1,128)S(1)} %bitcast.5), custom_call_target="tpu_custom_call" | custom-call | tf_op jit(solution)/shard_map/pallas_call | solution.py:348
  (31 shorter events, 0.3 us)
Async XLA Ops:
  0.0 7.5 %copy-start.4 = (f32[16,2048]{1,0:T(8,128)S(1)}, f32[16,2048]{1,0:T(8,128)}, u32[]{:S(2)}) copy-start(f32[16,2048]{1,0:T(8,128)} %refs_1_.1) | copy-start | bytes 393220
  0.0 7.5 %copy-start.3 = (f32[16,2048]{1,0:T(8,128)S(1)}, f32[16,2048]{1,0:T(8,128)}, u32[]{:S(2)}) copy-start(f32[16,2048]{1,0:T(8,128)} %refs_0_.1) | copy-start | bytes 393220
  0.0 7.5 %copy-start.1 = (bf16[256,2048]{1,0:T(8,128)(2,1)S(1)}, bf16[256,2048]{1,0:T(8,128)(2,1)}, u32[]{:S(2)}) copy-start(bf16[256,2048]{1,0:T(8,128)(2,1)} %v_ref.5) | copy-start | bytes 3145732
  0.0 7.5 %copy-start = (bf16[256,2048]{1,0:T(8,128)(2,1)S(1)}, bf16[256,2048]{1,0:T(8,128)(2,1)}, u32[]{:S(2)}) copy-start(bf16[256,2048]{1,0:T(8,128)(2,1)} %k_ref.5) | copy-start | bytes 3145732
  4.4 8.5 %copy-start.7 = (f32[16,2048]{1,0:T(8,128)S(1)}, f32[16,2048]{1,0:T(8,128)}, u32[]{:S(2)}) copy-start(f32[16,2048]{1,0:T(8,128)} %refs_2_.1) | copy-start | bytes 393220
  4.4 8.5 %copy-start.8 = (f32[16,2048]{1,0:T(8,128)S(1)}, f32[16,2048]{1,0:T(8,128)}, u32[]{:S(2)}) copy-start(f32[16,2048]{1,0:T(8,128)} %refs_3_.1) | copy-start | bytes 393220
  4.4 8.5 %copy-start.13 = (f32[2048]{0:T(1024)S(1)}, f32[2048]{0:T(1024)}, u32[]{:S(2)}) copy-start(f32[2048]{0:T(1024)} %param.16) | copy-start | bytes 24580
  4.4 6.6 %collective-permute-start = (f32[32,1024]{1,0:T(8,128)S(1)}, f32[32,1024]{1,0:T(8,128)S(1)}, u32[]{:S(2)}, u32[]{:S(2)}) collective-permute-start(f32[32,1024]{1,0:T(8,128)S(1)} %get-tuple-element.28), channel_id=1, source_target_pairs={{0,4},{4,0},{8,12},{12,8},{16,20},{20,16},{24,28},{28,24},{1,5},{5... | collective-permute-start | bytes 393224 | tf_op jit(solution)/shard_map/ppermute | solution.py:360
  11.0 5.0 %collective-permute-start.1 = (f32[32,1024]{1,0:T(8,128)S(1)}, f32[32,1024]{1,0:T(8,128)S(1)}, u32[]{:S(2)}, u32[]{:S(2)}) collective-permute-start(f32[32,1024]{1,0:T(8,128)S(1)} %maximum_add_fusion.after_ref), channel_id=1, source_target_pairs={{0,8},{4,12},{8,0},{12,4},{16,24},{20,28},{24,16},{28,20},{1,9},{5... | collective-permute-start | bytes 393224 | tf_op jit(solution)/shard_map/ppermute | solution.py:360
  16.1 7.6 %collective-permute-start.2 = (f32[32,1024]{1,0:T(8,128)S(1)}, f32[32,1024]{1,0:T(8,128)S(1)}, u32[]{:S(2)}, u32[]{:S(2)}) collective-permute-start(f32[32,1024]{1,0:T(8,128)S(1)} %fusion.after_ref), channel_id=1, source_target_pairs={{0,16},{4,20},{8,24},{12,28},{16,0},{20,4},{24,8},{28,12},{1,17},{... | collective-permute-start | bytes 393224 | tf_op jit(solution)/shard_map/ppermute | solution.py:360
  19.0 6.4 %copy-start.2 = (bf16[256,2048]{1,0:T(8,128)(2,1)S(1)}, bf16[256,2048]{1,0:T(8,128)(2,1)}, u32[]{:S(2)}) copy-start(bf16[256,2048]{1,0:T(8,128)(2,1)} %q_ref.3) | copy-start | bytes 3145732
  19.0 6.4 %copy-start.5 = (f32[6,512,128]{2,1,0:T(8,128)S(1)}, f32[6,512,128]{2,1,0:T(8,128)}, u32[]{:S(2)}) copy-start(f32[6,512,128]{2,1,0:T(8,128)} %get-tuple-element.37.l_ref) | copy-start | bytes 4718596
  19.0 6.4 %copy-start.9 = (f32[8,256,128]{2,1,0:T(8,128)S(1)}, f32[8,256,128]{2,1,0:T(8,128)}, u32[]{:S(2)}) copy-start(f32[8,256,128]{2,1,0:T(8,128)} %get-tuple-element.39.y_ref) | copy-start | bytes 3145732
  19.0 6.4 %copy-start.11 = (f32[2,512,128]{2,1,0:T(8,128)S(1)}, f32[2,512,128]{2,1,0:T(8,128)}, u32[]{:S(2)}) copy-start(f32[2,512,128]{2,1,0:T(8,128)} %get-tuple-element.38.tail_ref) | copy-start | bytes 1572868
  23.9 5.0 %collective-permute-start.3 = (f32[32,1024]{1,0:T(8,128)S(1)}, f32[32,1024]{1,0:T(8,128)S(1)}, u32[]{:S(2)}, u32[]{:S(2)}) collective-permute-start(f32[32,1024]{1,0:T(8,128)S(1)} %get-tuple-element.52), channel_id=1, source_target_pairs={{0,4},{4,0},{8,12},{12,8},{16,20},{20,16},{24,28},{28,24},{1,5},{5... | collective-permute-start | bytes 393224 | tf_op jit(solution)/shard_map/ppermute | solution.py:360
  25.4 3.5 %copy-start.6 = (f32[6,512,128]{2,1,0:T(8,128)S(1)}, f32[6,512,128]{2,1,0:T(8,128)}, u32[]{:S(2)}) copy-start(f32[6,512,128]{2,1,0:T(8,128)} %get-tuple-element.42.l_ref) | copy-start | bytes 4718596
  25.4 3.5 %copy-start.10 = (f32[8,256,128]{2,1,0:T(8,128)S(1)}, f32[8,256,128]{2,1,0:T(8,128)}, u32[]{:S(2)}) copy-start(f32[8,256,128]{2,1,0:T(8,128)} %get-tuple-element.44.y_ref) | copy-start | bytes 3145732
  25.4 3.5 %copy-start.12 = (f32[2,512,128]{2,1,0:T(8,128)S(1)}, f32[2,512,128]{2,1,0:T(8,128)}, u32[]{:S(2)}) copy-start(f32[2,512,128]{2,1,0:T(8,128)} %get-tuple-element.43.tail_ref) | copy-start | bytes 1572868
  28.9 7.9 %copy-start.14 = (f32[2048]{0:T(1024)S(1)}, f32[2048]{0:T(1024)}, u32[]{:S(2)}) copy-start(f32[2048]{0:T(1024)} %param.17) | copy-start | bytes 24580
  31.9 1.2 %collective-permute-start.4 = (f32[256]{0:T(256)S(1)}, f32[256]{0:T(256)S(1)}, u32[]{:S(2)}, u32[]{:S(2)}) collective-permute-start(f32[256]{0:T(256)S(1)} %add_reduce_fusion), channel_id=1, source_target_pairs={{0,1},{1,0},{2,3},{3,2},{4,5},{5,4},{6,7},{7,6},{8,9},{9,8},{10,11... | collective-permute-start | bytes 3080 | tf_op jit(solution)/shard_map/ppermute | solution.py:360
  33.1 3.6 %collective-permute-start.5 = (f32[256]{0:T(256)S(1)}, f32[256]{0:T(256)S(1)}, u32[]{:S(2)}, u32[]{:S(2)}) collective-permute-start(f32[256]{0:T(256)S(1)} %add.60), channel_id=1, source_target_pairs={{0,2},{1,3},{2,0},{3,1},{4,6},{5,7},{6,4},{7,5},{8,10},{9,11},{10,... | collective-permute-start | bytes 3080 | tf_op jit(solution)/shard_map/ppermute | solution.py:360

commit v6 on v5

--- a/solution.py
+++ b/solution.py
@@ -39,7 +39,10 @@
 def pole_power(decay, angle, count):
     phase = angle * float(count)
     n = jnp.floor(phase * 0.6366197723675814 + 0.5)
-    r = ((phase - n * 1.5703125) - n * 4.837512969970703125e-4) - n * 7.549789948768648e-8
+    if count == 1:
+        r = (phase - n * 1.57079637050628662109375) + n * 4.37113900018624283e-8
+    else:
+        r = ((phase - n * 1.5703125) - n * 4.837512969970703125e-4) - n * 7.549789948768648e-8
     cos, sin = cos_sin(r, n)
     size = jnp.exp(decay * -float(count))
     return size * cos, size * sin
@@ -266,10 +269,11 @@
 
 
 def far_kernel(off_ref, s_ref, l_ref, tail_ref, y_ref, q_ref, table_ref, *refs):
-    if len(refs) > 4:
+    first_power = None
+    if len(refs) > 5:
         *poles, gated_ref, power_ref, next_ref, state, conv = refs
     else:
-        gated_ref, power_ref, state, conv = refs
+        first_power, gated_ref, power_ref, state, conv = refs
         next_ref = None
     rows = q_ref.shape[0]
     modes = s_ref.shape[0] // 2
@@ -279,7 +283,7 @@
     starts = range(0, blocks, SUB)
     apart = 2 * modes + 1
     every = slice(None)
-    power_ref[...] = jnp.zeros_like(power_ref)
+    power_ref[...] = jnp.zeros_like(power_ref) if first_power is None else first_power[...]
 
     def group(g, l_ref):
         src, dst = lanes(off_ref[0] * half, g), lanes(0, g)
@@ -403,7 +407,7 @@
 
     def far(offset, start, local, tail, y, *ins):
         scratch = [pltpu.VMEM(((blocks + 1) * (states + 1) + SUB, LANE), F32), padded]
-        outs = [(rows, half), (rows, LANE)] + [table] * (len(ins) > 1)
+        outs = [(rows, half), (rows, LANE)] + [table] * (len(ins) > 2)
         return call(far_kernel, offset, [start, local, tail, y, q, *ins], outs, [], scratch)
 
     scratch = [
@@ -450,8 +454,8 @@
     other_start = exchange(jnp.where(upper, before, after_low), "seq", 1)
     own_table, *other_ready = ready[1]
     own_gated, own_power, other_table = far(own, own_start, own_local, *ready[0], own_table, *poles)
-    other_gated, other_power = far(other, other_start, sent_local, *other_ready, other_table)
-    power = jnp.sum(own_power + other_power, axis=1)
+    other_gated, power = far(other, other_start, sent_local, *other_ready, other_table, own_power)
+    power = jnp.sum(power, axis=1)
     distance = 1
     while distance < lax.axis_size("ch"):
         power = power + exchange(power, "ch", distance)

time: 38 us -> 38 us (level)
  transfers between devices with their start and end apart: 6 -> 6, of which waited for: 6 -> 6; matrix products, arithmetic and copies ran while one was open for 0% -> 0% of each run, Pallas kernels for 33% -> 32%
where the time goes in v6:
time: 38 us; the launch traced here: 37.9 us
  Pallas kernels  20.6 us (54%)
  starting transfers between devices  10.9 us (29%)
  waiting for transfers between devices  5.6 us (15%)
  other arithmetic  0.38 us (1%)
    pallas_call x7, Pallas kernels, call(): pl.pallas_call(kernel, in_specs=[pl.BlockSpec(memory_space=pltpu.SMEM)] +...  20.6 us
    ppermute x6, starting transfers between devices, exchange(): lax.ppermute(x, axis, [(i, i ^ distance) for i in range(lax.axis_size(axi...  10.9 us
    ppermute x6, waiting for transfers between devices, exchange(): lax.ppermute(x, axis, [(i, i ^ distance) for i in range(lax.axis_size(axi...  5.6 us
  transfers between devices with their start and end apart: 6, of which 6 were waited for; matrix products, arithmetic and copies ran while one was open for 0% of the time, Pallas kernels for 32%

profile of v6, /device:TPU:0, one launch (start us, length us, event | category | flops | bytes accessed | tf_op | source)
XLA Modules:
  0.0 37.9 jit_solution(17385042825548594436)
XLA Ops:
  0.0 4.3 %shard_map.92 = (f32[32,1024]{1,0:T(8,128)S(1)}, f32[6,512,128]{2,1,0:T(8,128)}) custom-call(s32[1]{0:T(128)S(6)} %sub.21.off_ref, bf16[256,2048]{1,0:T(8,128)(2,1)} %k_ref.5, bf16[256,2048]{1,0:T(8,128)(2,1)} %v_ref.5, f32[16,2048]{1,0:T(8,128)} %refs_0_.1, f32[16,2048]{1,0:T(8,128)} %refs_1_.1), custom_call_target="tpu_custom_call" | custom-call | tf_op jit(solution)/shard_map/pallas_call | solution.py:352
  4.4 0.0 copy-start.7
  4.4 0.0 copy-start.8
  4.4 0.0 copy-start.13
  4.4 3.1 %collective-permute-start = (f32[32,1024]{1,0:T(8,128)S(1)}, f32[32,1024]{1,0:T(8,128)S(1)}, u32[]{:S(2)}, u32[]{:S(2)}) collective-permute-start(f32[32,1024]{1,0:T(8,128)S(1)} %get-tuple-element.28), channel_id=1, source_target_pairs={{0,4},{4,0},{8,12},{12,8},{16,20},{20,16},{24,28},{28,24},{1,5},{5... | collective-permute-start | bytes 393224 | tf_op jit(solution)/shard_map/ppermute | solution.py:364
  7.5 0.0 copy-done.4
  7.5 0.0 copy-done.3
  7.5 3.1 %shard_map.91 = (f32[32,1024]{1,0:T(8,128)S(1)}, f32[32,1024]{1,0:T(8,128)S(1)}, f32[6,512,128]{2,1,0:T(8,128)}) custom-call(s32[1]{0:T(128)} %bitcast.off_ref, bf16[256,2048]{1,0:T(8,128)(2,1)S(1)} %copy-done, bf16[256,2048]{1,0:T(8,128)(2,1)S(1)} %copy-done.1, f32[16,2048]{1,0:T(8,128)S(1)} %copy-done.3, f32[16,2048]{1,0:T(8,128)S(1)} %copy-done.4), custom_call_target="tpu_custom_call" | custom-call | tf_op jit(solution)/shard_map/pallas_call | solution.py:352
  10.6 0.4 collective-permute-done
  11.0 1.9 %collective-permute-start.1 = (f32[32,1024]{1,0:T(8,128)S(1)}, f32[32,1024]{1,0:T(8,128)S(1)}, u32[]{:S(2)}, u32[]{:S(2)}) collective-permute-start(f32[32,1024]{1,0:T(8,128)S(1)} %maximum_add_fusion.after_ref), channel_id=1, source_target_pairs={{0,8},{4,12},{8,0},{12,4},{16,24},{20,28},{24,16},{28,20},{1,9},{5... | collective-permute-start | bytes 393224 | tf_op jit(solution)/shard_map/ppermute | solution.py:364
  12.9 0.0 copy-done.13
  12.9 2.8 %shard_map.93 = (f32[2,512,128]{2,1,0:T(8,128)}, f32[8,256,128]{2,1,0:T(8,128)}) custom-call(s32[1]{0:T(128)} %bitcast.off_ref, f32[32,1024]{1,0:T(8,128)S(1)} %maximum_add_fusion.after_ref, bf16[256,2048]{1,0:T(8,128)(2,1)S(1)} %copy-done, bf16[256,2048]{1,0:T(8,128)(2,1)S(1)} %copy-done.1, f32[16,2048]{1,0:T(8,128)S(1)} %copy-done.3, ...), custom_call_target="tpu_custom_call" | custom-call | tf_op jit(solution)/shard_map/pallas_call | solution.py:352
  15.7 0.3 collective-permute-done.1
  16.1 2.9 %collective-permute-start.2 = (f32[32,1024]{1,0:T(8,128)S(1)}, f32[32,1024]{1,0:T(8,128)S(1)}, u32[]{:S(2)}, u32[]{:S(2)}) collective-permute-start(f32[32,1024]{1,0:T(8,128)S(1)} %fusion.after_ref), channel_id=1, source_target_pairs={{0,16},{4,20},{8,24},{12,28},{16,0},{20,4},{24,8},{28,12},{1,17},{... | collective-permute-start | bytes 393224 | tf_op jit(solution)/shard_map/ppermute | solution.py:364
  19.0 3.1 %shard_map.94 = (f32[8,544,128]{2,1,0:T(8,128)S(1)}, f32[2,512,128]{2,1,0:T(8,128)}, f32[8,256,128]{2,1,0:T(8,128)}) custom-call(s32[1]{0:T(128)S(6)} %sub.21.off_ref, f32[32,1024]{1,0:T(8,128)S(1)} %fusion.after_ref, bf16[256,2048]{1,0:T(8,128)(2,1)S(1)} %copy-done, bf16[256,2048]{1,0:T(8,128)(2,1)S(1)} %copy-done.1, f32[16,2048]{1,0:T(8,128)S(1)} %copy-done.3, ...), custom_call_target="tpu_custom_call" | custom-call | tf_op jit(solution)/shard_map/pallas_call | solution.py:352
  22.2 1.6 %collective-permute-done.2 = f32[32,1024]{1,0:T(8,128)S(1)} collective-permute-done((f32[32,1024]{1,0:T(8,128)S(1)}, f32[32,1024]{1,0:T(8,128)S(1)}, u32[]{:S(2)}, u32[]{:S(2)}) %collective-permute-start.2) | collective-permute-done | bytes 131104 | tf_op jit(solution)/shard_map/ppermute | solution.py:364
  23.8 1.6 %collective-permute-start.3 = (f32[32,1024]{1,0:T(8,128)S(1)}, f32[32,1024]{1,0:T(8,128)S(1)}, u32[]{:S(2)}, u32[]{:S(2)}) collective-permute-start(f32[32,1024]{1,0:T(8,128)S(1)} %get-tuple-element.52), channel_id=1, source_target_pairs={{0,4},{4,0},{8,12},{12,8},{16,20},{20,16},{24,28},{28,24},{1,5},{5... | collective-permute-start | bytes 393224 | tf_op jit(solution)/shard_map/ppermute | solution.py:364
  25.4 0.0 copy-done.2
  25.4 0.0 copy-start.6
  25.4 0.0 copy-start.10
  25.4 0.0 copy-start.12
  25.4 3.3 %shard_map.95 = (f32[256,1024]{1,0:T(8,128)S(1)}, f32[256,128]{1,0:T(8,128)S(1)}, f32[8,544,128]{2,1,0:T(8,128)S(1)}) custom-call(s32[1]{0:T(128)} %bitcast.off_ref, f32[32,1024]{1,0:T(8,128)S(1)} %get-tuple-element.53.s_ref, f32[6,512,128]{2,1,0:T(8,128)S(1)} %copy-done.5, f32[2,512,128]{2,1,0:T(8,128)S(1)} %copy-done.11, f32[8,256,128]{2,1,0:T(8,128)S(1)} %copy-done.9, ...), custom_call_target="tpu_custom_call" | custom-call | tf_op jit(solution)/shard_map/pallas_call | solution.py:352
  28.7 0.2 collective-permute-done.3.s_ref
  28.9 0.0 copy-start.14
  28.9 2.9 %shard_map.96 = (f32[256,1024]{1,0:T(8,128)S(1)}, f32[256,128]{1,0:T(8,128)S(1)}) custom-call(s32[1]{0:T(128)S(6)} %sub.21.off_ref, f32[32,1024]{1,0:T(8,128)S(1)} %collective-permute-done.3.s_ref, f32[6,512,128]{2,1,0:T(8,128)S(1)} %copy-done.6, f32[2,512,128]{2,1,0:T(8,128)S(1)} %copy-done.12, f32[8,256,128]{2,1,0:T(8,128)S(1)} %copy-done.10, ...), custom_call_target="tpu_custom_call" | custom-call | tf_op jit(solution)/shard_map/pallas_call | solution.py:352
  31.8 0.1 reduce_sum.9
  31.9 0.1 collective-permute-start.4
  32.0 1.1 %collective-permute-done.4 = f32[256]{0:T(256)S(1)} collective-permute-done((f32[256]{0:T(256)S(1)}, f32[256]{0:T(256)S(1)}, u32[]{:S(2)}, u32[]{:S(2)}) %collective-permute-start.4) | collective-permute-done | bytes 1056 | tf_op jit(solution)/shard_map/ppermute | solution.py:364
  33.1 1.5 %collective-permute-start.5 = (f32[256]{0:T(256)S(1)}, f32[256]{0:T(256)S(1)}, u32[]{:S(2)}, u32[]{:S(2)}) collective-permute-start(f32[256]{0:T(256)S(1)} %add.56), channel_id=1, source_target_pairs={{0,2},{1,3},{2,0},{3,1},{4,6},{5,7},{6,4},{7,5},{8,10},{9,11},{10,... | collective-permute-start | bytes 3080 | tf_op jit(solution)/shard_map/ppermute | solution.py:364
  34.6 2.1 %collective-permute-done.5 = f32[256]{0:T(256)S(1)} collective-permute-done((f32[256]{0:T(256)S(1)}, f32[256]{0:T(256)S(1)}, u32[]{:S(2)}, u32[]{:S(2)}) %collective-permute-start.5) | collective-permute-done | bytes 1056 | tf_op jit(solution)/shard_map/ppermute | solution.py:364
  36.7 0.1 broadcast_in_dim.20.scale_ref
  36.8 1.1 %shard_map.97 = bf16[256,2048]{1,0:T(8,128)(2,1)} custom-call(s32[1]{0:T(128)} %bitcast.off_ref, f32[256,1024]{1,0:T(8,128)S(1)} %get-tuple-element.41.own_ref, f32[256,1024]{1,0:T(8,128)S(1)} %get-tuple-element.47.other_ref, f32[256,128]{1,0:T(8,128)S(1)} %broadcast_in_dim.20.scale_ref, f32[1,2048]{1,0:T(1,128)S(1)} %bitcast.5), custom_call_target="tpu_custom_call" | custom-call | tf_op jit(solution)/shard_map/pallas_call | solution.py:352
  (31 shorter events, 0.3 us)
Async XLA Ops:
  0.0 7.5 %copy-start.4 = (f32[16,2048]{1,0:T(8,128)S(1)}, f32[16,2048]{1,0:T(8,128)}, u32[]{:S(2)}) copy-start(f32[16,2048]{1,0:T(8,128)} %refs_1_.1) | copy-start | bytes 393220
  0.0 7.5 %copy-start.3 = (f32[16,2048]{1,0:T(8,128)S(1)}, f32[16,2048]{1,0:T(8,128)}, u32[]{:S(2)}) copy-start(f32[16,2048]{1,0:T(8,128)} %refs_0_.1) | copy-start | bytes 393220
  0.0 7.5 %copy-start.1 = (bf16[256,2048]{1,0:T(8,128)(2,1)S(1)}, bf16[256,2048]{1,0:T(8,128)(2,1)}, u32[]{:S(2)}) copy-start(bf16[256,2048]{1,0:T(8,128)(2,1)} %v_ref.5) | copy-start | bytes 3145732
  0.0 7.5 %copy-start = (bf16[256,2048]{1,0:T(8,128)(2,1)S(1)}, bf16[256,2048]{1,0:T(8,128)(2,1)}, u32[]{:S(2)}) copy-start(bf16[256,2048]{1,0:T(8,128)(2,1)} %k_ref.5) | copy-start | bytes 3145732
  4.4 8.5 %copy-start.7 = (f32[16,2048]{1,0:T(8,128)S(1)}, f32[16,2048]{1,0:T(8,128)}, u32[]{:S(2)}) copy-start(f32[16,2048]{1,0:T(8,128)} %refs_2_.1) | copy-start | bytes 393220
  4.4 8.5 %copy-start.8 = (f32[16,2048]{1,0:T(8,128)S(1)}, f32[16,2048]{1,0:T(8,128)}, u32[]{:S(2)}) copy-start(f32[16,2048]{1,0:T(8,128)} %refs_3_.1) | copy-start | bytes 393220
  4.4 8.5 %copy-start.13 = (f32[2048]{0:T(1024)S(1)}, f32[2048]{0:T(1024)}, u32[]{:S(2)}) copy-start(f32[2048]{0:T(1024)} %param.16) | copy-start | bytes 24580
  4.4 6.6 %collective-permute-start = (f32[32,1024]{1,0:T(8,128)S(1)}, f32[32,1024]{1,0:T(8,128)S(1)}, u32[]{:S(2)}, u32[]{:S(2)}) collective-permute-start(f32[32,1024]{1,0:T(8,128)S(1)} %get-tuple-element.28), channel_id=1, source_target_pairs={{0,4},{4,0},{8,12},{12,8},{16,20},{20,16},{24,28},{28,24},{1,5},{5... | collective-permute-start | bytes 393224 | tf_op jit(solution)/shard_map/ppermute | solution.py:364
  11.0 5.0 %collective-permute-start.1 = (f32[32,1024]{1,0:T(8,128)S(1)}, f32[32,1024]{1,0:T(8,128)S(1)}, u32[]{:S(2)}, u32[]{:S(2)}) collective-permute-start(f32[32,1024]{1,0:T(8,128)S(1)} %maximum_add_fusion.after_ref), channel_id=1, source_target_pairs={{0,8},{4,12},{8,0},{12,4},{16,24},{20,28},{24,16},{28,20},{1,9},{5... | collective-permute-start | bytes 393224 | tf_op jit(solution)/shard_map/ppermute | solution.py:364
  16.1 7.6 %collective-permute-start.2 = (f32[32,1024]{1,0:T(8,128)S(1)}, f32[32,1024]{1,0:T(8,128)S(1)}, u32[]{:S(2)}, u32[]{:S(2)}) collective-permute-start(f32[32,1024]{1,0:T(8,128)S(1)} %fusion.after_ref), channel_id=1, source_target_pairs={{0,16},{4,20},{8,24},{12,28},{16,0},{20,4},{24,8},{28,12},{1,17},{... | collective-permute-start | bytes 393224 | tf_op jit(solution)/shard_map/ppermute | solution.py:364
  19.0 6.4 %copy-start.2 = (bf16[256,2048]{1,0:T(8,128)(2,1)S(1)}, bf16[256,2048]{1,0:T(8,128)(2,1)}, u32[]{:S(2)}) copy-start(bf16[256,2048]{1,0:T(8,128)(2,1)} %q_ref.3) | copy-start | bytes 3145732
  19.0 6.4 %copy-start.5 = (f32[6,512,128]{2,1,0:T(8,128)S(1)}, f32[6,512,128]{2,1,0:T(8,128)}, u32[]{:S(2)}) copy-start(f32[6,512,128]{2,1,0:T(8,128)} %get-tuple-element.37.l_ref) | copy-start | bytes 4718596
  19.0 6.4 %copy-start.9 = (f32[8,256,128]{2,1,0:T(8,128)S(1)}, f32[8,256,128]{2,1,0:T(8,128)}, u32[]{:S(2)}) copy-start(f32[8,256,128]{2,1,0:T(8,128)} %get-tuple-element.39.y_ref) | copy-start | bytes 3145732
  19.0 6.4 %copy-start.11 = (f32[2,512,128]{2,1,0:T(8,128)S(1)}, f32[2,512,128]{2,1,0:T(8,128)}, u32[]{:S(2)}) copy-start(f32[2,512,128]{2,1,0:T(8,128)} %get-tuple-element.38.tail_ref) | copy-start | bytes 1572868
  23.8 5.0 %collective-permute-start.3 = (f32[32,1024]{1,0:T(8,128)S(1)}, f32[32,1024]{1,0:T(8,128)S(1)}, u32[]{:S(2)}, u32[]{:S(2)}) collective-permute-start(f32[32,1024]{1,0:T(8,128)S(1)} %get-tuple-element.52), channel_id=1, source_target_pairs={{0,4},{4,0},{8,12},{12,8},{16,20},{20,16},{24,28},{28,24},{1,5},{5... | collective-permute-start | bytes 393224 | tf_op jit(solution)/shard_map/ppermute | solution.py:364
  25.4 3.5 %copy-start.6 = (f32[6,512,128]{2,1,0:T(8,128)S(1)}, f32[6,512,128]{2,1,0:T(8,128)}, u32[]{:S(2)}) copy-start(f32[6,512,128]{2,1,0:T(8,128)} %get-tuple-element.42.l_ref) | copy-start | bytes 4718596
  25.4 3.5 %copy-start.10 = (f32[8,256,128]{2,1,0:T(8,128)S(1)}, f32[8,256,128]{2,1,0:T(8,128)}, u32[]{:S(2)}) copy-start(f32[8,256,128]{2,1,0:T(8,128)} %get-tuple-element.44.y_ref) | copy-start | bytes 3145732
  25.4 3.4 %copy-start.12 = (f32[2,512,128]{2,1,0:T(8,128)S(1)}, f32[2,512,128]{2,1,0:T(8,128)}, u32[]{:S(2)}) copy-start(f32[2,512,128]{2,1,0:T(8,128)} %get-tuple-element.43.tail_ref) | copy-start | bytes 1572868
  28.9 7.9 %copy-start.14 = (f32[2048]{0:T(1024)S(1)}, f32[2048]{0:T(1024)}, u32[]{:S(2)}) copy-start(f32[2048]{0:T(1024)} %param.17) | copy-start | bytes 24580
  31.9 1.2 %collective-permute-start.4 = (f32[256]{0:T(256)S(1)}, f32[256]{0:T(256)S(1)}, u32[]{:S(2)}, u32[]{:S(2)}) collective-permute-start(f32[256]{0:T(256)S(1)} %reduce_sum.9), channel_id=1, source_target_pairs={{0,1},{1,0},{2,3},{3,2},{4,5},{5,4},{6,7},{7,6},{8,9},{9,8},{10,11... | collective-permute-start | bytes 3080 | tf_op jit(solution)/shard_map/ppermute | solution.py:364
  33.1 3.6 %collective-permute-start.5 = (f32[256]{0:T(256)S(1)}, f32[256]{0:T(256)S(1)}, u32[]{:S(2)}, u32[]{:S(2)}) collective-permute-start(f32[256]{0:T(256)S(1)} %add.56), channel_id=1, source_target_pairs={{0,2},{1,3},{2,0},{3,1},{4,6},{5,7},{6,4},{7,5},{8,10},{9,11},{10,... | collective-permute-start | bytes 3080 | tf_op jit(solution)/shard_map/ppermute | solution.py:364
